TPU v7x, 32 devices: a whole 2x2x4 slice. The times are simulated.
32 devices in a mesh: dp: 4 (over y, core), tensor: 8 (over z, x).
Axes of the slice: x: 2, y: 2, z: 4, core: 2. Of those that a mesh axis runs over, the one named last changes fastest.
Arguments:
- queries: bfloat16 [4096, 1024], P('dp'), may hold values from -6 to 6
- passages: bfloat16 [4096, 1024], P('dp'), may hold values from -6 to 6
- query_lengths: int32 [4], replicated, may hold values from 256 to 1024, as said below
- passage_lengths: int32 [4], replicated, may hold values from 256 to 1024, as said below
- w_qkv: bfloat16 [3, 1024, 1024], P(None, None, 'tensor'), may hold values from -0.1875 to 0.1875
- qv_bias: bfloat16 [2, 1024], P(None, 'tensor'), may hold values from -2 to 2
- w_out: bfloat16 [1024, 1024], P('tensor'), may hold values from -1.5 to 1.5
- w_in: bfloat16 [1024, 4096], P(None, 'tensor'), may hold values from -0.1875 to 0.1875
- in_bias: bfloat16 [4096], P('tensor'), may hold values from -3 to 3
- w_down: bfloat16 [4096, 1024], P('tensor'), may hold values from -0.09375 to 0.09375
- norm_gain: float32 [2, 1024], replicated, may hold values from 0.5 to 1.5
- norm_shift: float32 [2, 1024], replicated, may hold values from -2 to 2
- layer_bias: float32 [3, 1024], replicated, may hold values from -2 to 2
- w_colbert: bfloat16 [1024, 1024], replicated, may hold values from -0.1875 to 0.1875
- dense_cot: float32 [4, 4], replicated, may hold values from -8 to 8
- colbert_cot: float32 [4, 4], replicated, may hold values from -64 to 64
Outputs:
- out_queries: bfloat16 [4096, 1024], P(('dp', 'tensor'))
- out_passages: bfloat16 [4096, 1024], P(('dp', 'tensor'))
- grad_queries: float32 [4096, 1024], P(('dp', 'tensor'))
- grad_passages: float32 [4096, 1024], P(('dp', 'tensor'))
- grad_w_qkv: float32 [3, 1024, 1024], P(None, None, 'tensor')
- grad_qv_bias: float32 [2, 1024], P(None, 'tensor')
- grad_w_out: float32 [1024, 1024], P('tensor')
- grad_w_in: float32 [1024, 4096], P(None, 'tensor')
- grad_in_bias: float32 [4096], P('tensor')
- grad_w_down: float32 [4096, 1024], P('tensor')
- grad_norm_gain: float32 [2, 1024], replicated
- grad_norm_shift: float32 [2, 1024], replicated
- grad_layer_bias: float32 [3, 1024], replicated
- grad_w_colbert: float32 [1024, 1024], replicated
Inputs may be any that keep to these rules, and one draw needn't show every extreme that they name: `query_lengths`: in every data group the query or the passage uses all its positions; in every draw some query uses all 1024 and some passage all 1024. `passage_lengths`: drawn together with query_lengths.
All inputs are finite; a program needn't handle non-finite values.
Results may differ from a plain program's by a relative error of at most 0.023.
Values may be sent and summed in bfloat16 or wider, within the bound.
A program may use at most 192 MiB of HBM per device.

v0:
```python
import jax
import jax.numpy as jnp
from jax import lax
from jax.sharding import PartitionSpec as P

D = 1024
HEAD_DIM = 64
QLEN = 1024
PLEN = 1024


def inner_rows(left, right):
    return lax.dot_general(
        left, right, (((1,), (1,)), ((), ())), preferred_element_type=jnp.float32
    )


def outer_rows(left, right):
    return lax.dot_general(
        left, right, (((0,), (0,)), ((), ())), preferred_element_type=jnp.float32
    )


def exact_rows(left, right):
    return lax.dot_general(
        left,
        right,
        (((1,), (1,)), ((), ())),
        precision=lax.Precision.HIGHEST,
        preferred_element_type=jnp.float32,
    )


def layer_norm(hidden, gain, shift):
    centre = hidden - jnp.mean(hidden, axis=-1, keepdims=True)
    inverse = lax.rsqrt(jnp.mean(centre * centre, axis=-1, keepdims=True) + 1e-05)
    normal = centre * inverse
    return (normal * gain + shift, normal, inverse)


def norm_back(grad, normal, inverse, gain):
    scaled = grad * gain
    middle = (
        scaled
        - jnp.mean(scaled, axis=-1, keepdims=True)
        - normal * jnp.mean(scaled * normal, axis=-1, keepdims=True)
    )
    return (middle * inverse, jnp.sum(grad * normal, axis=0), jnp.sum(grad, axis=0))


def gelu_slope(inner):
    return (
        0.5 * (1.0 + lax.erf(inner * 0.7071067811865476))
        + inner * jnp.exp(-0.5 * inner * inner) * 0.3989422804014327
    )


def attend(query, key, value, keep, scale):
    span = query.shape[0]
    block = min(512, span)

    def one_block(index):
        rows = lax.dynamic_slice_in_dim(query, index * block, block, 0)
        scores = jnp.einsum("qhd,khd->hqk", rows, key, preferred_element_type=jnp.float32) * scale
        scores = jnp.where(keep[None, None, :], scores, -1e30)
        top = jnp.max(scores, axis=-1, keepdims=True)
        raised = jnp.exp(scores - top)
        total = jnp.sum(raised, axis=-1, keepdims=True)
        weights = (raised / total).astype(jnp.bfloat16)
        context = jnp.einsum("hqk,khd->qhd", weights, value, preferred_element_type=jnp.float32)
        return (context.astype(jnp.bfloat16), (top + jnp.log(total))[..., 0])

    context, logsum = lax.map(one_block, jnp.arange(span // block))
    return (context.reshape(span, -1), logsum)


def attend_back(query, key, value, keep, scale, logsum, grad_context):
    span = query.shape[0]
    block = min(512, span)

    def one_block(carry, index):
        grad_key, grad_value = carry
        rows = lax.dynamic_slice_in_dim(query, index * block, block, 0)
        grad_rows = lax.dynamic_slice_in_dim(grad_context, index * block, block, 0)
        scores = jnp.einsum("qhd,khd->hqk", rows, key, preferred_element_type=jnp.float32) * scale
        scores = jnp.where(keep[None, None, :], scores, -1e30)
        probs = jnp.exp(scores - logsum[index][..., None])
        weights = probs.astype(jnp.bfloat16)
        grad_probs = jnp.einsum(
            "qhd,khd->hqk", grad_rows, value, preferred_element_type=jnp.float32
        )
        middle = jnp.sum(probs * grad_probs, axis=-1, keepdims=True)
        grad_scores = (probs * (grad_probs - middle)).astype(jnp.bfloat16)
        grad_query = (
            jnp.einsum("hqk,khd->qhd", grad_scores, key, preferred_element_type=jnp.float32) * scale
        )
        grad_key = (
            grad_key
            + jnp.einsum("hqk,qhd->khd", grad_scores, rows, preferred_element_type=jnp.float32)
            * scale
        )
        grad_value = grad_value + jnp.einsum(
            "hqk,qhd->khd", weights, grad_rows, preferred_element_type=jnp.float32
        )
        return ((grad_key, grad_value), grad_query)

    empty = jnp.zeros(key.shape, jnp.float32)
    (grad_key, grad_value), grad_query = lax.scan(
        one_block, (empty, empty), jnp.arange(span // block)
    )
    return (grad_query.reshape(span, -1), grad_key.reshape(span, -1), grad_value.reshape(span, -1))


def layer_forward(tokens, length, weights):
    w_qkv, qv_bias, w_out, w_in, in_bias, w_down, norm_gain, norm_shift, layer_bias = weights
    span = tokens.shape[0]
    share = span // lax.axis_size("tensor")
    rank = lax.axis_index("tensor")
    heads = w_qkv.shape[2] // HEAD_DIM
    scale = HEAD_DIM ** (-0.5)
    query = (jnp.dot(tokens, w_qkv[0], preferred_element_type=jnp.float32) + qv_bias[0]).astype(
        jnp.bfloat16
    )
    key = jnp.dot(tokens, w_qkv[1], preferred_element_type=jnp.float32).astype(jnp.bfloat16)
    value = (jnp.dot(tokens, w_qkv[2], preferred_element_type=jnp.float32) + qv_bias[1]).astype(
        jnp.bfloat16
    )
    keep = jnp.arange(span) < length
    shaped = (
        query.reshape(span, heads, HEAD_DIM),
        key.reshape(span, heads, HEAD_DIM),
        value.reshape(span, heads, HEAD_DIM),
    )
    context, logsum = attend(shaped[0], shaped[1], shaped[2], keep, scale)
    attention = lax.psum_scatter(
        jnp.dot(context, w_out, preferred_element_type=jnp.float32).astype(jnp.bfloat16),
        "tensor",
        scatter_dimension=0,
        tiled=True,
    ).astype(jnp.float32)
    mine = lax.dynamic_slice_in_dim(tokens, rank * share, share, 0).astype(jnp.float32)
    first, first_normal, first_inverse = layer_norm(
        mine + attention + layer_bias[0], norm_gain[0], norm_shift[0]
    )
    normed = lax.all_gather(first.astype(jnp.bfloat16), "tensor", axis=0, tiled=True)
    inner = jnp.dot(normed, w_in, preferred_element_type=jnp.float32) + in_bias
    active = jax.nn.gelu(inner, approximate=False).astype(jnp.bfloat16)
    feed = lax.psum_scatter(
        jnp.dot(active, w_down, preferred_element_type=jnp.float32).astype(jnp.bfloat16),
        "tensor",
        scatter_dimension=0,
        tiled=True,
    ).astype(jnp.float32)
    output, out_normal, out_inverse = layer_norm(
        first + feed + layer_bias[1], norm_gain[1], norm_shift[1]
    )
    return (
        shaped,
        keep,
        logsum,
        context,
        first_normal,
        first_inverse,
        normed,
        inner,
        active,
        out_normal,
        out_inverse,
        output,
    )


def layer_back(grad_out, kept, tokens, weights):
    w_qkv, qv_bias, w_out, w_in, in_bias, w_down, norm_gain, norm_shift, layer_bias = weights
    (
        shaped,
        keep,
        logsum,
        context,
        first_normal,
        first_inverse,
        normed,
        inner,
        active,
        out_normal,
        out_inverse,
        output,
    ) = kept
    span = tokens.shape[0]
    scale = HEAD_DIM ** (-0.5)
    grad_mid, gain_two, shift_two = norm_back(grad_out, out_normal, out_inverse, norm_gain[1])
    feed_grad = lax.all_gather(grad_mid.astype(jnp.bfloat16), "tensor", axis=0, tiled=True)
    grad_active = inner_rows(feed_grad, w_down)
    grad_w_down = outer_rows(active, feed_grad)
    grad_inner = (grad_active * gelu_slope(inner)).astype(jnp.bfloat16)
    grad_w_in = outer_rows(normed, grad_inner)
    grad_in_bias = jnp.sum(grad_inner.astype(jnp.float32), axis=0)
    grad_first = grad_mid + lax.psum_scatter(
        inner_rows(grad_inner, w_in).astype(jnp.bfloat16), "tensor", scatter_dimension=0, tiled=True
    ).astype(jnp.float32)
    grad_hidden, gain_one, shift_one = norm_back(
        grad_first, first_normal, first_inverse, norm_gain[0]
    )
    attn_grad = lax.all_gather(grad_hidden.astype(jnp.bfloat16), "tensor", axis=0, tiled=True)
    grad_context = inner_rows(attn_grad, w_out).astype(jnp.bfloat16)
    grad_w_out = outer_rows(context, attn_grad)
    heads = context.shape[1] // HEAD_DIM
    grad_parts = attend_back(
        shaped[0],
        shaped[1],
        shaped[2],
        keep,
        scale,
        logsum,
        grad_context.reshape(span, heads, HEAD_DIM),
    )
    rounded = [part.astype(jnp.bfloat16) for part in grad_parts]
    grad_w_qkv = jnp.stack([outer_rows(tokens, part) for part in rounded])
    grad_qv_bias = jnp.stack(
        [
            jnp.sum(rounded[0].astype(jnp.float32), axis=0),
            jnp.sum(rounded[2].astype(jnp.float32), axis=0),
        ]
    )
    total = inner_rows(rounded[0], w_qkv[0])
    total = total + inner_rows(rounded[1], w_qkv[1])
    grad_tokens = grad_hidden + lax.psum_scatter(
        (total + inner_rows(rounded[2], w_qkv[2])).astype(jnp.bfloat16),
        "tensor",
        scatter_dimension=0,
        tiled=True,
    ).astype(jnp.float32)
    gains = jnp.stack([gain_one, gain_two])
    shifts = jnp.stack([shift_one, shift_two])
    biases = jnp.stack([jnp.sum(grad_hidden, axis=0), jnp.sum(grad_mid, axis=0)])
    return (
        grad_tokens,
        (grad_w_qkv, grad_qv_bias, grad_w_out, grad_w_in, grad_in_bias, grad_w_down),
        (gains, shifts, biases),
    )


def row_vectors(output, w_colbert, colbert_bias, start):
    count = output.shape[0]
    projected = (
        jnp.dot(output.astype(jnp.bfloat16), w_colbert, preferred_element_type=jnp.float32)
        + colbert_bias
    )
    leading = start + jnp.arange(count) == 0
    chosen = jnp.where(leading[:, None], output, projected)
    inverse = lax.rsqrt(jnp.sum(chosen * chosen, axis=-1, keepdims=True) + 1e-06)
    unit = chosen * inverse
    return (unit.astype(jnp.bfloat16), unit, inverse, leading)


def row_back(grad_vec, unit, inverse, leading, output, w_colbert):
    grad_chosen = inverse * (grad_vec - unit * jnp.sum(grad_vec * unit, axis=-1, keepdims=True))
    grad_proj = jnp.where(leading[:, None], 0.0, grad_chosen).astype(jnp.bfloat16)
    grad_out = jnp.where(leading[:, None], grad_chosen, 0.0) + inner_rows(grad_proj, w_colbert)
    return (
        grad_out,
        outer_rows(output.astype(jnp.bfloat16), grad_proj),
        jnp.sum(grad_proj.astype(jnp.float32), axis=0),
    )


def per_device(
    queries,
    passages,
    query_lengths,
    passage_lengths,
    w_qkv,
    qv_bias,
    w_out,
    w_in,
    in_bias,
    w_down,
    norm_gain,
    norm_shift,
    layer_bias,
    w_colbert,
    dense_cot,
    colbert_cot,
):
    weights = (w_qkv, qv_bias, w_out, w_in, in_bias, w_down, norm_gain, norm_shift, layer_bias)
    group = lax.axis_index("dp")
    rank = lax.axis_index("tensor")
    count_q = query_lengths.shape[0]
    count_p = passage_lengths.shape[0]
    query_ids = jnp.arange(count_q)
    passage_ids = jnp.arange(count_p)
    length_q = jnp.sum(jnp.where(query_ids == group, query_lengths, 0))
    length_p = jnp.sum(jnp.where(passage_ids == group, passage_lengths, 0))
    kept_q = layer_forward(queries, length_q, weights)
    kept_p = layer_forward(passages, length_p, weights)
    output_q = kept_q[-1]
    output_p = kept_p[-1]
    share_q = output_q.shape[0]
    share_p = output_p.shape[0]
    vec_q, unit_q, inverse_q, leading_q = row_vectors(
        output_q, w_colbert, layer_bias[2], rank * share_q
    )
    vec_p, unit_p, inverse_p, leading_p = row_vectors(
        output_p, w_colbert, layer_bias[2], rank * share_p
    )
    place_q = rank * share_q + jnp.arange(share_q)
    valid_q = (place_q >= 1) & (place_q < length_q)
    place_p = rank * share_p + jnp.arange(share_p)
    valid_p = (place_p >= 1) & (place_p < length_p)
    scale = D**0.5
    colbert_row = lax.dynamic_slice_in_dim(colbert_cot, group, 1, 0)[0]
    dense_row = lax.dynamic_slice_in_dim(dense_cot, group, 1, 0)[0]
    colbert_col = lax.dynamic_slice_in_dim(colbert_cot, group, 1, 1)[:, 0]
    dense_col = lax.dynamic_slice_in_dim(dense_cot, group, 1, 1)[:, 0]

    def passage_rows(count):
        spot = jnp.arange(count)
        table = (spot // PLEN)[:, None] == passage_ids[None, :]
        place = spot % PLEN
        length = jnp.sum(jnp.where(table, passage_lengths[None, :], 0), axis=1)
        return (table, place, (place >= 1) & (place < length))

    piece = lax.all_gather(vec_p, ("dp", "tensor"), axis=0, tiled=True)
    table, place, valid = passage_rows(piece.shape[0])
    dots = inner_rows(vec_q, piece)
    raised = jnp.where(valid[None, :], jnp.exp(dots * scale - scale), 0.0)
    sums = jnp.dot(
        raised,
        table.astype(jnp.float32),
        precision=lax.Precision.HIGHEST,
        preferred_element_type=jnp.float32,
    )
    logsum = scale + jnp.log(sums)
    piece = lax.all_gather(vec_p, ("dp", "tensor"), axis=0, tiled=True)
    table, place, valid = passage_rows(piece.shape[0])
    dots = inner_rows(vec_q, piece)
    shift = exact_rows(logsum, table.astype(jnp.float32))
    weight_late = jnp.sum(jnp.where(table, colbert_row[None, :], 0.0), axis=1)
    weight_dense = jnp.sum(jnp.where(table, dense_row[None, :], 0.0), axis=1)
    late = jnp.where(
        valid_q[:, None] & valid[None, :],
        scale * weight_late[None, :] * jnp.exp(dots * scale - shift),
        0.0,
    )
    dense = jnp.where(leading_q[:, None] & (place == 0)[None, :], 50.0 * weight_dense[None, :], 0.0)
    grad_vec_q = jnp.dot(
        (late + dense).astype(jnp.bfloat16), piece, preferred_element_type=jnp.float32
    )
    all_logsums = lax.all_gather(logsum, ("dp", "tensor"), axis=0, tiled=True)
    mine_column = (passage_ids == group).astype(jnp.float32)
    own_shift = jnp.dot(
        all_logsums,
        mine_column,
        precision=lax.Precision.HIGHEST,
        preferred_element_type=jnp.float32,
    )
    rows = lax.all_gather(vec_q, ("dp", "tensor"), axis=0, tiled=True)
    count = rows.shape[0]
    spot = jnp.arange(count)
    table = (spot // QLEN)[:, None] == query_ids[None, :]
    place = spot % QLEN
    length = jnp.sum(jnp.where(table, query_lengths[None, :], 0), axis=1)
    valid = (place >= 1) & (place < length)
    weight_late = jnp.sum(jnp.where(table, colbert_col[None, :], 0.0), axis=1)
    weight_dense = jnp.sum(jnp.where(table, dense_col[None, :], 0.0), axis=1)
    shift = own_shift
    dots = inner_rows(rows, vec_p)
    late = jnp.where(
        valid[:, None] & valid_p[None, :],
        scale * weight_late[:, None] * jnp.exp(dots * scale - shift[:, None]),
        0.0,
    )
    dense = jnp.where((place == 0)[:, None] & leading_p[None, :], 50.0 * weight_dense[:, None], 0.0)
    grad_vec_p = outer_rows((late + dense).astype(jnp.bfloat16), rows)
    grad_out_q, colbert_weight_q, colbert_bias_q = row_back(
        grad_vec_q, unit_q, inverse_q, leading_q, output_q, w_colbert
    )
    grad_out_p, colbert_weight_p, colbert_bias_p = row_back(
        grad_vec_p, unit_p, inverse_p, leading_p, output_p, w_colbert
    )
    grad_queries, head_q, shared_q = layer_back(grad_out_q, kept_q, queries, weights)
    grad_passages, head_p, shared_p = layer_back(grad_out_p, kept_p, passages, weights)
    head_sum = (
        lax.psum((head_q[0] + head_p[0]).astype(jnp.bfloat16), "dp").astype(jnp.float32),
        lax.psum((head_q[1] + head_p[1]).astype(jnp.bfloat16), "dp").astype(jnp.float32),
        lax.psum((head_q[2] + head_p[2]).astype(jnp.bfloat16), "dp").astype(jnp.float32),
        lax.psum((head_q[3] + head_p[3]).astype(jnp.bfloat16), "dp").astype(jnp.float32),
        lax.psum((head_q[4] + head_p[4]).astype(jnp.bfloat16), "dp").astype(jnp.float32),
        lax.psum((head_q[5] + head_p[5]).astype(jnp.bfloat16), "dp").astype(jnp.float32),
    )
    bias_grad = jnp.concatenate(
        [shared_q[2] + shared_p[2], (colbert_bias_q + colbert_bias_p)[None, :]], axis=0
    )
    shared = lax.psum(
        (
            shared_q[0] + shared_p[0],
            shared_q[1] + shared_p[1],
            bias_grad,
            colbert_weight_q + colbert_weight_p,
        ),
        ("dp", "tensor"),
    )
    return (
        output_q.astype(jnp.bfloat16),
        output_p.astype(jnp.bfloat16),
        grad_queries,
        grad_passages,
        head_sum[0],
        head_sum[1],
        head_sum[2],
        head_sum[3],
        head_sum[4],
        head_sum[5],
        shared[0],
        shared[1],
        shared[2],
        shared[3],
    )


def solution(mesh):
    return jax.shard_map(
        per_device,
        mesh=mesh,
        in_specs=(
            P("dp", None),
            P("dp", None),
            P(),
            P(),
            P(None, None, "tensor"),
            P(None, "tensor"),
            P("tensor", None),
            P(None, "tensor"),
            P("tensor"),
            P("tensor", None),
            P(),
            P(),
            P(),
            P(),
            P(),
            P(),
        ),
        out_specs=(
            P(("dp", "tensor"), None),
            P(("dp", "tensor"), None),
            P(("dp", "tensor"), None),
            P(("dp", "tensor"), None),
            P(None, None, "tensor"),
            P(None, "tensor"),
            P("tensor", None),
            P(None, "tensor"),
            P("tensor"),
            P("tensor", None),
            P(),
            P(),
            P(),
            P(),
        ),
        check_vma=False,
    )
```

profile of v0, /device:TPU:1, one launch (start us, length us, event | category | flops | bytes accessed | tf_op | source)
XLA Modules:
  0.0 1371.7 jit_solution(5043304720532055914)
XLA Ops:
  15.5 11.8 while.57
  39.1 10.4 while.56
  52.1 49.1 %reduce-scatter.13.cloned.1.call-done = bf16[128,1024]{1,0:T(8,128)(2,1)} async-done(((bf16[1024,1024]{1,0:T(8,128)(2,1)}), bf16[128,1024]{1,0:T(8,128)(2,1)}) %reduce-scatter.13.cloned.1.call-update) | async-done | bytes 262160 | tf_op jit(solution)/shard_map/reduce_scatter | solution.py:135
  101.3 70.0 %reduce-scatter.9.cloned.1.call-done = bf16[128,1024]{1,0:T(8,128)(2,1)} async-done(((bf16[1024,1024]{1,0:T(8,128)(2,1)}), bf16[128,1024]{1,0:T(8,128)(2,1)}) %reduce-scatter.9.cloned.1.call-update) | async-done | bytes 262160 | tf_op jit(solution)/shard_map/reduce_scatter | solution.py:135
  177.5 48.3 %all-gather.9.cloned.1.call-done = bf16[1024,1024]{1,0:T(8,128)(2,1)} async-done(((bf16[128,1024]{1,0:T(8,128)(2,1)}), bf16[1024,1024]{1,0:T(8,128)(2,1)}) %all-gather.9.cloned.1.call-update) | async-done | bytes 2097168 | tf_op jit(solution)/shard_map/all_gather | solution.py:145
  225.8 4.2 fusion.217
  229.9 46.2 %all-gather.11.cloned.1.call-done = bf16[1024,1024]{1,0:T(8,128)(2,1)} async-done(((bf16[128,1024]{1,0:T(8,128)(2,1)}), bf16[1024,1024]{1,0:T(8,128)(2,1)}) %all-gather.11.cloned.1.call-update) | async-done | bytes 2097168 | tf_op jit(solution)/shard_map/all_gather | solution.py:145
  276.1 12.9 fusion.98
  296.6 61.8 %reduce-scatter.11.cloned.1.call-done = bf16[128,1024]{1,0:T(8,128)(2,1)} async-done(((bf16[1024,1024]{1,0:T(8,128)(2,1)}), bf16[128,1024]{1,0:T(8,128)(2,1)}) %reduce-scatter.11.cloned.1.call-update) | async-done | bytes 262160 | tf_op jit(solution)/shard_map/reduce_scatter | solution.py:148
  358.5 70.8 %reduce-scatter.15.cloned.1.call-done = bf16[128,1024]{1,0:T(8,128)(2,1)} async-done(((bf16[1024,1024]{1,0:T(8,128)(2,1)}), bf16[128,1024]{1,0:T(8,128)(2,1)}) %reduce-scatter.15.cloned.1.call-update) | async-done | bytes 262160 | tf_op jit(solution)/shard_map/reduce_scatter | solution.py:148
  443.3 70.8 %all-gather.13.cloned.1.call-done = bf16[4096,1024]{1,0:T(8,128)(2,1)} async-done(((bf16[128,1024]{1,0:T(8,128)(2,1)}), bf16[4096,1024]{1,0:T(8,128)(2,1)}) %all-gather.13.cloned.1.call-update) | async-done | bytes 8388624 | tf_op jit(solution)/shard_map/all_gather | solution.py:334
  514.2 6.5 convolution_multiply_fusion.5
  522.0 60.5 %all_gather.34 = f32[4096,4]{0,1:T(4,128)S(1)} all-gather(f32[128,4]{0,1:T(4,128)S(1)} %fusion.140), channel_id=1, replica_groups=mesh['dp'=4,'tensor'=8] {'dp','tensor'}, dimensions={0}, use_global_device_ids=true | all-gather | bytes 67584 | tf_op jit(solution)/shard_map/all_gather | solution.py:349
  586.8 7.7 all-gather.19.cloned.1.call-done
  594.5 12.7 multiply_reduce_fusion.8
  617.1 44.1 %all-gather.21.cloned.1.call-done = bf16[1024,1024]{1,0:T(8,128)(2,1)} async-done(((bf16[128,1024]{1,0:T(8,128)(2,1)}), bf16[1024,1024]{1,0:T(8,128)(2,1)}) %all-gather.21.cloned.1.call-update) | async-done | bytes 2097168 | tf_op jit(solution)/shard_map/all_gather | solution.py:192
  661.3 4.5 convert_reduce_fusion
  669.5 42.1 %all-gather.15.cloned.1.call-done = bf16[1024,1024]{1,0:T(8,128)(2,1)} async-done(((bf16[128,1024]{1,0:T(8,128)(2,1)}), bf16[1024,1024]{1,0:T(8,128)(2,1)}) %all-gather.15.cloned.1.call-update) | async-done | bytes 2097168 | tf_op jit(solution)/shard_map/all_gather | solution.py:192
  711.6 3.9 convert_reduce_fusion.1
  719.2 62.0 %reduce-scatter.21.cloned.1.call-done = bf16[128,1024]{1,0:T(8,128)(2,1)} async-done(((bf16[1024,1024]{1,0:T(8,128)(2,1)}), bf16[128,1024]{1,0:T(8,128)(2,1)}) %reduce-scatter.21.cloned.1.call-update) | async-done | bytes 262160 | tf_op jit(solution)/shard_map/reduce_scatter | solution.py:198
  781.1 70.6 %reduce-scatter.17.cloned.1.call-done = bf16[128,1024]{1,0:T(8,128)(2,1)} async-done(((bf16[1024,1024]{1,0:T(8,128)(2,1)}), bf16[128,1024]{1,0:T(8,128)(2,1)}) %reduce-scatter.17.cloned.1.call-update) | async-done | bytes 262160 | tf_op jit(solution)/shard_map/reduce_scatter | solution.py:198
  867.8 37.2 %all-gather.23.cloned.1.call-done = bf16[1024,1024]{1,0:T(8,128)(2,1)} async-done(((bf16[128,1024]{1,0:T(8,128)(2,1)}), bf16[1024,1024]{1,0:T(8,128)(2,1)}) %all-gather.23.cloned.1.call-update) | async-done | bytes 2097168 | tf_op jit(solution)/shard_map/all_gather | solution.py:204
  908.2 36.3 %while.59 = (s32[]{:T(128)}, f32[1024,2,64]{0,2,1:T(8,128)}, f32[1024,2,64]{0,2,1:T(8,128)}, bf16[2,512,2,64]{1,3,2,0:T(8,128)(2,1)}, s32[2]{0:T(128)S(1)}, /*in...) while((s32[]{:T(128)}, f32[1024,2,64]{0,2,1:T(8,128)}, ...), condition=%wide.region_48.49_spmd.clone, body=%wide.region_46.48_spmd.clone.sunk | while | flops 687538176 | bytes 72909248 | solution.py:108
  932.3 4.0 multiply_reduce_fusion.25
  958.1 34.0 %while.58 = (s32[]{:T(128)}, f32[1024,2,64]{0,2,1:T(8,128)S(1)}, f32[1024,2,64]{0,2,1:T(8,128)}, bf16[2,512,2,64]{1,3,2,0:T(8,128)(2,1)}, s32[2]{0:T(128)S(1)}, ...) while((s32[]{:T(128)}, f32[1024,2,64]{0,2,1:T(8,128)S(1)}, ...), condition=%wide.region_35.36_spmd.clone, body=%wide.region_33.35_spmd.clone.sunk | while | flops 687538176 | bytes 72909248 | solution.py:108
  1017.4 42.2 %all-reduce = (f32[2,1024]{1,0:T(2,128)}, f32[2,1024]{1,0:T(2,128)}, f32[3,1024]{1,0:T(4,128)}) all-reduce(f32[2,1024]{1,0:T(2,128)S(1)} %maximum_add_fusion.1, f32[2,1024]{1,0:T(2,128)S(1)} %maximum_add_fusion.2, f32[3,1024]{1,0:T(4,128)S(1)} %pad_maximum_fusion), channel_id=1, replica_groups=mesh['dp'=4,'tensor'=8] {'dp','tensor'}, use_global_device_ids=true, to_apply=%region_66.67 | all-reduce | flops 7168 | bytes 57344 | tf_op jit(solution)/shard_map/psum | solution.py:394
  1060.2 6.4 all-reduce.1
  1067.8 5.7 all-reduce.8.cloned.1.call-done
  1080.3 62.4 %reduce-scatter.23.cloned.1.call-done = bf16[128,1024]{1,0:T(8,128)(2,1)} async-done(((bf16[1024,1024]{1,0:T(8,128)(2,1)}), bf16[128,1024]{1,0:T(8,128)(2,1)}) %reduce-scatter.23.cloned.1.call-update) | async-done | bytes 262160 | tf_op jit(solution)/shard_map/reduce_scatter | solution.py:227
  1144.5 68.1 %reduce-scatter.19.cloned.1.call-done = bf16[128,1024]{1,0:T(8,128)(2,1)} async-done(((bf16[1024,1024]{1,0:T(8,128)(2,1)}), bf16[128,1024]{1,0:T(8,128)(2,1)}) %reduce-scatter.19.cloned.1.call-update) | async-done | bytes 262160 | tf_op jit(solution)/shard_map/reduce_scatter | solution.py:227
  1214.5 145.0 %all-reduce.6.cloned.1.call-done = f32[1024,1024]{1,0:T(8,128)} async-done(((f32[1024,1024]{1,0:T(8,128)}), f32[1024,1024]{1,0:T(8,128)}) %all-reduce.6.cloned.1.call-update) | async-done | bytes 4194320 | tf_op jit(solution)/shard_map/psum | solution.py:394
  1359.5 4.9 copy.98
  (517 shorter events, 216.9 us)
Async XLA Ops:
  7.2 426.0 %copy-start = (bf16[1024,1024]{1,0:T(8,128)(2,1)S(1)}, bf16[1024,1024]{1,0:T(8,128)(2,1)}, u32[]{:S(2)}) copy-start(bf16[1024,1024]{1,0:T(8,128)(2,1)} %param.37) | copy-start | bytes 6291460
  7.2 94.1 %reduce-scatter.13.cloned.1.call-start = ((), (), s32[]{:S(2)}) async-start(), calls=%async_computation.11 | async-start | bytes 2359296 | tf_op jit(solution)/shard_map/reduce_scatter | solution.py:135
  32.4 138.9 %reduce-scatter.9.cloned.1.call-start = ((), (), s32[]{:S(2)}) async-start(), calls=%async_computation.8 | async-start | bytes 2359296 | tf_op jit(solution)/shard_map/reduce_scatter | solution.py:135
  52.0 173.7 %all-gather.9.cloned.1.call-start = ((), (), s32[]{:S(2)}) async-start(), calls=%async_computation.9 | async-start | bytes 2359296 | tf_op jit(solution)/shard_map/all_gather | solution.py:145
  101.3 73.1 %copy-start.25 = (bf16[128,1024]{1,0:T(8,128)(2,1)S(1)}, bf16[128,1024]{1,0:T(8,128)(2,1)}, u32[]{:S(2)}) copy-start(bf16[128,1024]{1,0:T(8,128)(2,1)} %reduce-scatter.13.cloned.1.call-done) | copy-start | bytes 786436
  171.3 54.5 %copy-start.115 = (bf16[1024,512]{1,0:T(8,128)(2,1)S(1)}, bf16[1024,512]{1,0:T(8,128)(2,1)}, u32[]{:S(2)}) copy-start(bf16[1024,512]{1,0:T(8,128)(2,1)} %param.31) | copy-start | bytes 3145732
  176.6 99.5 %all-gather.11.cloned.1.call-start = ((), (), s32[]{:S(2)}) async-start(), calls=%async_computation.12 | async-start | bytes 2359296 | tf_op jit(solution)/shard_map/all_gather | solution.py:145
  177.2 181.3 %reduce-scatter.11.cloned.1.call-start = ((), (), s32[]{:S(2)}) async-start(), calls=%async_computation.10 | async-start | bytes 2359296 | tf_op jit(solution)/shard_map/reduce_scatter | solution.py:148
  177.4 98.7 %copy-start.104 = (f32[512]{0:T(512)}, f32[512]{0:T(512)S(1)}, u32[]{:S(2)}) copy-start(f32[512]{0:T(512)S(1)} %convert_element_type.296) | copy-start | bytes 6148
  229.9 60.1 %copy-start.113 = (bf16[512,1024]{1,0:T(8,128)(2,1)S(1)}, bf16[512,1024]{1,0:T(8,128)(2,1)}, u32[]{:S(2)}) copy-start(bf16[512,1024]{1,0:T(8,128)(2,1)} %param.33) | copy-start | bytes 3145732
  292.7 136.6 %reduce-scatter.15.cloned.1.call-start = ((), (), s32[]{:S(2)}) async-start(), calls=%async_computation.13 | async-start | bytes 2359296 | tf_op jit(solution)/shard_map/reduce_scatter | solution.py:148
  296.5 217.6 %all-gather.13.cloned.1.call-start = ((), (), s32[]{:S(2)}) async-start(), calls=%async_computation.14 | async-start | bytes 8650752 | tf_op jit(solution)/shard_map/all_gather | solution.py:334
  296.6 315.4 %copy-start.81 = (pred[128]{0:T(512)(128)(4,1)}, pred[128]{0:T(512)(128)(4,1)S(1)}, u32[]{:S(2)}) copy-start(pred[128]{0:T(512)(128)(4,1)S(1)} %fusion.199) | copy-start | bytes 388
  435.4 159.1 %all-gather.19.cloned.1.call-start = ((), (), s32[]{:S(2)}) async-start(), calls=%async_computation.19 | async-start | bytes 8650752 | tf_op jit(solution)/shard_map/all_gather | solution.py:357
  438.6 222.6 %all-gather.21.cloned.1.call-start = ((), (), s32[]{:S(2)}) async-start(), calls=%async_computation.20 | async-start | bytes 2359296 | tf_op jit(solution)/shard_map/all_gather | solution.py:192
  514.2 70.4 %copy-start.14 = (bf16[4096,1024]{1,0:T(8,128)(2,1)S(1)}, bf16[4096,1024]{1,0:T(8,128)(2,1)}, u32[]{:S(2)}) copy-start(bf16[4096,1024]{1,0:T(8,128)(2,1)} %all-gather.13.cloned.1.call-done) | copy-start | bytes 25165828
  520.7 62.0 %copy-start.96 = (pred[4096]{0:T(1024)(128)(4,1)S(1)}, pred[4096]{0:T(1024)(128)(4,1)}, u32[]{:S(2)}) copy-start(pred[4096]{0:T(1024)(128)(4,1)} %fusion.187) | copy-start | bytes 12292
  520.7 62.0 %copy-start.118 = (pred[128]{0:T(512)(128)(4,1)S(1)}, pred[128]{0:T(512)(128)(4,1)}, u32[]{:S(2)}) copy-start(pred[128]{0:T(512)(128)(4,1)} %compare_and_fusion.1) | copy-start | bytes 388
  614.8 96.8 %all-gather.15.cloned.1.call-start = ((), (), s32[]{:S(2)}) async-start(), calls=%async_computation.15 | async-start | bytes 2359296 | tf_op jit(solution)/shard_map/all_gather | solution.py:192
  616.9 164.2 %reduce-scatter.21.cloned.1.call-start = ((), (), s32[]{:S(2)}) async-start(), calls=%async_computation.21 | async-start | bytes 2359296 | tf_op jit(solution)/shard_map/reduce_scatter | solution.py:198
  669.4 182.3 %reduce-scatter.17.cloned.1.call-start = ((), (), s32[]{:S(2)}) async-start(), calls=%async_computation.16 | async-start | bytes 2359296 | tf_op jit(solution)/shard_map/reduce_scatter | solution.py:198
  719.1 132.7 %copy-start.27 = (bf16[128,1024]{1,0:T(8,128)(2,1)S(1)}, bf16[128,1024]{1,0:T(8,128)(2,1)}, u32[]{:S(2)}) copy-start(bf16[128,1024]{1,0:T(8,128)(2,1)} %reduce-scatter.9.cloned.1.call-done) | copy-start | bytes 786436
  719.1 132.7 %copy-start.39 = (f32[128,1024]{1,0:T(8,128)S(1)}, f32[128,1024]{1,0:T(8,128)}, u32[]{:S(2)}) copy-start(f32[128,1024]{1,0:T(8,128)} %get-tuple-element.517) | copy-start | bytes 1572868
  719.1 185.9 %all-gather.23.cloned.1.call-start = ((), (), s32[]{:S(2)}) async-start(), calls=%async_computation.22 | async-start | bytes 2359296 | tf_op jit(solution)/shard_map/all_gather | solution.py:204
  781.1 72.6 %copy-start.74 = (bf16[128,1024]{1,0:T(8,128)(2,1)S(1)}, bf16[128,1024]{1,0:T(8,128)(2,1)}, u32[]{:S(2)}) copy-start(bf16[128,1024]{1,0:T(8,128)(2,1)} %reduce-scatter.21.cloned.1.call-done) | copy-start | bytes 786436
  855.9 99.1 %all-gather.17.cloned.1.call-start = ((), (), s32[]{:S(2)}) async-start(), calls=%async_computation.17 | async-start | bytes 2359296 | tf_op jit(solution)/shard_map/all_gather | solution.py:204
  867.5 206.0 %all-reduce.8.cloned.1.call-start = ((), (), s32[]{:S(2)}) async-start(), calls=%async_computation.25 | async-start | bytes 6291456 | tf_op jit(solution)/shard_map/psum | solution.py:384
  1003.3 139.5 %reduce-scatter.23.cloned.1.call-start = ((), (), s32[]{:S(2)}) async-start(), calls=%async_computation.23 | async-start | bytes 2359296 | tf_op jit(solution)/shard_map/reduce_scatter | solution.py:227
  1008.2 204.4 %reduce-scatter.19.cloned.1.call-start = ((), (), s32[]{:S(2)}) async-start(), calls=%async_computation.18 | async-start | bytes 2359296 | tf_op jit(solution)/shard_map/reduce_scatter | solution.py:227
  1011.9 347.5 %all-reduce.6.cloned.1.call-start = ((), (), s32[]{:S(2)}) async-start(), calls=%async_computation.24 | async-start | bytes 8388608 | tf_op jit(solution)/shard_map/psum | solution.py:394
  1078.0 64.7 %copy-start.33 = (f32[128,1024]{1,0:T(8,128)S(1)}, f32[128,1024]{1,0:T(8,128)}, u32[]{:S(2)}) copy-start(f32[128,1024]{1,0:T(8,128)} %copy-done.32) | copy-start | bytes 1572868
  1078.0 134.6 %copy-start.35 = (f32[128,1024]{1,0:T(8,128)S(1)}, f32[128,1024]{1,0:T(8,128)}, u32[]{:S(2)}) copy-start(f32[128,1024]{1,0:T(8,128)} %copy-done.34) | copy-start | bytes 1572868
  (124 other events, 764.2 us)
Sparse Core Ops, SparseCore 0:
  32.5 68.7 reduce-scatter.12
  105.4 65.8 reduce-scatter.8
  176.7 49.0 all-gather.8
  228.3 47.7 all-gather.10
  292.8 65.6 reduce-scatter.10
  362.4 66.7 reduce-scatter.14
  435.5 78.6 all-gather.12
  517.7 76.7 all-gather.18
  614.9 46.3 all-gather.20
  663.8 47.7 all-gather.14
  715.7 65.3 reduce-scatter.20
  785.1 66.6 reduce-scatter.16
  856.0 49.0 all-gather.22
  907.0 47.8 all-gather.16
  1003.4 70.1 all-reduce.7
  1076.9 65.7 reduce-scatter.22
  1146.1 66.5 reduce-scatter.18
  1218.6 140.7 all-reduce.5
where the time goes:
time: 1380 us; the launch traced here: 1370 us
  waiting for transfers between devices  964 us (70%)
  matrix products  177 us (13%)
  blocking collectives  109 us (8%)
  other arithmetic  54.9 us (4%)
  local copies, waits for them, and re-layouts  35.1 us (3%)
  between operations  16.2 us (1%)
    psum x1, waiting for transfers between devices, per_device(): lax.psum((shared_q[0] + shared_p[0], shared_q[1] + shared_p[1], bias_grad...  145 us
    reduce_scatter x2, waiting for transfers between devices, layer_forward(): lax.psum_scatter(jnp.dot(active, w_down, preferred_element_type=jnp.float...  133 us
    reduce_scatter x2, waiting for transfers between devices, layer_back(): lax.psum_scatter(inner_rows(grad_inner, w_in).astype(jnp.bfloat16), 'tens...  133 us
    reduce_scatter x2, waiting for transfers between devices, layer_back(): lax.psum_scatter((total + inner_rows(rounded[2], w_qkv[2])).astype(jnp.bf...  131 us
    reduce_scatter x2, waiting for transfers between devices, layer_forward(): lax.psum_scatter(jnp.dot(context, w_out, preferred_element_type=jnp.float...  119 us
    all_gather x2, waiting for transfers between devices, layer_forward(): lax.all_gather(first.astype(jnp.bfloat16), 'tensor', axis=0, tiled=True)  94.5 us
    all_gather x2, waiting for transfers between devices, layer_back(): lax.all_gather(grad_mid.astype(jnp.bfloat16), 'tensor', axis=0, tiled=True)  86.2 us
    all_gather x1, waiting for transfers between devices, per_device(): piece = lax.all_gather(vec_p, ('dp', 'tensor'), axis=0, tiled=True)  70.8 us
  transfers between devices with their start and end apart: 18, of which 18 were waited for; matrix products, arithmetic and copies ran while one was open for 10% of the time, Pallas kernels for 0%

commit v1 on v0

v1 whole, which is shorter than its diff:
```python
import functools

import jax
import jax.numpy as jnp
from jax import lax
from jax.experimental import pallas as pl
from jax.experimental.pallas import tpu as pltpu
from jax.sharding import PartitionSpec as P

HEAD_DIM = 64
BF = jnp.bfloat16
F32 = jnp.float32
BLOCK = 256


def dot(left, right):
    return jnp.dot(left, right, preferred_element_type=F32)


def inner_rows(left, right):
    return lax.dot_general(left, right, (((1,), (1,)), ((), ())), preferred_element_type=F32)


def outer_rows(left, right):
    return lax.dot_general(left, right, (((0,), (0,)), ((), ())), preferred_element_type=F32)


def steps_of(size):
    steps = []
    while size > 1:
        size //= 2
        steps.append(size)
    return steps


def offsets(steps):
    found = [0]
    for step in steps:
        found = found + [item ^ step for item in found]
    return found


def swap(value, axis, step):
    size = lax.axis_size(axis)
    return lax.ppermute(value, axis, [(index, index ^ step) for index in range(size)])


def spread(value, axis, steps):
    held = value[None]
    for step in steps:
        held = jnp.concatenate([held, swap(held, axis, step)], axis=0)
    return held


def fold(parts, axis, steps):
    for step in reversed(steps):
        half = parts.shape[0] // 2
        came = swap(parts[half:].astype(BF), axis, step)
        parts = parts[:half].astype(F32) + came.astype(F32)
    return parts[0]


def natural(parts, axis, steps, dim=0):
    order = offsets(steps)
    size = len(order)
    place = [0] * size
    for spot, item in enumerate(order):
        place[item] = spot
    table = jnp.array(place, jnp.int32)
    rank = lax.axis_index(axis)
    return jnp.concatenate(
        [lax.dynamic_slice_in_dim(parts, table[item ^ rank], 1, dim) for item in range(size)], axis=dim
    )


def xored(parts, axis, steps, dim=0):
    rank = lax.axis_index(axis)
    return jnp.concatenate(
        [lax.dynamic_slice_in_dim(parts, item ^ rank, 1, dim) for item in offsets(steps)], axis=dim
    )


def trade(parts, steps, dim):
    rank = lax.axis_index("tensor")
    got = []
    for item in offsets(steps):
        piece = lax.dynamic_index_in_dim(parts, item ^ rank, dim, keepdims=False)
        got.append(swap(piece, "tensor", item) if item else piece)
    return got


def layer_norm(hidden, gain, shift):
    centre = hidden - jnp.mean(hidden, axis=-1, keepdims=True)
    inverse = lax.rsqrt(jnp.mean(centre * centre, axis=-1, keepdims=True) + 1e-05)
    normal = centre * inverse
    return (normal * gain + shift, normal, inverse)


def norm_back(grad, normal, inverse, gain):
    scaled = grad * gain
    middle = (
        scaled
        - jnp.mean(scaled, axis=-1, keepdims=True)
        - normal * jnp.mean(scaled * normal, axis=-1, keepdims=True)
    )
    return (middle * inverse, jnp.sum(grad * normal, axis=0), jnp.sum(grad, axis=0))


def gelu_slope(inner):
    return (
        0.5 * (1.0 + lax.erf(inner * 0.7071067811865476))
        + inner * jnp.exp(-0.5 * inner * inner) * 0.3989422804014327
    )


def head_mask(columns, head):
    lane = lax.broadcasted_iota(jnp.int32, (1, columns), 1)
    return (lane >= head * HEAD_DIM) & (lane < (head + 1) * HEAD_DIM)


def attend_kernel(lens, x, w, b, q, k, v, ctx, lse):
    span, columns = q.shape[1], q.shape[2]
    heads = columns // HEAD_DIM
    length = lens[pl.program_id(0)]
    scale = HEAD_DIM**-0.5
    rows = x[0]
    q[0] = (dot(rows, w[0]) + b[0:1, :].astype(F32)).astype(BF)
    k[0] = dot(rows, w[1]).astype(BF)
    v[0] = (dot(rows, w[2]) + b[1:2, :].astype(F32)).astype(BF)
    keys = k[0]
    values = v[0]
    keep = lax.broadcasted_iota(jnp.int32, (1, span), 1) < length
    block = min(BLOCK, span)

    @pl.loop(0, span // block)
    def _(index):
        at = pl.ds(pl.multiple_of(index * block, block), block)
        query = q[0, at, :]
        total = jnp.zeros((block, columns), F32)
        for head in range(heads):
            mask = head_mask(columns, head)
            mine = jnp.where(mask, query, jnp.zeros_like(query)) * jnp.asarray(scale, BF)
            scores = jnp.where(keep, inner_rows(mine, keys), -1e30)
            top = jnp.max(scores, axis=-1, keepdims=True)
            raised = jnp.exp(scores - top)
            mass = jnp.sum(raised, axis=-1, keepdims=True)
            part = dot(raised.astype(BF), values) / mass
            total = jnp.where(mask, part, total)
            column = jnp.broadcast_to(top + jnp.log(mass), (block, 128))
            lse[0, head : head + 1, at] = column.T[0:1, :]
        ctx[0, at, :] = total.astype(BF)


def attend_back_kernel(lens, q, k, v, g, lse, out, dk_sum, dv_sum):
    span, columns = q.shape[1], q.shape[2]
    heads = columns // HEAD_DIM
    length = lens[pl.program_id(0)]
    scale = HEAD_DIM**-0.5
    keys = k[0]
    values = v[0]
    keep = lax.broadcasted_iota(jnp.int32, (span, 1), 0) < length
    block = min(BLOCK, span)
    dk_sum[...] = jnp.zeros_like(dk_sum)
    dv_sum[...] = jnp.zeros_like(dv_sum)

    @pl.loop(0, span // block)
    def _(index):
        at = pl.ds(pl.multiple_of(index * block, block), block)
        query = q[0, at, :]
        grad = g[0, at, :]
        total = jnp.zeros((block, columns), F32)
        for head in range(heads):
            mask = head_mask(columns, head)
            mine = jnp.where(mask, query, jnp.zeros_like(query)) * jnp.asarray(scale, BF)
            back = jnp.where(mask, grad, jnp.zeros_like(grad))
            scores = jnp.where(keep, inner_rows(keys, mine), -1e30)
            probs = jnp.exp(scores - lse[0, head : head + 1, at])
            slope = inner_rows(values, back)
            middle = jnp.sum(probs * slope, axis=0, keepdims=True)
            turn = (probs * (slope - middle)).astype(BF)
            dv_sum[...] += dot(probs.astype(BF), back)
            dk_sum[...] += dot(turn, mine)
            part = outer_rows(turn, keys) * scale
            total = jnp.where(mask, part, total)
        out[0, at, 0:columns] = total.astype(BF)

    out[0, :, columns : 2 * columns] = dk_sum[...].astype(BF)
    out[0, :, 2 * columns : 3 * columns] = dv_sum[...].astype(BF)


def attend(lens, tokens, w_qkv, qv_bias):
    count, span, width = tokens.shape
    columns = w_qkv.shape[2]
    heads = columns // HEAD_DIM
    flat = jax.ShapeDtypeStruct((count, span, columns), BF)
    rows = pl.BlockSpec((1, span, columns), lambda i, n: (i, 0, 0))
    return pl.pallas_call(
        attend_kernel,
        out_shape=(flat, flat, flat, flat, jax.ShapeDtypeStruct((count, heads, span), F32)),
        grid_spec=pltpu.PrefetchScalarGridSpec(
            num_scalar_prefetch=1,
            grid=(count,),
            in_specs=[
                pl.BlockSpec((1, span, width), lambda i, n: (i, 0, 0)),
                pl.BlockSpec((3, width, columns), lambda i, n: (0, 0, 0)),
                pl.BlockSpec((2, columns), lambda i, n: (0, 0)),
            ],
            out_specs=[rows, rows, rows, rows, pl.BlockSpec((1, heads, span), lambda i, n: (i, 0, 0))],
        ),
        compiler_params=pltpu.CompilerParams(vmem_limit_bytes=48 * 2**20),
        cost_estimate=pl.CostEstimate(
            flops=20 * 10**9, bytes_accessed=8 * 2**20, transcendentals=count * heads * span * span
        ),
        name="attend",
    )(lens, tokens, w_qkv, qv_bias)


def attend_back(lens, query, key, value, grad, lse):
    count, span, columns = query.shape
    heads = columns // HEAD_DIM
    rows = pl.BlockSpec((1, span, columns), lambda i, n: (i, 0, 0))
    return pl.pallas_call(
        attend_back_kernel,
        out_shape=jax.ShapeDtypeStruct((count, span, 3 * columns), BF),
        grid_spec=pltpu.PrefetchScalarGridSpec(
            num_scalar_prefetch=1,
            grid=(count,),
            in_specs=[rows, rows, rows, rows, pl.BlockSpec((1, heads, span), lambda i, n: (i, 0, 0))],
            out_specs=pl.BlockSpec((1, span, 3 * columns), lambda i, n: (i, 0, 0)),
            scratch_shapes=[pltpu.VMEM((span, columns), F32), pltpu.VMEM((span, columns), F32)],
        ),
        compiler_params=pltpu.CompilerParams(vmem_limit_bytes=48 * 2**20),
        cost_estimate=pl.CostEstimate(
            flops=40 * 10**9, bytes_accessed=8 * 2**20, transcendentals=count * heads * span * span
        ),
        name="attend_back",
    )(lens, query, key, value, grad, lse)


def per_device(
    queries,
    passages,
    query_lengths,
    passage_lengths,
    w_qkv,
    qv_bias,
    w_out,
    w_in,
    in_bias,
    w_down,
    norm_gain,
    norm_shift,
    layer_bias,
    w_colbert,
    dense_cot,
    colbert_cot,
):
    groups, ranks = lax.axis_size("dp"), lax.axis_size("tensor")
    group, rank = lax.axis_index("dp"), lax.axis_index("tensor")
    all_t, all_d = steps_of(ranks), steps_of(groups)
    far_t, near_t = all_t[:-1], all_t[-1:]
    far_d, near_d = all_d[:-1], all_d[-1:]
    span, width = queries.shape
    share = span // ranks
    columns = w_qkv.shape[2]
    hidden = w_in.shape[1]
    piece = hidden // groups

    up_mine = lax.dynamic_slice_in_dim(w_in, group * piece, piece, 1).T
    down_mine = lax.dynamic_slice_in_dim(w_down, group * piece, piece, 0)
    up = spread(up_mine, "tensor", all_t).reshape(-1, width)
    down = spread(down_mine, "tensor", all_t).reshape(-1, width)
    slim = columns // groups
    out_mine = lax.dynamic_slice_in_dim(w_out, group * slim, slim, 0)
    out_all = spread(spread(out_mine, "tensor", all_t), "dp", all_d)
    out_all = natural(out_all, "dp", all_d).transpose(1, 0, 2, 3).reshape(ranks * columns, width)
    bias_all = lax.all_gather(in_bias, "tensor").reshape(ranks, groups, piece)
    bias_mine = lax.dynamic_index_in_dim(bias_all, group, 1, keepdims=False)
    bias_units = xored(bias_mine, "tensor", all_t).reshape(-1).astype(F32)

    tokens = jnp.stack([queries, passages])
    lens = jnp.stack([query_lengths[group], passage_lengths[group]])
    query, key, value, context, lse = attend(lens, tokens, w_qkv, qv_bias)
    context = context.reshape(2, ranks, share, columns)
    context_rows = jnp.concatenate(trade(context, all_t, 1), axis=-1).reshape(2 * share, ranks * columns)

    mine = lax.dynamic_index_in_dim(
        tokens.reshape(2, ranks, share, width), rank, 1, keepdims=False
    ).reshape(2 * share, width)
    first, first_normal, first_inverse = layer_norm(
        mine.astype(F32) + dot(context_rows, out_all) + layer_bias[0], norm_gain[0], norm_shift[0]
    )
    normed = spread(first.astype(BF), "dp", all_d).reshape(-1, width)
    inner = inner_rows(normed, up) + bias_units
    active = jax.nn.gelu(inner, approximate=False).astype(BF)
    feed = fold(dot(active, down).reshape(groups, 2 * share, width), "dp", all_d)
    output, out_normal, out_inverse = layer_norm(
        first + feed + layer_bias[1], norm_gain[1], norm_shift[1]
    )
    output_low = output.astype(BF)

    place = rank * share + jnp.arange(share)
    leading = jnp.concatenate([place == 0, place == 0])[:, None]
    chosen = jnp.where(leading, output, dot(output_low, w_colbert) + layer_bias[2])
    inverse = lax.rsqrt(jnp.sum(chosen * chosen, axis=-1, keepdims=True) + 1e-06)
    unit = chosen * inverse
    vectors = unit.astype(BF)
    rows_q = spread(spread(vectors[:share], "tensor", far_t), "dp", near_d).reshape(-1, width)
    rows_p = spread(spread(vectors[share:], "dp", far_d), "tensor", near_t).reshape(-1, width)
    off_zt, off_xt = jnp.array(offsets(far_t)), jnp.array(offsets(near_t))
    off_yd, off_cd = jnp.array(offsets(far_d)), jnp.array(offsets(near_d))
    count_z, count_x, count_y, count_c = len(off_zt), len(off_xt), len(off_yd), len(off_cd)
    spot = jnp.arange(share)
    place_q = jnp.broadcast_to(
        ((rank ^ off_zt)[None, :, None] * share + spot[None, None, :]), (count_c, count_z, share)
    )
    group_q = group ^ off_cd
    length_q = query_lengths[group_q]
    valid_q = ((place_q >= 1) & (place_q < length_q[:, None, None])).reshape(-1)
    lead_q = (place_q == 0).reshape(-1)
    place_p = jnp.broadcast_to(
        ((rank ^ off_xt)[:, None, None] * share + spot[None, None, :]), (count_x, count_y, share)
    )
    group_p = group ^ off_yd
    length_p = passage_lengths[group_p]
    valid_p = (place_p >= 1) & (place_p < length_p[None, :, None])
    lead_p = place_p == 0
    scale = float(width) ** 0.5
    many_q = count_c * count_z * share
    dots = inner_rows(rows_p, rows_q).reshape(count_x, count_y, share, many_q)
    raised = jnp.where(valid_p[..., None], jnp.exp(dots * scale - scale), 0.0)
    sums = jnp.sum(raised, axis=(0, 2)).reshape(count_y, count_c, count_z, share)
    order = offsets(far_t)
    for step in far_t:
        came = swap(sums, "tensor", step)
        came = jnp.stack([came[:, :, order.index(item ^ step)] for item in order], axis=2)
        sums = sums + came
    late = scale * colbert_cot[group_q][:, group_p].T
    late = jnp.broadcast_to(late[:, :, None, None], (count_y, count_c, count_z, share))
    late = jnp.where(valid_q[None], late.reshape(count_y, many_q) / sums.reshape(count_y, many_q), 0.0)
    dense = 50.0 * dense_cot[group_q][:, group_p].T
    dense = jnp.broadcast_to(dense[:, :, None], (count_y, count_c, count_z * share)).reshape(count_y, many_q)
    dense = jnp.where(lead_q[None], dense, 0.0)
    pull = raised * late[None, :, None, :] + jnp.where(lead_p[..., None], dense[None, :, None, :], 0.0)
    pull = pull.astype(BF).reshape(-1, many_q)
    grad_q = fold(
        fold(outer_rows(pull, rows_p).reshape(count_c, count_z, share, width), "dp", near_d),
        "tensor",
        far_t,
    )
    grad_p = fold(
        fold(dot(pull, rows_q).reshape(count_x, count_y, share, width), "tensor", near_t), "dp", far_d
    )
    grad_vec = jnp.concatenate([grad_q, grad_p])

    grad_chosen = inverse * (grad_vec - unit * jnp.sum(grad_vec * unit, axis=-1, keepdims=True))
    grad_proj = jnp.where(leading, 0.0, grad_chosen).astype(BF)
    grad_out = jnp.where(leading, grad_chosen, 0.0) + inner_rows(grad_proj, w_colbert)
    colbert_bias = jnp.sum(grad_proj.astype(F32), axis=0)
    left = xored(output_low.reshape(2 * share, ranks, -1), "tensor", all_t, 1).reshape(2 * share, width)
    right = xored(grad_proj.reshape(2 * share, groups, -1), "dp", all_d, 1)
    colbert = jnp.stack([outer_rows(left, right[:, index]) for index in range(groups)])
    colbert = colbert.reshape(groups, ranks, width // ranks, width // groups)
    colbert = fold(fold(colbert, "dp", all_d), "tensor", all_t).astype(BF)
    colbert = spread(spread(colbert, "tensor", all_t), "dp", all_d)
    colbert = natural(natural(colbert, "dp", all_d, 0), "tensor", all_t, 1)
    colbert = colbert.transpose(1, 2, 0, 3).reshape(width, width).astype(F32)

    grad_mid, gain_two, shift_two = norm_back(grad_out, out_normal, out_inverse, norm_gain[1])
    feed_grad = spread(grad_mid.astype(BF), "dp", all_d).reshape(-1, width)
    grad_inner = (inner_rows(feed_grad, down) * gelu_slope(inner)).astype(BF)
    back = fold(dot(grad_inner, up).reshape(groups, 2 * share, width), "dp", all_d)
    grad_hidden, gain_one, shift_one = norm_back(
        grad_mid + back, first_normal, first_inverse, norm_gain[0]
    )
    attn_grad = grad_hidden.astype(BF)
    grad_context = inner_rows(attn_grad, out_all).astype(BF).reshape(2, share, ranks, columns)
    order = offsets(all_t)
    parts = []
    for index, item in enumerate(order):
        part = grad_context[:, :, index]
        parts.append(swap(part, "tensor", item) if item else part)
    heads_grad = natural(jnp.stack(parts, axis=1), "tensor", all_t, 1).reshape(2, span, columns)

    def unit_grads(left, right):
        whole = outer_rows(left, right).reshape(ranks, piece, width)
        own = fold(whole, "tensor", all_t).astype(BF)
        return natural(spread(own, "dp", all_d), "dp", all_d).reshape(hidden, width)

    grad_down = unit_grads(active, feed_grad).astype(F32)
    grad_up = unit_grads(grad_inner, normed).astype(F32).T
    grad_in_bias = natural(jnp.sum(grad_inner.astype(F32), axis=0).reshape(ranks, piece), "tensor", all_t)

    whole = outer_rows(context_rows, attn_grad).reshape(ranks, groups, slim, width).transpose(1, 0, 2, 3)
    whole = fold(xored(whole, "dp", all_d), "dp", all_d)
    own = fold(whole, "tensor", all_t).astype(BF)
    grad_w_out = natural(spread(own, "dp", all_d), "dp", all_d).reshape(columns, width).astype(F32)

    turned = attend_back(lens, query, key, value, heads_grad, lse)
    got = trade(turned.reshape(2, ranks, share, 3 * columns), all_t, 1)
    got = jnp.concatenate(got, axis=-1).reshape(2 * share, ranks * 3 * columns)
    slice_in = width // groups
    w_mine, _ = lax.optimization_barrier(
        (lax.dynamic_slice_in_dim(w_qkv, group * slice_in, slice_in, 1), output_low)
    )
    w_mine = w_mine.transpose(0, 2, 1).reshape(3 * columns, slice_in)
    w_back = spread(spread(w_mine, "tensor", all_t), "dp", all_d).reshape(groups, -1, slice_in)
    added = jnp.stack([dot(got, w_back[index]) for index in range(groups)])
    added = natural(added, "dp", all_d).transpose(1, 0, 2).reshape(2 * share, width)
    grad_tokens = grad_hidden + added
    tall = tokens.reshape(2 * span, width)
    turned = turned.reshape(2 * span, 3 * columns)
    grad_qkv = outer_rows(tall, turned)
    sums_qkv = jnp.sum(turned.astype(F32), axis=0, keepdims=True)
    grad_qkv = jnp.concatenate([grad_qkv, jnp.broadcast_to(sums_qkv, (8, 3 * columns))])
    for step in reversed(all_d):
        low = grad_qkv.astype(BF)
        grad_qkv = low.astype(F32) + swap(low, "dp", step).astype(F32)
    grad_w_qkv = grad_qkv[:width].reshape(width, 3, columns).transpose(1, 0, 2)
    sums_qkv = grad_qkv[width].reshape(3, columns)
    grad_qv_bias = jnp.stack([sums_qkv[0], sums_qkv[2]])

    spaced = jnp.where(
        (jnp.arange(groups) == group)[None, :, None], grad_in_bias[:, None, :], 0.0
    ).reshape(-1, width)
    small = jnp.concatenate(
        [
            jnp.stack(
                [
                    gain_one,
                    gain_two,
                    shift_one,
                    shift_two,
                    jnp.sum(grad_hidden, axis=0),
                    jnp.sum(grad_mid, axis=0),
                    colbert_bias,
                ]
            ),
            spaced,
        ]
    )
    small = lax.psum(small, ("dp", "tensor"))
    grad_in_bias = lax.dynamic_index_in_dim(small[7:].reshape(ranks, hidden), rank, 0, keepdims=False)
    return (
        output_low[:share],
        output_low[share:],
        grad_tokens[:share],
        grad_tokens[share:],
        grad_w_qkv,
        grad_qv_bias,
        grad_w_out,
        grad_up,
        grad_in_bias,
        grad_down,
        small[0:2],
        small[2:4],
        small[4:7],
        colbert,
    )


def solution(mesh):
    both = P(("dp", "tensor"), None)
    return jax.shard_map(
        per_device,
        mesh=mesh,
        in_specs=(
            P("dp", None),
            P("dp", None),
            P(),
            P(),
            P(None, None, "tensor"),
            P(None, "tensor"),
            P("tensor", None),
            P(None, "tensor"),
            P("tensor"),
            P("tensor", None),
            P(),
            P(),
            P(),
            P(),
            P(),
            P(),
        ),
        out_specs=(
            both,
            both,
            both,
            both,
            P(None, None, "tensor"),
            P(None, "tensor"),
            P("tensor", None),
            P(None, "tensor"),
            P("tensor"),
            P("tensor", None),
            P(),
            P(),
            P(),
            P(),
        ),
        check_vma=False,
    )
```

time: 1380 us -> 771 us (0.56)
  waiting for transfers between devices: 964 us -> 253 us
  matrix products: 177 us -> 51.3 us
  starting transfers between devices: 1.74 us -> 120 us
  local copies, waits for them, and re-layouts: 35.1 us -> 102 us
  Pallas kernels: 0 us -> 32.9 us
  other arithmetic: 54.9 us -> 84.2 us
  blocking collectives: 109 us -> 90.3 us
    reduce_scatter x8 -> x0, waiting for transfers between devices: 515 us -> none  [the longest x2 133 us: layer_forward(): lax.psum_scatter(jnp.dot(active, w_down, preferred_element_type=jnp.float...]
    all_gather x8 -> x0, waiting for transfers between devices: 298 us -> none  [the longest x2 94.5 us: layer_forward(): lax.all_gather(first.astype(jnp.bfloat16), 'tensor', axis=0, tiled=True)]
    ppermute x0 -> x86, waiting for transfers between devices: none -> 253 us  [swap(): lax.ppermute(value, axis, [(index, index ^ step) for index in range(size)])]
    psum x2 -> x0, waiting for transfers between devices: 151 us -> none  [the longest x1 145 us: per_device(): lax.psum((shared_q[0] + shared_p[0], shared_q[1] + shared_p[1], bias_grad...]
    ppermute x0 -> x86, starting transfers between devices: none -> 120 us  [swap(): lax.ppermute(value, axis, [(index, index ^ step) for index in range(size)])]
    dot_general x46 -> x9, matrix products: 105 us -> 14.2 us  [dot(): return jnp.dot(left, right, preferred_element_type=F32)]
    concatenate x1 -> x39, other arithmetic: 0.01 us -> 37.6 us  [the longest x30 34.7 us: spread(): held = jnp.concatenate([held, swap(held, axis, step)], axis=0)]
    pallas_call x0 -> x2, Pallas kernels: none -> 32.9 us  [the longest x1 17 us: attend_back(): pl.pallas_call(attend_back_kernel, out_shape=jax.ShapeDtypeStruct((count,...]
  transfers between devices with their start and end apart: 18 -> 86, of which waited for: 18 -> 35; matrix products, arithmetic and copies ran while one was open for 10% -> 25% of each run, Pallas kernels for 0% -> 4%
where the time goes in v1:
time: 771 us; the launch traced here: 760 us
  waiting for transfers between devices  253 us (33%)
  starting transfers between devices  120 us (16%)
  local copies, waits for them, and re-layouts  102 us (13%)
  blocking collectives  90.3 us (12%)
  other arithmetic  84.2 us (11%)
  matrix products  51.3 us (7%)
  Pallas kernels  32.9 us (4%)
  between operations  26.8 us (3%)
    ppermute x86, waiting for transfers between devices, swap(): lax.ppermute(value, axis, [(index, index ^ step) for index in range(size)])  253 us
    ppermute x86, starting transfers between devices, swap(): lax.ppermute(value, axis, [(index, index ^ step) for index in range(size)])  120 us
    all_gather x1, blocking collectives, per_device(): bias_all = lax.all_gather(in_bias, 'tensor').reshape(ranks, groups, piece)  49.7 us
    unnamed x275, local copies, waits for them, and re-layouts  44.2 us
    psum x1, blocking collectives, per_device(): small = lax.psum(small, ('dp', 'tensor'))  40.6 us
    concatenate x30, other arithmetic, spread(): held = jnp.concatenate([held, swap(held, axis, step)], axis=0)  34.7 us
    dot_general x5, matrix products, inner_rows(): lax.dot_general(left, right, (((1,), (1,)), ((), ())), preferred_element_...  23.8 us
    pallas_call x1, Pallas kernels, attend_back(): pl.pallas_call(attend_back_kernel, out_shape=jax.ShapeDtypeStruct((count,...  17 us
  transfers between devices with their start and end apart: 86, of which 35 were waited for; matrix products, arithmetic and copies ran while one was open for 25% of the time, Pallas kernels for 4%

profile of v1, /device:TPU:1, one launch (start us, length us, event | category | flops | bytes accessed | tf_op | source)
XLA Modules:
  0.0 760.2 jit_solution(5455468491742463344)
XLA Ops:
  8.6 4.7 pad_maximum_fusion.x
  13.3 15.9 %attend.1 = (bf16[2,1024,128]{2,1,0:T(8,128)(2,1)S(1)}, bf16[2,1024,128]{2,1,0:T(8,128)(2,1)S(1)}, bf16[2,1024,128]{2,1,0:T(8,128)(2,1)S(1)}, bf16[2,1024,128]{2,1,0:T(8,128)(2,1)S(1)}, f32[2,2,1024]{2,1,0:T(2,128)S(1)}) custom-call(s32[2]{0:T(128)S(1)} %pad_add_fusion.1.lens, bf16[2,1024,1024]{2,1,0:T(8,128)(2,1)} %pad_maximum_fusion.x, ...), custom_call_target="tpu_custom_call" | custom-call | flops 20000000000 | bytes 8388608 | tf_op jit(solution)/shard_map/attend/pallas_call | solution.py:197
  52.3 7.0 collective-permute-done.10
  60.4 4.6 collective-permute-start.11
  88.8 15.3 %collective-permute-done.14 = bf16[1,128,1024]{2,1,0:T(8,128)(2,1)S(1)} collective-permute-done((bf16[1,128,1024]{2,1,0:T(8,128)(2,1)}, bf16[1,128,1024]{2,1,0:T(8,128)(2,1)S(1)}, u32[]{:S(2)}, u32[]{:S(2)}) %collective-permute-start.14) | collective-permute-done | bytes 262176 | tf_op jit(solution)/shard_map/ppermute | solution.py:45
  105.3 4.5 collective-permute-done.17
  116.3 4.9 collective-permute-done.15
  122.4 10.2 %collective-permute-done.18 = bf16[2,128,1024]{2,1,0:T(8,128)(2,1)S(1)} collective-permute-done((bf16[2,128,1024]{2,1,0:T(8,128)(2,1)S(1)}, bf16[2,128,1024]{2,1,0:T(8,128)(2,1)S(1)}, u32[]{:S(2)}, u32[]{:S(2)}) %collective-permute-start.18) | collective-permute-done | bytes 524320 | tf_op jit(solution)/shard_map/ppermute | solution.py:45
  135.3 49.7 %all-gather.1 = bf16[8,1,512]{2,1,0:T(2,128)(2,1)S(1)} all-gather(bf16[1,1,512]{2,1,0:T(2,128)(2,1)S(1)} %reshape.554), channel_id=2, replica_groups=mesh['dp'=4,'tensor'=8] {'tensor'}, dimensions={0}, use_global_device_ids=true | all-gather | bytes 9216 | tf_op jit(solution)/shard_map/all_gather | solution.py:277
  191.4 12.4 %fusion.2 = (bf16[1024,1024]{1,0:T(8,128)(2,1)S(1)}, f32[1024,1024]{1,0:T(8,128)}) fusion(f32[1024]{0:T(1024)S(1)} %bitcast_convert_fusion.5, bf16[1024,1024]{1,0:T(8,128)(2,1)S(1)} %bitcast.434, bf16[1024,1024]{1,0:T(8,128)(2,1)S(1)} %bitcast.432), kind=kOutput, calls=%fused_computation.10 | convolution fusion | flops 2216689664 | bytes 10489856 | tf_op jit(solution)/shard_map/dot_general | solution.py:21
  209.3 4.9 collective-permute-start.20
  220.1 11.7 %collective-permute-done.21 = bf16[1,256,1024]{2,1,0:T(8,128)(2,1)S(1)} collective-permute-done((bf16[1,256,1024]{2,1,0:T(8,128)(2,1)S(1)}, bf16[1,256,1024]{2,1,0:T(8,128)(2,1)S(1)}, u32[]{:S(2)}, u32[]{:S(2)}) %collective-permute-start.21) | collective-permute-done | bytes 524320 | tf_op jit(solution)/shard_map/ppermute | solution.py:45
  236.1 13.5 %collective-permute-done.24 = bf16[1,128,1024]{2,1,0:T(8,128)(2,1)} collective-permute-done((bf16[1,128,1024]{2,1,0:T(8,128)(2,1)}, bf16[1,128,1024]{2,1,0:T(8,128)(2,1)}, u32[]{:S(2)}, u32[]{:S(2)}) %collective-permute-start.24) | collective-permute-done | bytes 262176 | tf_op jit(solution)/shard_map/ppermute | solution.py:45
  252.2 12.5 %collective-permute-done.25 = bf16[2,128,1024]{2,1,0:T(8,128)(2,1)} collective-permute-done((bf16[2,128,1024]{2,1,0:T(8,128)(2,1)}, bf16[2,128,1024]{2,1,0:T(8,128)(2,1)}, u32[]{:S(2)}, u32[]{:S(2)}) %collective-permute-start.25) | collective-permute-done | bytes 524320 | tf_op jit(solution)/shard_map/ppermute | solution.py:45
  271.6 5.0 collective-permute-done.22
  279.7 10.8 %collective-permute-done.23 = bf16[1,2,128,1024]{3,2,1,0:T(8,128)(2,1)S(1)} collective-permute-done((bf16[1,2,128,1024]{3,2,1,0:T(8,128)(2,1)S(1)}, bf16[1,2,128,1024]{3,2,1,0:T(8,128)(2,1)S(1)}, u32[]{:S(2)}, u32[]{:S(2)}) %collective-permute-start.23) | collective-permute-done | bytes 524320 | tf_op jit(solution)/shard_map/ppermute | solution.py:45
  330.0 19.3 %collective-permute-done.32 = bf16[1,2,128,1024]{3,2,1,0:T(8,128)(2,1)S(1)} collective-permute-done((bf16[1,2,128,1024]{3,2,1,0:T(8,128)(2,1)S(1)}, bf16[1,2,128,1024]{3,2,1,0:T(8,128)(2,1)S(1)}, u32[]{:S(2)}, u32[]{:S(2)}) %collective-permute-start.32) | collective-permute-done | bytes 524320 | tf_op jit(solution)/shard_map/ppermute | solution.py:45
  357.5 8.3 %collective-permute-done.31 = bf16[1,128,1024]{2,1,0:T(8,128)(2,1)S(1)} collective-permute-done((bf16[1,128,1024]{2,1,0:T(8,128)(2,1)S(1)}, bf16[1,128,1024]{2,1,0:T(8,128)(2,1)S(1)}, u32[]{:S(2)}, u32[]{:S(2)}) %collective-permute-start.31) | collective-permute-done | bytes 262176 | tf_op jit(solution)/shard_map/ppermute | solution.py:45
  394.2 7.0 collective-permute-done.34
  416.9 7.2 collective-permute-done.77
  439.6 4.4 fusion.95
  464.2 37.6 %collective-permute-done.83 = bf16[4,128,256]{2,1,0:T(8,128)(2,1)S(1)} collective-permute-done((bf16[4,128,256]{2,1,0:T(8,128)(2,1)S(1)}, bf16[4,128,256]{2,1,0:T(8,128)(2,1)S(1)}, u32[]{:S(2)}, u32[]{:S(2)}) %collective-permute-start.83) | collective-permute-done | bytes 262176 | tf_op jit(solution)/shard_map/ppermute | solution.py:45
  518.7 7.2 collective-permute-done.37
  527.2 40.6 %psum.7 = f32[11,1024]{1,0:T(8,128)S(1)} all-reduce(f32[11,1024]{1,0:T(8,128)S(1)} %concatenate.283), channel_id=1, replica_groups=mesh['dp'=4,'tensor'=8] {'dp','tensor'}, use_global_device_ids=true, to_apply=%region_20.21 | all-reduce | flops 11264 | bytes 90112 | tf_op jit(solution)/shard_map/psum | solution.py:442
  605.0 17.0 %attend_back.1 = bf16[2,1024,384]{2,1,0:T(8,128)(2,1)S(1)} custom-call(s32[2]{0:T(128)S(1)} %pad_add_fusion.1.lens, bf16[2,1024,128]{2,1,0:T(8,128)(2,1)S(1)} %get-tuple-element.21.q, bf16[2,1024,128]{2,1,0:T(8,128)(2,1)S(1)} %copy-done.5, bf16[2,1024,128]{2,1,0:T(8,128)(2,1)S(1)} %copy-done.7, bf16[2,1024,128]{2,1,0:T(8,128)(2,1)S(1)} %bitcast.399, ...), custom_call_target="tpu_custom_call" | custom-call | flops 40000000000 | bytes 8388608 | tf_op jit(solution)/shard_map/attend_back/pallas_call | solution.py:222
  645.5 7.9 %collective-permute-done.49 = bf16[2,128,384]{2,1,0:T(8,128)(2,1)S(1)} collective-permute-done((bf16[2,128,384]{2,1,0:T(8,128)(2,1)}, bf16[2,128,384]{2,1,0:T(8,128)(2,1)S(1)}, u32[]{:S(2)}, u32[]{:S(2)}) %collective-permute-start.49) | collective-permute-done | bytes 196640 | tf_op jit(solution)/shard_map/ppermute | solution.py:45
  655.4 5.3 collective-permute-done.51
  660.7 6.8 collective-permute-start.57
  681.2 5.5 collective-permute-done.69
  687.6 4.7 collective-permute-done.74
  707.0 17.9 %collective-permute-done.60 = bf16[1,8,32,1024]{3,2,1,0:T(8,128)(2,1)S(1)} collective-permute-done((bf16[1,8,32,1024]{3,2,1,0:T(8,128)(2,1)S(1)}, bf16[1,8,32,1024]{3,2,1,0:T(8,128)(2,1)S(1)}, u32[]{:S(2)}, u32[]{:S(2)}) %collective-permute-start.60) | collective-permute-done | bytes 524320 | tf_op jit(solution)/shard_map/ppermute | solution.py:45
  729.3 5.6 collective-permute-done.61
  (673 shorter events, 343.5 us)
Async XLA Ops:
  1.7 33.5 %collective-permute-start.7 = (bf16[1,32,1024]{2,1,0:T(8,128)(2,1)S(1)}, bf16[1,32,1024]{2,1,0:T(8,128)(2,1)}, u32[]{:S(2)}, u32[]{:S(2)}) collective-permute-start(bf16[1,32,1024]{2,1,0:T(8,128)(2,1)S(1)} %dynamic-slice_bitcast_fusion.10), channel_id=1, source_target_pairs={{0,4},{1,5},{2,6},{3,7},{4,0},{5,1},{6,2},{7,3},{8,12},{9,13},{10,... | collective-permute-start | bytes 196616 | tf_op jit(solution)/shard_map/ppermute | solution.py:45
  30.4 43.6 %collective-permute-start = (bf16[2,128,128]{2,1,0:T(8,128)(2,1)}, bf16[2,128,128]{2,1,0:T(8,128)(2,1)}, u32[]{:S(2)}, u32[]{:S(2)}) collective-permute-start(bf16[2,128,128]{2,1,0:T(8,128)(2,1)} %get-tuple-element.155), channel_id=1, source_target_pairs={{0,4},{1,5},{2,6},{3,7},{4,0},{5,1},{6,2},{7,3},{8,12},{9,13},{10,... | collective-permute-start | bytes 196616 | tf_op jit(solution)/shard_map/ppermute | solution.py:45
  30.4 46.6 %collective-permute-start.1 = (bf16[2,128,128]{2,1,0:T(8,128)(2,1)}, bf16[2,128,128]{2,1,0:T(8,128)(2,1)}, u32[]{:S(2)}, u32[]{:S(2)}) collective-permute-start(bf16[2,128,128]{2,1,0:T(8,128)(2,1)} %get-tuple-element.154), channel_id=1, source_target_pairs={{0,2},{1,3},{2,0},{3,1},{4,6},{5,7},{6,4},{7,5},{8,10},{9,11},{10,... | collective-permute-start | bytes 196616 | tf_op jit(solution)/shard_map/ppermute | solution.py:45
  31.8 47.9 %collective-permute-start.2 = (bf16[2,128,128]{2,1,0:T(8,128)(2,1)}, bf16[2,128,128]{2,1,0:T(8,128)(2,1)}, u32[]{:S(2)}, u32[]{:S(2)}) collective-permute-start(bf16[2,128,128]{2,1,0:T(8,128)(2,1)} %get-tuple-element.153), channel_id=1, source_target_pairs={{0,6},{1,7},{2,4},{3,5},{4,2},{5,3},{6,0},{7,1},{8,14},{9,15},{10,... | collective-permute-start | bytes 196616 | tf_op jit(solution)/shard_map/ppermute | solution.py:45
  34.0 49.1 %collective-permute-start.3 = (bf16[2,128,128]{2,1,0:T(8,128)(2,1)}, bf16[2,128,128]{2,1,0:T(8,128)(2,1)}, u32[]{:S(2)}, u32[]{:S(2)}) collective-permute-start(bf16[2,128,128]{2,1,0:T(8,128)(2,1)} %get-tuple-element.152), channel_id=1, source_target_pairs={{0,1},{1,0},{2,3},{3,2},{4,5},{5,4},{6,7},{7,6},{8,9},{9,8},{10,11... | collective-permute-start | bytes 196616 | tf_op jit(solution)/shard_map/ppermute | solution.py:45
  60.4 49.5 %collective-permute-start.11 = (bf16[2,8,32,1024]{3,2,0,1:T(8,128)(2,1)}, bf16[2,8,32,1024]{3,2,0,1:T(8,128)(2,1)}, u32[]{:S(2)}, u32[]{:S(2)}) collective-permute-start(bf16[2,8,32,1024]{3,2,0,1:T(8,128)(2,1)} %pad_maximum_fusion.12), channel_id=1, source_target_pairs={{0,8},{8,0},{16,24},{24,16},{1,9},{9,1},{17,25},{25,17},{2,10},{10... | collective-permute-start | bytes 3145736 | tf_op jit(solution)/shard_map/ppermute | solution.py:45
  85.0 24.8 %collective-permute-start.17 = (bf16[1,128,1024]{2,1,0:T(8,128)(2,1)}, bf16[1,128,1024]{2,1,0:T(8,128)(2,1)S(1)}, u32[]{:S(2)}, u32[]{:S(2)}) collective-permute-start(bf16[1,128,1024]{2,1,0:T(8,128)(2,1)} %dynamic-slice_bitcast_fusion.2), channel_id=1, source_target_pairs={{0,4},{1,5},{2,6},{3,7},{4,0},{5,1},{6,2},{7,3},{8,12},{9,13},{10,... | collective-permute-start | bytes 786440 | tf_op jit(solution)/shard_map/ppermute | solution.py:45
  109.8 22.7 %collective-permute-start.18 = (bf16[2,128,1024]{2,1,0:T(8,128)(2,1)S(1)}, bf16[2,128,1024]{2,1,0:T(8,128)(2,1)S(1)}, u32[]{:S(2)}, u32[]{:S(2)}) collective-permute-start(bf16[2,128,1024]{2,1,0:T(8,128)(2,1)S(1)} %pad_maximum_fusion.33), channel_id=1, source_target_pairs={{0,2},{1,3},{2,0},{3,1},{4,6},{5,7},{6,4},{7,5},{8,10},{9,11},{10,... | collective-permute-start | bytes 1572872 | tf_op jit(solution)/shard_map/ppermute | solution.py:45
  122.4 62.7 %collective-permute-start.16 = (bf16[4,128,1024]{2,1,0:T(8,128)(2,1)}, bf16[4,128,1024]{2,1,0:T(8,128)(2,1)}, u32[]{:S(2)}, u32[]{:S(2)}) collective-permute-start(bf16[4,128,1024]{2,1,0:T(8,128)(2,1)} %pad_maximum_fusion.14), channel_id=1, source_target_pairs={{0,1},{1,0},{2,3},{3,2},{4,5},{5,4},{6,7},{7,6},{8,9},{9,8},{10,11... | collective-permute-start | bytes 3145736 | tf_op jit(solution)/shard_map/ppermute | solution.py:45
  133.7 53.2 %collective-permute-start.19 = (bf16[4,128,1024]{2,1,0:T(8,128)(2,1)}, bf16[4,128,1024]{2,1,0:T(8,128)(2,1)}, u32[]{:S(2)}, u32[]{:S(2)}) collective-permute-start(bf16[4,128,1024]{2,1,0:T(8,128)(2,1)} %pad_maximum_fusion.15), channel_id=1, source_target_pairs={{0,1},{1,0},{2,3},{3,2},{4,5},{5,4},{6,7},{7,6},{8,9},{9,8},{10,11... | collective-permute-start | bytes 3145736 | tf_op jit(solution)/shard_map/ppermute | solution.py:45
  134.9 54.3 %collective-permute-start.13 = (bf16[2,256,1024]{2,1,0:T(8,128)(2,1)}, bf16[2,256,1024]{2,1,0:T(8,128)(2,1)}, u32[]{:S(2)}, u32[]{:S(2)}) collective-permute-start(bf16[2,256,1024]{2,1,0:T(8,128)(2,1)} %pad_maximum_fusion.13), channel_id=1, source_target_pairs={{0,8},{8,0},{16,24},{24,16},{1,9},{9,1},{17,25},{25,17},{2,10},{10... | collective-permute-start | bytes 3145736 | tf_op jit(solution)/shard_map/ppermute | solution.py:45
  305.5 22.3 %collective-permute-start.29 = (bf16[1,4,128,1024]{3,2,1,0:T(8,128)(2,1)}, bf16[1,4,128,1024]{3,2,1,0:T(8,128)(2,1)}, u32[]{:S(2)}, u32[]{:S(2)}) collective-permute-start(bf16[1,4,128,1024]{3,2,1,0:T(8,128)(2,1)} %bitcast.72), channel_id=1, source_target_pairs={{0,8},{8,0},{16,24},{24,16},{1,9},{9,1},{17,25},{25,17},{2,10},{10... | collective-permute-start | bytes 3145736 | tf_op jit(solution)/shard_map/ppermute | solution.py:45
  321.8 32.4 %collective-permute-start.54 = (bf16[4,384,256]{2,1,0:T(8,128)(2,1)S(1)}, bf16[4,384,256]{2,1,0:T(8,128)(2,1)S(1)}, u32[]{:S(2)}, u32[]{:S(2)}) collective-permute-start(bf16[4,384,256]{2,1,0:T(8,128)(2,1)S(1)} %pad_maximum_fusion.29), channel_id=1, source_target_pairs={{0,1},{1,0},{2,3},{3,2},{4,5},{5,4},{6,7},{7,6},{8,9},{9,8},{10,11... | collective-permute-start | bytes 2359304 | tf_op jit(solution)/shard_map/ppermute | solution.py:45
  326.5 22.9 %collective-permute-start.32 = (bf16[1,2,128,1024]{3,2,1,0:T(8,128)(2,1)S(1)}, bf16[1,2,128,1024]{3,2,1,0:T(8,128)(2,1)S(1)}, u32[]{:S(2)}, u32[]{:S(2)}) collective-permute-start(bf16[1,2,128,1024]{3,2,1,0:T(8,128)(2,1)S(1)} %bitcast.447), channel_id=1, source_target_pairs={{0,1},{1,0},{2,3},{3,2},{4,5},{5,4},{6,7},{7,6},{8,9},{9,8},{10,11... | collective-permute-start | bytes 1572872 | tf_op jit(solution)/shard_map/ppermute | solution.py:45
  329.7 21.2 %collective-permute-start.30 = (bf16[2,128,1024]{2,1,0:T(8,128)(2,1)S(1)}, bf16[2,128,1024]{2,1,0:T(8,128)(2,1)S(1)}, u32[]{:S(2)}, u32[]{:S(2)}) collective-permute-start(bf16[2,128,1024]{2,1,0:T(8,128)(2,1)S(1)} %fusion.33), channel_id=1, source_target_pairs={{0,2},{1,3},{2,0},{3,1},{4,6},{5,7},{6,4},{7,5},{8,10},{9,11},{10,... | collective-permute-start | bytes 1572872 | tf_op jit(solution)/shard_map/ppermute | solution.py:45
  357.2 55.4 %collective-permute-start.55 = (bf16[1,8,384,256]{3,2,1,0:T(8,128)(2,1)}, bf16[1,8,384,256]{3,2,1,0:T(8,128)(2,1)}, u32[]{:S(2)}, u32[]{:S(2)}) collective-permute-start(bf16[1,8,384,256]{3,2,1,0:T(8,128)(2,1)} %get-tuple-element.102), channel_id=1, source_target_pairs={{0,16},{8,24},{16,0},{24,8},{1,17},{9,25},{17,1},{25,9},{2,18},{10... | collective-permute-start | bytes 4718600 | tf_op jit(solution)/shard_map/ppermute | solution.py:45
  374.4 32.1 %collective-permute-start.76 = (bf16[2,8,128,256]{3,2,1,0:T(8,128)(2,1)}, bf16[2,8,128,256]{3,2,1,0:T(8,128)(2,1)}, u32[]{:S(2)}, u32[]{:S(2)}) collective-permute-start(bf16[2,8,128,256]{3,2,1,0:T(8,128)(2,1)} %pad_maximum_fusion.26), channel_id=1, source_target_pairs={{0,8},{8,0},{16,24},{24,16},{1,9},{9,1},{17,25},{25,17},{2,10},{10... | collective-permute-start | bytes 3145736 | tf_op jit(solution)/shard_map/ppermute | solution.py:45
  376.3 24.9 %collective-permute-start.34 = (bf16[1,256,1024]{2,1,0:T(8,128)(2,1)S(1)}, bf16[1,256,1024]{2,1,0:T(8,128)(2,1)S(1)}, u32[]{:S(2)}, u32[]{:S(2)}) collective-permute-start(bf16[1,256,1024]{2,1,0:T(8,128)(2,1)S(1)} %convert_bitcast_fusion.1), channel_id=1, source_target_pairs={{0,16},{8,24},{16,0},{24,8},{1,17},{9,25},{17,1},{25,9},{2,18},{10... | collective-permute-start | bytes 1572872 | tf_op jit(solution)/shard_map/ppermute | solution.py:45
  402.3 23.7 %collective-permute-start.35 = (bf16[2,256,1024]{2,1,0:T(8,128)(2,1)}, bf16[2,256,1024]{2,1,0:T(8,128)(2,1)}, u32[]{:S(2)}, u32[]{:S(2)}) collective-permute-start(bf16[2,256,1024]{2,1,0:T(8,128)(2,1)} %pad_maximum_fusion.18), channel_id=1, source_target_pairs={{0,8},{8,0},{16,24},{24,16},{1,9},{9,1},{17,25},{25,17},{2,10},{10... | collective-permute-start | bytes 3145736 | tf_op jit(solution)/shard_map/ppermute | solution.py:45
  416.5 43.7 %collective-permute-start.56 = (bf16[2,8,384,256]{3,2,1,0:T(8,128)(2,1)}, bf16[2,8,384,256]{3,2,1,0:T(8,128)(2,1)}, u32[]{:S(2)}, u32[]{:S(2)}) collective-permute-start(bf16[2,8,384,256]{3,2,1,0:T(8,128)(2,1)} %pad_maximum_fusion.1), channel_id=1, source_target_pairs={{0,8},{8,0},{16,24},{24,16},{1,9},{9,1},{17,25},{25,17},{2,10},{10... | collective-permute-start | bytes 9437192 | tf_op jit(solution)/shard_map/ppermute | solution.py:45
  445.2 58.0 %collective-permute-start.36 = (bf16[2,256,1024]{2,1,0:T(8,128)(2,1)}, bf16[2,256,1024]{2,1,0:T(8,128)(2,1)}, u32[]{:S(2)}, u32[]{:S(2)}) collective-permute-start(bf16[2,256,1024]{2,1,0:T(8,128)(2,1)} %bitcast.85), channel_id=1, source_target_pairs={{0,8},{8,0},{16,24},{24,16},{1,9},{9,1},{17,25},{25,17},{2,10},{10... | collective-permute-start | bytes 3145736 | tf_op jit(solution)/shard_map/ppermute | solution.py:45
  448.7 56.7 %collective-permute-start.66 = (bf16[4,128,1024]{2,1,0:T(8,128)(2,1)}, bf16[4,128,1024]{2,1,0:T(8,128)(2,1)}, u32[]{:S(2)}, u32[]{:S(2)}) collective-permute-start(bf16[4,128,1024]{2,1,0:T(8,128)(2,1)} %bitcast.157), channel_id=1, source_target_pairs={{0,1},{1,0},{2,3},{3,2},{4,5},{5,4},{6,7},{7,6},{8,9},{9,8},{10,11... | collective-permute-start | bytes 3145736 | tf_op jit(solution)/shard_map/ppermute | solution.py:45
  458.6 50.7 %collective-permute-start.71 = (bf16[4,128,1024]{2,1,0:T(8,128)(2,1)}, bf16[4,128,1024]{2,1,0:T(8,128)(2,1)S(1)}, u32[]{:S(2)}, u32[]{:S(2)}) collective-permute-start(bf16[4,128,1024]{2,1,0:T(8,128)(2,1)} %bitcast.170), channel_id=1, source_target_pairs={{0,1},{1,0},{2,3},{3,2},{4,5},{5,4},{6,7},{7,6},{8,9},{9,8},{10,11... | collective-permute-start | bytes 3145736 | tf_op jit(solution)/shard_map/ppermute | solution.py:45
  459.1 42.7 %collective-permute-start.83 = (bf16[4,128,256]{2,1,0:T(8,128)(2,1)S(1)}, bf16[4,128,256]{2,1,0:T(8,128)(2,1)S(1)}, u32[]{:S(2)}, u32[]{:S(2)}) collective-permute-start(bf16[4,128,256]{2,1,0:T(8,128)(2,1)S(1)} %pad_maximum_fusion.41), channel_id=1, source_target_pairs={{0,1},{1,0},{2,3},{3,2},{4,5},{5,4},{6,7},{7,6},{8,9},{9,8},{10,11... | collective-permute-start | bytes 786440 | tf_op jit(solution)/shard_map/ppermute | solution.py:45
  508.2 73.2 %collective-permute-start.67 = (bf16[2,128,1024]{2,1,0:T(8,128)(2,1)}, bf16[2,128,1024]{2,1,0:T(8,128)(2,1)}, u32[]{:S(2)}, u32[]{:S(2)}) collective-permute-start(bf16[2,128,1024]{2,1,0:T(8,128)(2,1)} %slice.604), channel_id=1, source_target_pairs={{0,2},{1,3},{2,0},{3,1},{4,6},{5,7},{6,4},{7,5},{8,10},{9,11},{10,... | collective-permute-start | bytes 1572872 | tf_op jit(solution)/shard_map/ppermute | solution.py:45
  510.7 78.0 %collective-permute-start.72 = (bf16[2,128,1024]{2,1,0:T(8,128)(2,1)}, bf16[2,128,1024]{2,1,0:T(8,128)(2,1)}, u32[]{:S(2)}, u32[]{:S(2)}) collective-permute-start(bf16[2,128,1024]{2,1,0:T(8,128)(2,1)} %slice.603), channel_id=1, source_target_pairs={{0,2},{1,3},{2,0},{3,1},{4,6},{5,7},{6,4},{7,5},{8,10},{9,11},{10,... | collective-permute-start | bytes 1572872 | tf_op jit(solution)/shard_map/ppermute | solution.py:45
  515.9 180.0 %collective-permute-start.85 = (bf16[2,8,128,256]{3,2,1,0:T(8,128)(2,1)}, bf16[2,8,128,256]{3,2,1,0:T(8,128)(2,1)}, u32[]{:S(2)}, u32[]{:S(2)}) collective-permute-start(bf16[2,8,128,256]{3,2,1,0:T(8,128)(2,1)} %pad_maximum_fusion.27), channel_id=1, source_target_pairs={{0,8},{8,0},{16,24},{24,16},{1,9},{9,1},{17,25},{25,17},{2,10},{10... | collective-permute-start | bytes 3145736 | tf_op jit(solution)/shard_map/ppermute | solution.py:45
  600.8 103.9 %collective-permute-start.59 = (bf16[2,8,32,1024]{3,2,1,0:T(8,128)(2,1)}, bf16[2,8,32,1024]{3,2,1,0:T(8,128)(2,1)}, u32[]{:S(2)}, u32[]{:S(2)}) collective-permute-start(bf16[2,8,32,1024]{3,2,1,0:T(8,128)(2,1)} %pad_maximum_fusion.21), channel_id=1, source_target_pairs={{0,8},{8,0},{16,24},{24,16},{1,9},{9,1},{17,25},{25,17},{2,10},{10... | collective-permute-start | bytes 3145736 | tf_op jit(solution)/shard_map/ppermute | solution.py:45
  604.6 67.7 %collective-permute-start.68 = (bf16[1,128,1024]{2,1,0:T(8,128)(2,1)}, bf16[1,128,1024]{2,1,0:T(8,128)(2,1)}, u32[]{:S(2)}, u32[]{:S(2)}) collective-permute-start(bf16[1,128,1024]{2,1,0:T(8,128)(2,1)} %slice.610), channel_id=1, source_target_pairs={{0,4},{1,5},{2,6},{3,7},{4,0},{5,1},{6,2},{7,3},{8,12},{9,13},{10,... | collective-permute-start | bytes 786440 | tf_op jit(solution)/shard_map/ppermute | solution.py:45
  653.9 26.1 %collective-permute-start.73 = (bf16[1,128,1024]{2,1,0:T(8,128)(2,1)}, bf16[1,128,1024]{2,1,0:T(8,128)(2,1)S(1)}, u32[]{:S(2)}, u32[]{:S(2)}) collective-permute-start(bf16[1,128,1024]{2,1,0:T(8,128)(2,1)} %slice.609), channel_id=1, source_target_pairs={{0,4},{1,5},{2,6},{3,7},{4,0},{5,1},{6,2},{7,3},{8,12},{9,13},{10,... | collective-permute-start | bytes 786440 | tf_op jit(solution)/shard_map/ppermute | solution.py:45
  660.7 32.3 %collective-permute-start.57 = (bf16[1032,384]{1,0:T(8,128)(2,1)}, bf16[1032,384]{1,0:T(8,128)(2,1)}, u32[]{:S(2)}, u32[]{:S(2)}) collective-permute-start(bf16[1032,384]{1,0:T(8,128)(2,1)} %pad_maximum_fusion.28), channel_id=1, source_target_pairs={{0,8},{8,0},{16,24},{24,16},{1,9},{9,1},{17,25},{25,17},{2,10},{10... | collective-permute-start | bytes 2377736 | tf_op jit(solution)/shard_map/ppermute | solution.py:45
  694.4 52.3 %collective-permute-start.58 = (bf16[1032,384]{1,0:T(8,128)(2,1)S(1)}, bf16[1032,384]{1,0:T(8,128)(2,1)}, u32[]{:S(2)}, u32[]{:S(2)}) collective-permute-start(bf16[1032,384]{1,0:T(8,128)(2,1)S(1)} %add_convert_fusion.1), channel_id=1, source_target_pairs={{0,16},{8,24},{16,0},{24,8},{1,17},{9,25},{17,1},{25,9},{2,18},{10... | collective-permute-start | bytes 2377736 | tf_op jit(solution)/shard_map/ppermute | solution.py:45
  (172 other events, 1874.4 us)

commit v2 on v1

--- a/solution.py
+++ b/solution.py
@@ -235,6 +235,269 @@
         ),
         name="attend_back",
     )(lens, query, key, value, grad, lse)
+
+
+MESH = pl.DeviceIdType.MESH
+
+
+class Lattice:
+    def __init__(self, steps):
+        self.steps = steps
+        self.count = 1 << len(steps)
+
+    def peer(self, level):
+        axis, step = self.steps[level]
+        return {axis: lax.axis_index(axis) ^ step}
+
+    def shift(self, mask):
+        found = {"dp": 0, "tensor": 0}
+        for level, (axis, step) in enumerate(self.steps):
+            if mask >> level & 1:
+                found[axis] ^= step
+        return found["dp"], found["tensor"]
+
+
+def remote(src, dst, send, recv, peer):
+    return pltpu.make_async_remote_copy(
+        src_ref=src, dst_ref=dst, send_sem=send, recv_sem=recv, device_id=peer, device_id_type=MESH
+    )
+
+
+class Gather:
+    def __init__(self, lattice, view, send, recv, base=0, own=None):
+        self.lattice, self.view, self.send, self.recv, self.base = lattice, view, send, recv, base
+        self.own = own
+        self.sent = []
+
+    def copy(self, level, mask):
+        slot = self.base + (1 << level) + mask
+        place = self.view(mask)
+        src = self.own if mask == 0 and self.own is not None else place
+        return remote(src, place, self.send.at[slot], self.recv.at[slot], self.lattice.peer(level))
+
+    def start(self):
+        for level in range(len(self.lattice.steps)):
+            copy = self.copy(level, 0)
+            copy.start()
+            self.sent.append(copy)
+
+    def arrive(self, mask):
+        level = mask.bit_length() - 1
+        slot = self.base + mask
+        place = self.view(mask)
+        remote(place, place, self.send.at[slot], self.recv.at[slot], self.lattice.peer(level)).wait_recv()
+        for later in range(level + 1, len(self.lattice.steps)):
+            copy = self.copy(later, mask)
+            copy.start()
+            self.sent.append(copy)
+
+    def finish(self):
+        for copy in self.sent:
+            copy.wait_send()
+
+
+class Scatter:
+    def __init__(self, lattice, read, write, out, came, send, recv, base=0):
+        self.lattice, self.read, self.write = lattice, read, write
+        self.out, self.came, self.send, self.recv, self.base = out, came, send, recv, base
+        self.sent = []
+
+    def push(self, mask):
+        level = mask.bit_length() - 1
+        slot = self.base + mask
+        copy = remote(
+            self.out.at[mask - 1],
+            self.came.at[mask - 1],
+            self.send.at[slot],
+            self.recv.at[slot],
+            self.lattice.peer(level),
+        )
+        copy.start()
+        self.sent.append(copy)
+
+    def put(self, mask):
+        self.out[mask - 1] = self.read(mask).astype(BF)
+        self.push(mask)
+
+    def level(self, level):
+        for mask in reversed(range(1 << level)):
+            slot = (1 << level) + mask
+            place = self.came.at[slot - 1]
+            remote(
+                self.out.at[slot - 1],
+                place,
+                self.send.at[self.base + slot],
+                self.recv.at[self.base + slot],
+                self.lattice.peer(level),
+            ).wait_recv()
+            total = self.read(mask) + self.came[slot - 1].astype(F32)
+            if mask and mask >= 1 << (level - 1):
+                self.out[mask - 1] = total.astype(BF)
+                self.push(mask)
+            else:
+                self.write(mask, total)
+
+    def run(self):
+        for level in reversed(range(len(self.lattice.steps))):
+            self.level(level)
+
+    def finish(self):
+        for copy in self.sent:
+            copy.wait_send()
+
+
+def greet(peers):
+    barrier = pltpu.get_barrier_semaphore()
+    for peer in peers:
+        pl.semaphore_signal(barrier, inc=1, device_id=peer, device_id_type=MESH)
+    pl.semaphore_wait(barrier, len(peers))
+
+
+def score_kernel(
+    far_t, near_t, far_d, near_d,
+    vec, keep, lead, late, dense, grad,
+    rows_q, rows_p, raised, pull, sums, sums_in, sum_q, out_q, in_q, sum_p, out_p, in_p,
+    gq_send, gq_recv, gp_send, gp_recv, s_send, s_recv, rq_send, rq_recv, rp_send, rp_recv,
+):
+    group, rank = lax.axis_index("dp"), lax.axis_index("tensor")
+    share, width = vec.shape[0] // 2, vec.shape[1]
+    count_z = 1 << len(far_t)
+    count_y = 1 << len(far_d)
+    lattice_q = Lattice([("tensor", step) for step in far_t] + [("dp", step) for step in near_d])
+    lattice_p = Lattice([("dp", step) for step in far_d] + [("tensor", step) for step in near_t])
+    zs = [item for item in offsets(far_t) if item]
+    peers = [{"tensor": rank ^ item} for item in zs + near_t]
+    peers += [{"dp": group ^ item} for item in far_d + near_d]
+    greet(peers)
+
+    def spot_q(mask):
+        d, t = lattice_q.shift(mask)
+        return pl.multiple_of((((group ^ d) % 2) * count_z + (rank ^ t) // 2) * share, share)
+
+    def spot_p(mask):
+        d, t = lattice_p.shift(mask)
+        return pl.multiple_of((((rank ^ t) % 2) * count_y + (group ^ d) // 2) * share, share)
+
+    take_q = Gather(
+        lattice_q, lambda m: rows_q.at[pl.ds(spot_q(m), share)], gq_send, gq_recv, own=vec.at[pl.ds(0, share)]
+    )
+    take_p = Gather(
+        lattice_p, lambda m: rows_p.at[pl.ds(spot_p(m), share)], gp_send, gp_recv, own=vec.at[pl.ds(share, share)]
+    )
+    take_q.start()
+    take_p.start()
+    rows_q[pl.ds(spot_q(0), share), :] = vec[0:share, :]
+    rows_p[pl.ds(spot_p(0), share), :] = vec[share : 2 * share, :]
+    for mask in range(1, lattice_p.count):
+        take_p.arrive(mask)
+    for mask in range(1, lattice_q.count):
+        take_q.arrive(mask)
+
+    scale = float(width) ** 0.5
+    sums[...] = jnp.zeros_like(sums)
+    for block in range(lattice_p.count):
+        at = slice(block * share, (block + 1) * share)
+        dots = inner_rows(rows_p[at, :], rows_q[...])
+        value = jnp.where(keep[at, 0:1] > 0.0, jnp.exp(dots * scale - scale), 0.0)
+        raised[at, :] = value
+        which = block % count_y
+        sums[which : which + 1, :] += jnp.sum(value, axis=0, keepdims=True)
+    copies = []
+    for index, item in enumerate(zs):
+        copy = remote(sums, sums_in.at[index], s_send.at[index], s_recv.at[index], {"tensor": rank ^ item})
+        copy.start()
+        copies.append(copy)
+    total = sums[...]
+    for index, copy in enumerate(copies):
+        copy.wait_recv()
+        total = total + sums_in[index]
+    for block in range(lattice_p.count):
+        at = slice(block * share, (block + 1) * share)
+        which = block % count_y
+        ratio = late[which : which + 1, :] / total[which : which + 1, :]
+        pull[at, :] = (
+            raised[at, :] * ratio + jnp.where(lead[at, 0:1] > 0.0, dense[which : which + 1, :], 0.0)
+        ).astype(BF)
+
+    half_q = count_z * share
+    half_p = count_y * share
+    mine_q, mine_p = group % 2, rank % 2
+
+    def fill_q(half):
+        at = pl.ds(pl.multiple_of(half * half_q, half_q), half_q)
+        sum_q[at, :] = outer_rows(pull[:, at], rows_p[...])
+
+    def fill_p(half):
+        at = pl.ds(pl.multiple_of(half * half_p, half_p), half_p)
+        sum_p[at, :] = dot(pull[at, :], rows_q[...])
+
+    def reader(ref, spot):
+        return lambda m: ref[pl.ds(spot(m), share), :]
+
+    def writer(ref, spot):
+        def write(m, value):
+            ref[pl.ds(spot(m), share), :] = value
+
+        return write
+
+    give_q = Scatter(lattice_q, reader(sum_q, spot_q), writer(sum_q, spot_q), out_q, in_q, rq_send, rq_recv)
+    give_p = Scatter(lattice_p, reader(sum_p, spot_p), writer(sum_p, spot_p), out_p, in_p, rp_send, rp_recv)
+    fill_q(1 - mine_q)
+    for mask in reversed(range(lattice_q.count // 2, lattice_q.count)):
+        give_q.put(mask)
+    fill_p(1 - mine_p)
+    for mask in reversed(range(lattice_p.count // 2, lattice_p.count)):
+        give_p.put(mask)
+    fill_q(mine_q)
+    give_q.level(len(lattice_q.steps) - 1)
+    fill_p(mine_p)
+    give_p.run()
+    for level in reversed(range(len(lattice_q.steps) - 1)):
+        give_q.level(level)
+    grad[0:share, :] = sum_q[pl.ds(spot_q(0), share), :]
+    grad[share : 2 * share, :] = sum_p[pl.ds(spot_p(0), share), :]
+    for move in (take_q, take_p, give_q, give_p):
+        move.finish()
+    for copy in copies:
+        copy.wait_send()
+
+
+def score(vec, keep, lead, late, dense):
+    groups, ranks = lax.axis_size("dp"), lax.axis_size("tensor")
+    all_t, all_d = steps_of(ranks), steps_of(groups)
+    share, width = vec.shape[0] // 2, vec.shape[1]
+    blocks_q, blocks_p = ranks, groups
+    many_q, many_p = blocks_q * share, blocks_p * share
+    peers = ranks // 2 - 1
+    dma = pltpu.SemaphoreType.DMA
+    return pl.pallas_call(
+        functools.partial(score_kernel, all_t[:-1], all_t[-1:], all_d[:-1], all_d[-1:]),
+        out_shape=jax.ShapeDtypeStruct(vec.shape, F32),
+        in_specs=[pl.BlockSpec(memory_space=pltpu.VMEM)] * 5,
+        out_specs=pl.BlockSpec(memory_space=pltpu.VMEM),
+        scratch_shapes=[
+            pltpu.VMEM((many_q, width), BF),
+            pltpu.VMEM((many_p, width), BF),
+            pltpu.VMEM((many_p, many_q), F32),
+            pltpu.VMEM((many_p, many_q), BF),
+            pltpu.VMEM((8, many_q), F32),
+            pltpu.VMEM((peers, 8, many_q), F32),
+            pltpu.VMEM((many_q, width), F32),
+            pltpu.VMEM((blocks_q - 1, share, width), BF),
+            pltpu.VMEM((blocks_q - 1, share, width), BF),
+            pltpu.VMEM((many_p, width), F32),
+            pltpu.VMEM((blocks_p - 1, share, width), BF),
+            pltpu.VMEM((blocks_p - 1, share, width), BF),
+            dma((blocks_q,)), dma((blocks_q,)), dma((blocks_p,)), dma((blocks_p,)),
+            dma((peers,)), dma((peers,)),
+            dma((blocks_q,)), dma((blocks_q,)), dma((blocks_p,)), dma((blocks_p,)),
+        ],
+        compiler_params=pltpu.CompilerParams(
+            collective_id=1, has_side_effects=True, vmem_limit_bytes=48 * 2**20
+        ),
+        cost_estimate=pl.CostEstimate(flops=4 * 2**30, bytes_accessed=4 * 2**20, transcendentals=2**19),
+        name="score",
+    )(vec, keep, lead, late, dense)
 
 
 def per_device(
@@ -305,53 +568,27 @@
     inverse = lax.rsqrt(jnp.sum(chosen * chosen, axis=-1, keepdims=True) + 1e-06)
     unit = chosen * inverse
     vectors = unit.astype(BF)
-    rows_q = spread(spread(vectors[:share], "tensor", far_t), "dp", near_d).reshape(-1, width)
-    rows_p = spread(spread(vectors[share:], "dp", far_d), "tensor", near_t).reshape(-1, width)
-    off_zt, off_xt = jnp.array(offsets(far_t)), jnp.array(offsets(near_t))
-    off_yd, off_cd = jnp.array(offsets(far_d)), jnp.array(offsets(near_d))
-    count_z, count_x, count_y, count_c = len(off_zt), len(off_xt), len(off_yd), len(off_cd)
+    half_t, half_d = ranks // 2, groups // 2
     spot = jnp.arange(share)
-    place_q = jnp.broadcast_to(
-        ((rank ^ off_zt)[None, :, None] * share + spot[None, None, :]), (count_c, count_z, share)
-    )
-    group_q = group ^ off_cd
-    length_q = query_lengths[group_q]
-    valid_q = ((place_q >= 1) & (place_q < length_q[:, None, None])).reshape(-1)
+    group_q = (group // 2) * 2 + jnp.arange(2)
+    rank_q = jnp.arange(half_t) * 2 + rank % 2
+    place_q = jnp.broadcast_to(rank_q[None, :, None] * share + spot[None, None, :], (2, half_t, share))
+    valid_q = ((place_q >= 1) & (place_q < query_lengths[group_q][:, None, None])).reshape(-1)
     lead_q = (place_q == 0).reshape(-1)
-    place_p = jnp.broadcast_to(
-        ((rank ^ off_xt)[:, None, None] * share + spot[None, None, :]), (count_x, count_y, share)
-    )
-    group_p = group ^ off_yd
-    length_p = passage_lengths[group_p]
-    valid_p = (place_p >= 1) & (place_p < length_p[None, :, None])
-    lead_p = place_p == 0
+    group_p = jnp.arange(half_d) * 2 + group % 2
+    rank_p = (rank // 2) * 2 + jnp.arange(2)
+    place_p = jnp.broadcast_to(rank_p[:, None, None] * share + spot[None, None, :], (2, half_d, share))
+    valid_p = ((place_p >= 1) & (place_p < passage_lengths[group_p][None, :, None])).reshape(-1, 1)
+    lead_p = (place_p == 0).reshape(-1, 1)
     scale = float(width) ** 0.5
-    many_q = count_c * count_z * share
-    dots = inner_rows(rows_p, rows_q).reshape(count_x, count_y, share, many_q)
-    raised = jnp.where(valid_p[..., None], jnp.exp(dots * scale - scale), 0.0)
-    sums = jnp.sum(raised, axis=(0, 2)).reshape(count_y, count_c, count_z, share)
-    order = offsets(far_t)
-    for step in far_t:
-        came = swap(sums, "tensor", step)
-        came = jnp.stack([came[:, :, order.index(item ^ step)] for item in order], axis=2)
-        sums = sums + came
-    late = scale * colbert_cot[group_q][:, group_p].T
-    late = jnp.broadcast_to(late[:, :, None, None], (count_y, count_c, count_z, share))
-    late = jnp.where(valid_q[None], late.reshape(count_y, many_q) / sums.reshape(count_y, many_q), 0.0)
-    dense = 50.0 * dense_cot[group_q][:, group_p].T
-    dense = jnp.broadcast_to(dense[:, :, None], (count_y, count_c, count_z * share)).reshape(count_y, many_q)
-    dense = jnp.where(lead_q[None], dense, 0.0)
-    pull = raised * late[None, :, None, :] + jnp.where(lead_p[..., None], dense[None, :, None, :], 0.0)
-    pull = pull.astype(BF).reshape(-1, many_q)
-    grad_q = fold(
-        fold(outer_rows(pull, rows_p).reshape(count_c, count_z, share, width), "dp", near_d),
-        "tensor",
-        far_t,
-    )
-    grad_p = fold(
-        fold(dot(pull, rows_q).reshape(count_x, count_y, share, width), "tensor", near_t), "dp", far_d
-    )
-    grad_vec = jnp.concatenate([grad_q, grad_p])
+
+    def along(table):
+        wide = jnp.broadcast_to(table[group_q][:, group_p].T[:, :, None], (half_d, 2, half_t * share))
+        return wide.reshape(half_d, -1)
+
+    late = jnp.where(valid_q[None], scale * along(colbert_cot), 0.0)
+    dense = jnp.where(lead_q[None], 50.0 * along(dense_cot), 0.0)
+    grad_vec = score(vectors, valid_p.astype(F32), lead_p.astype(F32), late, dense)
 
     grad_chosen = inverse * (grad_vec - unit * jnp.sum(grad_vec * unit, axis=-1, keepdims=True))
     grad_proj = jnp.where(leading, 0.0, grad_chosen).astype(BF)

time: 771 us -> 705 us (0.914)
  Pallas kernels: 32.9 us -> 90 us
  waiting for transfers between devices: 253 us -> 200 us
  blocking collectives: 90.3 us -> 60.5 us
  other arithmetic: 84.2 us -> 72.3 us
  matrix products: 51.3 us -> 39.5 us
  starting transfers between devices: 120 us -> 111 us
    pallas_call x0 -> x1, Pallas kernels: none -> 57.2 us  [score(): pl.pallas_call(functools.partial(score_kernel, all_t[:-1], all_t[-1:], al...]
    ppermute x86 -> x74, waiting for transfers between devices: 253 us -> 200 us  [swap(): lax.ppermute(value, axis, [(index, index ^ step) for index in range(size)])]
    all_gather x1, blocking collectives: 49.7 us -> 21.4 us  [per_device(): bias_all = lax.all_gather(in_bias, 'tensor').reshape(ranks, groups, piece)]
    ppermute x86 -> x74, starting transfers between devices: 120 us -> 111 us  [swap(): lax.ppermute(value, axis, [(index, index ^ step) for index in range(size)])]
    concatenate x30 -> x28, other arithmetic: 34.7 us -> 29.2 us  [spread(): held = jnp.concatenate([held, swap(held, axis, step)], axis=0)]
    dot_general x5 -> x4, matrix products: 23.8 us -> 19.4 us  [inner_rows(): lax.dot_general(left, right, (((1,), (1,)), ((), ())), preferred_element_...]
    unnamed x275 -> x241, local copies, waits for them, and re-layouts: 44.2 us -> 39.9 us
  transfers between devices with their start and end apart: 86 -> 74, of which waited for: 35 -> 27; matrix products, arithmetic and copies ran while one was open for 25% -> 21% of each run, Pallas kernels for 4% -> 2%
where the time goes in v2:
time: 705 us; the launch traced here: 695 us
  waiting for transfers between devices  200 us (28%)
  starting transfers between devices  111 us (16%)
  local copies, waits for them, and re-layouts  96 us (14%)
  Pallas kernels  90 us (13%)
  other arithmetic  72.3 us (10%)
  blocking collectives  60.5 us (9%)
  matrix products  39.5 us (6%)
  between operations  26.4 us (4%)
    ppermute x74, waiting for transfers between devices, swap(): lax.ppermute(value, axis, [(index, index ^ step) for index in range(size)])  200 us
    ppermute x74, starting transfers between devices, swap(): lax.ppermute(value, axis, [(index, index ^ step) for index in range(size)])  111 us
    pallas_call x1, Pallas kernels, score(): pl.pallas_call(functools.partial(score_kernel, all_t[:-1], all_t[-1:], al...  57.2 us
    unnamed x241, local copies, waits for them, and re-layouts  39.9 us
    psum x1, blocking collectives, per_device(): small = lax.psum(small, ('dp', 'tensor'))  39.1 us
    concatenate x28, other arithmetic, spread(): held = jnp.concatenate([held, swap(held, axis, step)], axis=0)  29.2 us
    all_gather x1, blocking collectives, per_device(): bias_all = lax.all_gather(in_bias, 'tensor').reshape(ranks, groups, piece)  21.4 us
    dot_general x4, matrix products, inner_rows(): lax.dot_general(left, right, (((1,), (1,)), ((), ())), preferred_element_...  19.4 us
  transfers between devices with their start and end apart: 74, of which 27 were waited for; matrix products, arithmetic and copies ran while one was open for 21% of the time, Pallas kernels for 2%

profile of v2, /device:TPU:1, one launch (start us, length us, event | category | flops | bytes accessed | tf_op | source)
XLA Modules:
  0.0 694.9 jit_solution(9867525046248567349)
XLA Ops:
  4.7 4.7 pad_maximum_fusion.x
  9.4 15.9 %attend.1 = (bf16[2,1024,128]{2,1,0:T(8,128)(2,1)S(1)}, bf16[2,1024,128]{2,1,0:T(8,128)(2,1)S(1)}, bf16[2,1024,128]{2,1,0:T(8,128)(2,1)S(1)}, bf16[2,1024,128]{2,1,0:T(8,128)(2,1)S(1)}, f32[2,2,1024]{2,1,0:T(2,128)S(1)}) custom-call(s32[2]{0:T(128)S(1)} %pad_add_fusion.1.lens, bf16[2,1024,1024]{2,1,0:T(8,128)(2,1)} %pad_maximum_fusion.x, ...), custom_call_target="tpu_custom_call" | custom-call | flops 20000000000 | bytes 8388608 | tf_op jit(solution)/shard_map/attend/pallas_call | solution.py:197
  35.1 21.4 %all-gather.1 = bf16[8,1,512]{2,1,0:T(2,128)(2,1)S(1)} all-gather(bf16[1,1,512]{2,1,0:T(2,128)(2,1)S(1)} %reshape.525), channel_id=2, replica_groups=mesh['dp'=4,'tensor'=8] {'tensor'}, dimensions={0}, use_global_device_ids=true | all-gather | bytes 9216 | tf_op jit(solution)/shard_map/all_gather | solution.py:540
  72.4 6.7 collective-permute-done.10
  81.0 10.1 %collective-permute-start.11 = (bf16[2,8,32,1024]{3,2,0,1:T(8,128)(2,1)}, bf16[2,8,32,1024]{3,2,0,1:T(8,128)(2,1)}, u32[]{:S(2)}, u32[]{:S(2)}) collective-permute-start(bf16[2,8,32,1024]{3,2,0,1:T(8,128)(2,1)} %pad_maximum_fusion.11), channel_id=1, source_target_pairs={{0,8},{8,0},{16,24},{24,16},{1,9},{9,1},{17,25},{25,17},{2,10},{10... | collective-permute-start | bytes 3145736 | tf_op jit(solution)/shard_map/ppermute | solution.py:45
  114.1 14.2 %collective-permute-done.14 = bf16[1,128,1024]{2,1,0:T(8,128)(2,1)S(1)} collective-permute-done((bf16[1,128,1024]{2,1,0:T(8,128)(2,1)}, bf16[1,128,1024]{2,1,0:T(8,128)(2,1)S(1)}, u32[]{:S(2)}, u32[]{:S(2)}) %collective-permute-start.14) | collective-permute-done | bytes 262176 | tf_op jit(solution)/shard_map/ppermute | solution.py:45
  130.2 3.7 collective-permute-done.17
  148.6 7.8 %collective-permute-done.18 = bf16[2,128,1024]{2,1,0:T(8,128)(2,1)} collective-permute-done((bf16[2,128,1024]{2,1,0:T(8,128)(2,1)}, bf16[2,128,1024]{2,1,0:T(8,128)(2,1)}, u32[]{:S(2)}, u32[]{:S(2)}) %collective-permute-start.18) | collective-permute-done | bytes 524320 | tf_op jit(solution)/shard_map/ppermute | solution.py:45
  162.8 9.0 %collective-permute-done.16 = bf16[4,128,1024]{2,1,0:T(8,128)(2,1)} collective-permute-done((bf16[4,128,1024]{2,1,0:T(8,128)(2,1)}, bf16[4,128,1024]{2,1,0:T(8,128)(2,1)}, u32[]{:S(2)}, u32[]{:S(2)}) %collective-permute-start.16) | collective-permute-done | bytes 1048608 | tf_op jit(solution)/shard_map/ppermute | solution.py:45
  173.5 20.7 %collective-permute-done.19 = bf16[4,128,1024]{2,1,0:T(8,128)(2,1)} collective-permute-done((bf16[4,128,1024]{2,1,0:T(8,128)(2,1)}, bf16[4,128,1024]{2,1,0:T(8,128)(2,1)}, u32[]{:S(2)}, u32[]{:S(2)}) %collective-permute-start.19) | collective-permute-done | bytes 1048608 | tf_op jit(solution)/shard_map/ppermute | solution.py:45
  198.1 12.4 %fusion.2 = (bf16[1024,1024]{1,0:T(8,128)(2,1)S(1)}, f32[1024,1024]{1,0:T(8,128)}) fusion(f32[1024]{0:T(1024)S(1)} %bitcast_convert_fusion.5, bf16[1024,1024]{1,0:T(8,128)(2,1)S(1)} %bitcast.397, bf16[1024,1024]{1,0:T(8,128)(2,1)S(1)} %bitcast.395), kind=kOutput, calls=%fused_computation.10 | convolution fusion | flops 2216689664 | bytes 10489856 | tf_op jit(solution)/shard_map/dot_general | solution.py:21
  225.4 12.3 %collective-permute-done.21 = bf16[1,256,1024]{2,1,0:T(8,128)(2,1)S(1)} collective-permute-done((bf16[1,256,1024]{2,1,0:T(8,128)(2,1)S(1)}, bf16[1,256,1024]{2,1,0:T(8,128)(2,1)S(1)}, u32[]{:S(2)}, u32[]{:S(2)}) %collective-permute-start.21) | collective-permute-done | bytes 524320 | tf_op jit(solution)/shard_map/ppermute | solution.py:45
  239.8 57.2 %score.1 = f32[256,1024]{1,0:T(8,128)S(1)} custom-call(bf16[256,1024]{1,0:T(8,128)(2,1)S(1)} %multiply_convert_fusion.vec, f32[512,1]{1,0:T(8,128)S(1)} %copy.147.keep, f32[512,1]{1,0:T(8,128)S(1)} %copy.148.lead, f32[2,1024]{1,0:T(2,128)S(1)} %broadcast_select_fusion.2.late, f32[2,1024]{1,0:T(2,128)S(1)} %broadcast_select_fusion.1.dense), custom_call_target="tpu_custom_call" | custom-call | flops 4294967296 | bytes 4194304 | tf_op jit(solution)/shard_map/score/pallas_call | solution.py:473
  311.2 10.5 %collective-permute-done.40 = bf16[1,384,256]{2,1,0:T(8,128)(2,1)S(1)} collective-permute-done((bf16[1,384,256]{2,1,0:T(8,128)(2,1)S(1)}, bf16[1,384,256]{2,1,0:T(8,128)(2,1)S(1)}, u32[]{:S(2)}, u32[]{:S(2)}) %collective-permute-start.40) | collective-permute-done | bytes 196640 | tf_op jit(solution)/shard_map/ppermute | solution.py:45
  325.8 6.3 collective-permute-done.41
  361.7 4.1 convert_reduce_fusion
  374.9 4.1 collective-permute-start.24
  389.4 43.8 %collective-permute-done.71 = bf16[4,128,256]{2,1,0:T(8,128)(2,1)S(1)} collective-permute-done((bf16[4,128,256]{2,1,0:T(8,128)(2,1)S(1)}, bf16[4,128,256]{2,1,0:T(8,128)(2,1)S(1)}, u32[]{:S(2)}, u32[]{:S(2)}) %collective-permute-start.71) | collective-permute-done | bytes 262176 | tf_op jit(solution)/shard_map/ppermute | solution.py:45
  445.6 4.0 pad_maximum_fusion.1
  452.6 4.7 collective-permute-done.25
  458.5 39.1 %psum.7 = f32[11,1024]{1,0:T(8,128)S(1)} all-reduce(f32[11,1024]{1,0:T(8,128)S(1)} %concatenate.258), channel_id=1, replica_groups=mesh['dp'=4,'tensor'=8] {'dp','tensor'}, use_global_device_ids=true, to_apply=%region_19.20 | all-reduce | flops 11264 | bytes 90112 | tf_op jit(solution)/shard_map/psum | solution.py:679
  529.2 4.1 collective-permute-done.32
  533.5 17.0 %attend_back.1 = bf16[2,1024,384]{2,1,0:T(8,128)(2,1)S(1)} custom-call(s32[2]{0:T(128)S(1)} %pad_add_fusion.1.lens, bf16[2,1024,128]{2,1,0:T(8,128)(2,1)S(1)} %copy-done.5, bf16[2,1024,128]{2,1,0:T(8,128)(2,1)S(1)} %copy-done.7, bf16[2,1024,128]{2,1,0:T(8,128)(2,1)S(1)} %copy-done.9, bf16[2,1024,128]{2,1,0:T(8,128)(2,1)S(1)} %bitcast.364, ...), custom_call_target="tpu_custom_call" | custom-call | flops 40000000000 | bytes 8388608 | tf_op jit(solution)/shard_map/attend_back/pallas_call | solution.py:222
  565.8 3.6 collective-permute-done.35
  569.4 6.6 collective-permute-start.37
  576.2 6.8 collective-permute-done.37
  585.2 15.6 %collective-permute-start.45 = (bf16[1032,384]{1,0:T(8,128)(2,1)S(1)}, bf16[1032,384]{1,0:T(8,128)(2,1)S(1)}, u32[]{:S(2)}, u32[]{:S(2)}) collective-permute-start(bf16[1032,384]{1,0:T(8,128)(2,1)S(1)} %pad_maximum_fusion.25), channel_id=1, source_target_pairs={{0,8},{8,0},{16,24},{24,16},{1,9},{9,1},{17,25},{25,17},{2,10},{10... | collective-permute-start | bytes 2377736 | tf_op jit(solution)/shard_map/ppermute | solution.py:45
  607.4 8.7 %collective-permute-start.47 = (bf16[2,8,32,1024]{3,2,1,0:T(8,128)(2,1)S(1)}, bf16[2,8,32,1024]{3,2,1,0:T(8,128)(2,1)S(1)}, u32[]{:S(2)}, u32[]{:S(2)}) collective-permute-start(bf16[2,8,32,1024]{3,2,1,0:T(8,128)(2,1)S(1)} %copy-done.67), channel_id=1, source_target_pairs={{0,8},{8,0},{16,24},{24,16},{1,9},{9,1},{17,25},{25,17},{2,10},{10... | collective-permute-start | bytes 3145736 | tf_op jit(solution)/shard_map/ppermute | solution.py:45
  631.1 19.2 %collective-permute-done.48 = bf16[1,8,32,1024]{3,2,1,0:T(8,128)(2,1)S(1)} collective-permute-done((bf16[1,8,32,1024]{3,2,1,0:T(8,128)(2,1)S(1)}, bf16[1,8,32,1024]{3,2,1,0:T(8,128)(2,1)S(1)}, u32[]{:S(2)}, u32[]{:S(2)}) %collective-permute-start.48) | collective-permute-done | bytes 524320 | tf_op jit(solution)/shard_map/ppermute | solution.py:45
  652.8 4.5 collective-permute-done.49
  657.6 3.7 collective-permute-done.50
  670.2 5.1 collective-permute-start.53
  (586 shorter events, 260.9 us)
Async XLA Ops:
  27.2 72.7 %collective-permute-start = (bf16[2,128,128]{2,1,0:T(8,128)(2,1)}, bf16[2,128,128]{2,1,0:T(8,128)(2,1)}, u32[]{:S(2)}, u32[]{:S(2)}) collective-permute-start(bf16[2,128,128]{2,1,0:T(8,128)(2,1)} %get-tuple-element.153), channel_id=1, source_target_pairs={{0,4},{1,5},{2,6},{3,7},{4,0},{5,1},{6,2},{7,3},{8,12},{9,13},{10,... | collective-permute-start | bytes 196616 | tf_op jit(solution)/shard_map/ppermute | solution.py:45
  30.4 71.2 %collective-permute-start.1 = (bf16[2,128,128]{2,1,0:T(8,128)(2,1)}, bf16[2,128,128]{2,1,0:T(8,128)(2,1)}, u32[]{:S(2)}, u32[]{:S(2)}) collective-permute-start(bf16[2,128,128]{2,1,0:T(8,128)(2,1)} %get-tuple-element.152), channel_id=1, source_target_pairs={{0,2},{1,3},{2,0},{3,1},{4,6},{5,7},{6,4},{7,5},{8,10},{9,11},{10,... | collective-permute-start | bytes 196616 | tf_op jit(solution)/shard_map/ppermute | solution.py:45
  31.7 71.8 %collective-permute-start.2 = (bf16[2,128,128]{2,1,0:T(8,128)(2,1)}, bf16[2,128,128]{2,1,0:T(8,128)(2,1)}, u32[]{:S(2)}, u32[]{:S(2)}) collective-permute-start(bf16[2,128,128]{2,1,0:T(8,128)(2,1)} %get-tuple-element.151), channel_id=1, source_target_pairs={{0,6},{1,7},{2,4},{3,5},{4,2},{5,3},{6,0},{7,1},{8,14},{9,15},{10,... | collective-permute-start | bytes 196616 | tf_op jit(solution)/shard_map/ppermute | solution.py:45
  31.7 76.7 %collective-permute-start.3 = (bf16[2,128,128]{2,1,0:T(8,128)(2,1)}, bf16[2,128,128]{2,1,0:T(8,128)(2,1)}, u32[]{:S(2)}, u32[]{:S(2)}) collective-permute-start(bf16[2,128,128]{2,1,0:T(8,128)(2,1)} %get-tuple-element.150), channel_id=1, source_target_pairs={{0,1},{1,0},{2,3},{3,2},{4,5},{5,4},{6,7},{7,6},{8,9},{9,8},{10,11... | collective-permute-start | bytes 196616 | tf_op jit(solution)/shard_map/ppermute | solution.py:45
  33.8 26.9 %collective-permute-start.7 = (bf16[1,32,1024]{2,1,0:T(8,128)(2,1)S(1)}, bf16[1,32,1024]{2,1,0:T(8,128)(2,1)S(1)}, u32[]{:S(2)}, u32[]{:S(2)}) collective-permute-start(bf16[1,32,1024]{2,1,0:T(8,128)(2,1)S(1)} %dynamic-slice_bitcast_fusion.10), channel_id=1, source_target_pairs={{0,4},{1,5},{2,6},{3,7},{4,0},{5,1},{6,2},{7,3},{8,12},{9,13},{10,... | collective-permute-start | bytes 196616 | tf_op jit(solution)/shard_map/ppermute | solution.py:45
  81.0 53.9 %collective-permute-start.11 = (bf16[2,8,32,1024]{3,2,0,1:T(8,128)(2,1)}, bf16[2,8,32,1024]{3,2,0,1:T(8,128)(2,1)}, u32[]{:S(2)}, u32[]{:S(2)}) collective-permute-start(bf16[2,8,32,1024]{3,2,0,1:T(8,128)(2,1)} %pad_maximum_fusion.11), channel_id=1, source_target_pairs={{0,8},{8,0},{16,24},{24,16},{1,9},{9,1},{17,25},{25,17},{2,10},{10... | collective-permute-start | bytes 3145736 | tf_op jit(solution)/shard_map/ppermute | solution.py:45
  108.3 20.0 %collective-permute-start.14 = (bf16[1,128,1024]{2,1,0:T(8,128)(2,1)}, bf16[1,128,1024]{2,1,0:T(8,128)(2,1)S(1)}, u32[]{:S(2)}, u32[]{:S(2)}) collective-permute-start(bf16[1,128,1024]{2,1,0:T(8,128)(2,1)} %bitcast.387), channel_id=1, source_target_pairs={{0,4},{1,5},{2,6},{3,7},{4,0},{5,1},{6,2},{7,3},{8,12},{9,13},{10,... | collective-permute-start | bytes 786440 | tf_op jit(solution)/shard_map/ppermute | solution.py:45
  109.8 24.1 %collective-permute-start.17 = (bf16[1,128,1024]{2,1,0:T(8,128)(2,1)}, bf16[1,128,1024]{2,1,0:T(8,128)(2,1)S(1)}, u32[]{:S(2)}, u32[]{:S(2)}) collective-permute-start(bf16[1,128,1024]{2,1,0:T(8,128)(2,1)} %dynamic-slice_bitcast_fusion.2), channel_id=1, source_target_pairs={{0,4},{1,5},{2,6},{3,7},{4,0},{5,1},{6,2},{7,3},{8,12},{9,13},{10,... | collective-permute-start | bytes 786440 | tf_op jit(solution)/shard_map/ppermute | solution.py:45
  134.8 21.6 %collective-permute-start.18 = (bf16[2,128,1024]{2,1,0:T(8,128)(2,1)}, bf16[2,128,1024]{2,1,0:T(8,128)(2,1)}, u32[]{:S(2)}, u32[]{:S(2)}) collective-permute-start(bf16[2,128,1024]{2,1,0:T(8,128)(2,1)} %pad_maximum_fusion.28), channel_id=1, source_target_pairs={{0,2},{1,3},{2,0},{3,1},{4,6},{5,7},{6,4},{7,5},{8,10},{9,11},{10,... | collective-permute-start | bytes 1572872 | tf_op jit(solution)/shard_map/ppermute | solution.py:45
  140.6 19.8 %collective-permute-start.12 = (bf16[1,256,1024]{2,1,0:T(8,128)(2,1)}, bf16[1,256,1024]{2,1,0:T(8,128)(2,1)}, u32[]{:S(2)}, u32[]{:S(2)}) collective-permute-start(bf16[1,256,1024]{2,1,0:T(8,128)(2,1)} %fusion.29), channel_id=1, source_target_pairs={{0,16},{8,24},{16,0},{24,8},{1,17},{9,25},{17,1},{25,9},{2,18},{10... | collective-permute-start | bytes 1572872 | tf_op jit(solution)/shard_map/ppermute | solution.py:45
  147.5 24.3 %collective-permute-start.16 = (bf16[4,128,1024]{2,1,0:T(8,128)(2,1)}, bf16[4,128,1024]{2,1,0:T(8,128)(2,1)}, u32[]{:S(2)}, u32[]{:S(2)}) collective-permute-start(bf16[4,128,1024]{2,1,0:T(8,128)(2,1)} %pad_maximum_fusion.13), channel_id=1, source_target_pairs={{0,1},{1,0},{2,3},{3,2},{4,5},{5,4},{6,7},{7,6},{8,9},{9,8},{10,11... | collective-permute-start | bytes 3145736 | tf_op jit(solution)/shard_map/ppermute | solution.py:45
  158.6 35.7 %collective-permute-start.19 = (bf16[4,128,1024]{2,1,0:T(8,128)(2,1)}, bf16[4,128,1024]{2,1,0:T(8,128)(2,1)}, u32[]{:S(2)}, u32[]{:S(2)}) collective-permute-start(bf16[4,128,1024]{2,1,0:T(8,128)(2,1)} %pad_maximum_fusion.14), channel_id=1, source_target_pairs={{0,1},{1,0},{2,3},{3,2},{4,5},{5,4},{6,7},{7,6},{8,9},{9,8},{10,11... | collective-permute-start | bytes 3145736 | tf_op jit(solution)/shard_map/ppermute | solution.py:45
  161.7 34.2 %collective-permute-start.13 = (bf16[2,256,1024]{2,1,0:T(8,128)(2,1)S(1)}, bf16[2,256,1024]{2,1,0:T(8,128)(2,1)S(1)}, u32[]{:S(2)}, u32[]{:S(2)}) collective-permute-start(bf16[2,256,1024]{2,1,0:T(8,128)(2,1)S(1)} %pad_maximum_fusion.12), channel_id=1, source_target_pairs={{0,8},{8,0},{16,24},{24,16},{1,9},{9,1},{17,25},{25,17},{2,10},{10... | collective-permute-start | bytes 3145736 | tf_op jit(solution)/shard_map/ppermute | solution.py:45
  323.0 30.0 %collective-permute-start.65 = (bf16[1,8,128,256]{3,2,1,0:T(8,128)(2,1)}, bf16[1,8,128,256]{3,2,1,0:T(8,128)(2,1)}, u32[]{:S(2)}, u32[]{:S(2)}) collective-permute-start(bf16[1,8,128,256]{3,2,1,0:T(8,128)(2,1)} %slice.460), channel_id=1, source_target_pairs={{0,16},{8,24},{16,0},{24,8},{1,17},{9,25},{17,1},{25,9},{2,18},{10... | collective-permute-start | bytes 1572872 | tf_op jit(solution)/shard_map/ppermute | solution.py:45
  325.0 32.7 %collective-permute-start.23 = (bf16[2,256,1024]{2,1,0:T(8,128)(2,1)}, bf16[2,256,1024]{2,1,0:T(8,128)(2,1)}, u32[]{:S(2)}, u32[]{:S(2)}) collective-permute-start(bf16[2,256,1024]{2,1,0:T(8,128)(2,1)} %pad_maximum_fusion.15), channel_id=1, source_target_pairs={{0,8},{8,0},{16,24},{24,16},{1,9},{9,1},{17,25},{25,17},{2,10},{10... | collective-permute-start | bytes 3145736 | tf_op jit(solution)/shard_map/ppermute | solution.py:45
  333.1 21.9 %collective-permute-start.42 = (bf16[4,384,256]{2,1,0:T(8,128)(2,1)}, bf16[4,384,256]{2,1,0:T(8,128)(2,1)S(1)}, u32[]{:S(2)}, u32[]{:S(2)}) collective-permute-start(bf16[4,384,256]{2,1,0:T(8,128)(2,1)} %pad_maximum_fusion.26), channel_id=1, source_target_pairs={{0,1},{1,0},{2,3},{3,2},{4,5},{5,4},{6,7},{7,6},{8,9},{9,8},{10,11... | collective-permute-start | bytes 2359304 | tf_op jit(solution)/shard_map/ppermute | solution.py:45
  356.9 88.7 %collective-permute-start.43 = (bf16[1,8,384,256]{3,2,1,0:T(8,128)(2,1)}, bf16[1,8,384,256]{3,2,1,0:T(8,128)(2,1)S(1)}, u32[]{:S(2)}, u32[]{:S(2)}) collective-permute-start(bf16[1,8,384,256]{3,2,1,0:T(8,128)(2,1)} %get-tuple-element.102), channel_id=1, source_target_pairs={{0,16},{8,24},{16,0},{24,8},{1,17},{9,25},{17,1},{25,9},{2,18},{10... | collective-permute-start | bytes 4718600 | tf_op jit(solution)/shard_map/ppermute | solution.py:45
  374.9 58.8 %collective-permute-start.24 = (bf16[2,256,1024]{2,1,0:T(8,128)(2,1)}, bf16[2,256,1024]{2,1,0:T(8,128)(2,1)}, u32[]{:S(2)}, u32[]{:S(2)}) collective-permute-start(bf16[2,256,1024]{2,1,0:T(8,128)(2,1)} %bitcast.68), channel_id=1, source_target_pairs={{0,8},{8,0},{16,24},{24,16},{1,9},{9,1},{17,25},{25,17},{2,10},{10... | collective-permute-start | bytes 3145736 | tf_op jit(solution)/shard_map/ppermute | solution.py:45
  380.1 57.3 %collective-permute-start.54 = (bf16[4,128,1024]{2,1,0:T(8,128)(2,1)}, bf16[4,128,1024]{2,1,0:T(8,128)(2,1)}, u32[]{:S(2)}, u32[]{:S(2)}) collective-permute-start(bf16[4,128,1024]{2,1,0:T(8,128)(2,1)} %bitcast.140), channel_id=1, source_target_pairs={{0,1},{1,0},{2,3},{3,2},{4,5},{5,4},{6,7},{7,6},{8,9},{9,8},{10,11... | collective-permute-start | bytes 3145736 | tf_op jit(solution)/shard_map/ppermute | solution.py:45
  387.7 53.1 %collective-permute-start.59 = (bf16[4,128,1024]{2,1,0:T(8,128)(2,1)}, bf16[4,128,1024]{2,1,0:T(8,128)(2,1)}, u32[]{:S(2)}, u32[]{:S(2)}) collective-permute-start(bf16[4,128,1024]{2,1,0:T(8,128)(2,1)} %bitcast.153), channel_id=1, source_target_pairs={{0,1},{1,0},{2,3},{3,2},{4,5},{5,4},{6,7},{7,6},{8,9},{9,8},{10,11... | collective-permute-start | bytes 3145736 | tf_op jit(solution)/shard_map/ppermute | solution.py:45
  388.5 44.7 %collective-permute-start.71 = (bf16[4,128,256]{2,1,0:T(8,128)(2,1)S(1)}, bf16[4,128,256]{2,1,0:T(8,128)(2,1)S(1)}, u32[]{:S(2)}, u32[]{:S(2)}) collective-permute-start(bf16[4,128,256]{2,1,0:T(8,128)(2,1)S(1)} %pad_maximum_fusion.35), channel_id=1, source_target_pairs={{0,1},{1,0},{2,3},{3,2},{4,5},{5,4},{6,7},{7,6},{8,9},{9,8},{10,11... | collective-permute-start | bytes 786440 | tf_op jit(solution)/shard_map/ppermute | solution.py:45
  436.2 21.1 %collective-permute-start.25 = (bf16[1,256,1024]{2,1,0:T(8,128)(2,1)S(1)}, bf16[1,256,1024]{2,1,0:T(8,128)(2,1)S(1)}, u32[]{:S(2)}, u32[]{:S(2)}) collective-permute-start(bf16[1,256,1024]{2,1,0:T(8,128)(2,1)S(1)} %slice.464), channel_id=1, source_target_pairs={{0,16},{8,24},{16,0},{24,8},{1,17},{9,25},{17,1},{25,9},{2,18},{10... | collective-permute-start | bytes 1572872 | tf_op jit(solution)/shard_map/ppermute | solution.py:45
  440.2 70.1 %collective-permute-start.55 = (bf16[2,128,1024]{2,1,0:T(8,128)(2,1)}, bf16[2,128,1024]{2,1,0:T(8,128)(2,1)}, u32[]{:S(2)}, u32[]{:S(2)}) collective-permute-start(bf16[2,128,1024]{2,1,0:T(8,128)(2,1)} %slice.462), channel_id=1, source_target_pairs={{0,2},{1,3},{2,0},{3,1},{4,6},{5,7},{6,4},{7,5},{8,10},{9,11},{10,... | collective-permute-start | bytes 1572872 | tf_op jit(solution)/shard_map/ppermute | solution.py:45
  444.6 71.8 %collective-permute-start.60 = (bf16[2,128,1024]{2,1,0:T(8,128)(2,1)}, bf16[2,128,1024]{2,1,0:T(8,128)(2,1)}, u32[]{:S(2)}, u32[]{:S(2)}) collective-permute-start(bf16[2,128,1024]{2,1,0:T(8,128)(2,1)} %slice.461), channel_id=1, source_target_pairs={{0,2},{1,3},{2,0},{3,1},{4,6},{5,7},{6,4},{7,5},{8,10},{9,11},{10,... | collective-permute-start | bytes 1572872 | tf_op jit(solution)/shard_map/ppermute | solution.py:45
  449.6 234.6 %collective-permute-start.44 = (bf16[2,8,384,256]{3,2,1,0:T(8,128)(2,1)}, bf16[2,8,384,256]{3,2,1,0:T(8,128)(2,1)}, u32[]{:S(2)}, u32[]{:S(2)}) collective-permute-start(bf16[2,8,384,256]{3,2,1,0:T(8,128)(2,1)} %pad_maximum_fusion.1), channel_id=1, source_target_pairs={{0,8},{8,0},{16,24},{24,16},{1,9},{9,1},{17,25},{25,17},{2,10},{10... | collective-permute-start | bytes 9437192 | tf_op jit(solution)/shard_map/ppermute | solution.py:45
  452.6 167.5 %collective-permute-start.73 = (bf16[2,8,128,256]{3,2,1,0:T(8,128)(2,1)}, bf16[2,8,128,256]{3,2,1,0:T(8,128)(2,1)}, u32[]{:S(2)}, u32[]{:S(2)}) collective-permute-start(bf16[2,8,128,256]{3,2,1,0:T(8,128)(2,1)} %pad_maximum_fusion.24), channel_id=1, source_target_pairs={{0,8},{8,0},{16,24},{24,16},{1,9},{9,1},{17,25},{25,17},{2,10},{10... | collective-permute-start | bytes 3145736 | tf_op jit(solution)/shard_map/ppermute | solution.py:45
  500.6 20.3 %collective-permute-start.26 = (bf16[2,128,128]{2,1,0:T(8,128)(2,1)}, bf16[2,128,128]{2,1,0:T(8,128)(2,1)}, u32[]{:S(2)}, u32[]{:S(2)}) collective-permute-start(bf16[2,128,128]{2,1,0:T(8,128)(2,1)} %bitcast.360), channel_id=1, source_target_pairs={{0,4},{1,5},{2,6},{3,7},{4,0},{5,1},{6,2},{7,3},{8,12},{9,13},{10,... | collective-permute-start | bytes 196616 | tf_op jit(solution)/shard_map/ppermute | solution.py:45
  528.6 56.6 %collective-permute-start.56 = (bf16[1,128,1024]{2,1,0:T(8,128)(2,1)S(1)}, bf16[1,128,1024]{2,1,0:T(8,128)(2,1)}, u32[]{:S(2)}, u32[]{:S(2)}) collective-permute-start(bf16[1,128,1024]{2,1,0:T(8,128)(2,1)S(1)} %copy-done.76), channel_id=1, source_target_pairs={{0,4},{1,5},{2,6},{3,7},{4,0},{5,1},{6,2},{7,3},{8,12},{9,13},{10,... | collective-permute-start | bytes 786440 | tf_op jit(solution)/shard_map/ppermute | solution.py:45
  585.2 33.7 %collective-permute-start.45 = (bf16[1032,384]{1,0:T(8,128)(2,1)S(1)}, bf16[1032,384]{1,0:T(8,128)(2,1)S(1)}, u32[]{:S(2)}, u32[]{:S(2)}) collective-permute-start(bf16[1032,384]{1,0:T(8,128)(2,1)S(1)} %pad_maximum_fusion.25), channel_id=1, source_target_pairs={{0,8},{8,0},{16,24},{24,16},{1,9},{9,1},{17,25},{25,17},{2,10},{10... | collective-permute-start | bytes 2377736 | tf_op jit(solution)/shard_map/ppermute | solution.py:45
  607.4 21.2 %collective-permute-start.47 = (bf16[2,8,32,1024]{3,2,1,0:T(8,128)(2,1)S(1)}, bf16[2,8,32,1024]{3,2,1,0:T(8,128)(2,1)S(1)}, u32[]{:S(2)}, u32[]{:S(2)}) collective-permute-start(bf16[2,8,32,1024]{3,2,1,0:T(8,128)(2,1)S(1)} %copy-done.67), channel_id=1, source_target_pairs={{0,8},{8,0},{16,24},{24,16},{1,9},{9,1},{17,25},{25,17},{2,10},{10... | collective-permute-start | bytes 3145736 | tf_op jit(solution)/shard_map/ppermute | solution.py:45
  620.1 47.3 %collective-permute-start.46 = (bf16[1032,384]{1,0:T(8,128)(2,1)}, bf16[1032,384]{1,0:T(8,128)(2,1)}, u32[]{:S(2)}, u32[]{:S(2)}) collective-permute-start(bf16[1032,384]{1,0:T(8,128)(2,1)} %add_convert_fusion), channel_id=1, source_target_pairs={{0,16},{8,24},{16,0},{24,8},{1,17},{9,25},{17,1},{25,9},{2,18},{10... | collective-permute-start | bytes 2377736 | tf_op jit(solution)/shard_map/ppermute | solution.py:45
  629.0 21.3 %collective-permute-start.48 = (bf16[1,8,32,1024]{3,2,1,0:T(8,128)(2,1)S(1)}, bf16[1,8,32,1024]{3,2,1,0:T(8,128)(2,1)S(1)}, u32[]{:S(2)}, u32[]{:S(2)}) collective-permute-start(bf16[1,8,32,1024]{3,2,1,0:T(8,128)(2,1)S(1)} %slice.463), channel_id=1, source_target_pairs={{0,16},{8,24},{16,0},{24,8},{1,17},{9,25},{17,1},{25,9},{2,18},{10... | collective-permute-start | bytes 1572872 | tf_op jit(solution)/shard_map/ppermute | solution.py:45
  (139 other events, 1642.7 us)

commit v3 on v2

--- a/solution.py
+++ b/solution.py
@@ -116,125 +116,6 @@
 def head_mask(columns, head):
     lane = lax.broadcasted_iota(jnp.int32, (1, columns), 1)
     return (lane >= head * HEAD_DIM) & (lane < (head + 1) * HEAD_DIM)
-
-
-def attend_kernel(lens, x, w, b, q, k, v, ctx, lse):
-    span, columns = q.shape[1], q.shape[2]
-    heads = columns // HEAD_DIM
-    length = lens[pl.program_id(0)]
-    scale = HEAD_DIM**-0.5
-    rows = x[0]
-    q[0] = (dot(rows, w[0]) + b[0:1, :].astype(F32)).astype(BF)
-    k[0] = dot(rows, w[1]).astype(BF)
-    v[0] = (dot(rows, w[2]) + b[1:2, :].astype(F32)).astype(BF)
-    keys = k[0]
-    values = v[0]
-    keep = lax.broadcasted_iota(jnp.int32, (1, span), 1) < length
-    block = min(BLOCK, span)
-
-    @pl.loop(0, span // block)
-    def _(index):
-        at = pl.ds(pl.multiple_of(index * block, block), block)
-        query = q[0, at, :]
-        total = jnp.zeros((block, columns), F32)
-        for head in range(heads):
-            mask = head_mask(columns, head)
-            mine = jnp.where(mask, query, jnp.zeros_like(query)) * jnp.asarray(scale, BF)
-            scores = jnp.where(keep, inner_rows(mine, keys), -1e30)
-            top = jnp.max(scores, axis=-1, keepdims=True)
-            raised = jnp.exp(scores - top)
-            mass = jnp.sum(raised, axis=-1, keepdims=True)
-            part = dot(raised.astype(BF), values) / mass
-            total = jnp.where(mask, part, total)
-            column = jnp.broadcast_to(top + jnp.log(mass), (block, 128))
-            lse[0, head : head + 1, at] = column.T[0:1, :]
-        ctx[0, at, :] = total.astype(BF)
-
-
-def attend_back_kernel(lens, q, k, v, g, lse, out, dk_sum, dv_sum):
-    span, columns = q.shape[1], q.shape[2]
-    heads = columns // HEAD_DIM
-    length = lens[pl.program_id(0)]
-    scale = HEAD_DIM**-0.5
-    keys = k[0]
-    values = v[0]
-    keep = lax.broadcasted_iota(jnp.int32, (span, 1), 0) < length
-    block = min(BLOCK, span)
-    dk_sum[...] = jnp.zeros_like(dk_sum)
-    dv_sum[...] = jnp.zeros_like(dv_sum)
-
-    @pl.loop(0, span // block)
-    def _(index):
-        at = pl.ds(pl.multiple_of(index * block, block), block)
-        query = q[0, at, :]
-        grad = g[0, at, :]
-        total = jnp.zeros((block, columns), F32)
-        for head in range(heads):
-            mask = head_mask(columns, head)
-            mine = jnp.where(mask, query, jnp.zeros_like(query)) * jnp.asarray(scale, BF)
-            back = jnp.where(mask, grad, jnp.zeros_like(grad))
-            scores = jnp.where(keep, inner_rows(keys, mine), -1e30)
-            probs = jnp.exp(scores - lse[0, head : head + 1, at])
-            slope = inner_rows(values, back)
-            middle = jnp.sum(probs * slope, axis=0, keepdims=True)
-            turn = (probs * (slope - middle)).astype(BF)
-            dv_sum[...] += dot(probs.astype(BF), back)
-            dk_sum[...] += dot(turn, mine)
-            part = outer_rows(turn, keys) * scale
-            total = jnp.where(mask, part, total)
-        out[0, at, 0:columns] = total.astype(BF)
-
-    out[0, :, columns : 2 * columns] = dk_sum[...].astype(BF)
-    out[0, :, 2 * columns : 3 * columns] = dv_sum[...].astype(BF)
-
-
-def attend(lens, tokens, w_qkv, qv_bias):
-    count, span, width = tokens.shape
-    columns = w_qkv.shape[2]
-    heads = columns // HEAD_DIM
-    flat = jax.ShapeDtypeStruct((count, span, columns), BF)
-    rows = pl.BlockSpec((1, span, columns), lambda i, n: (i, 0, 0))
-    return pl.pallas_call(
-        attend_kernel,
-        out_shape=(flat, flat, flat, flat, jax.ShapeDtypeStruct((count, heads, span), F32)),
-        grid_spec=pltpu.PrefetchScalarGridSpec(
-            num_scalar_prefetch=1,
-            grid=(count,),
-            in_specs=[
-                pl.BlockSpec((1, span, width), lambda i, n: (i, 0, 0)),
-                pl.BlockSpec((3, width, columns), lambda i, n: (0, 0, 0)),
-                pl.BlockSpec((2, columns), lambda i, n: (0, 0)),
-            ],
-            out_specs=[rows, rows, rows, rows, pl.BlockSpec((1, heads, span), lambda i, n: (i, 0, 0))],
-        ),
-        compiler_params=pltpu.CompilerParams(vmem_limit_bytes=48 * 2**20),
-        cost_estimate=pl.CostEstimate(
-            flops=20 * 10**9, bytes_accessed=8 * 2**20, transcendentals=count * heads * span * span
-        ),
-        name="attend",
-    )(lens, tokens, w_qkv, qv_bias)
-
-
-def attend_back(lens, query, key, value, grad, lse):
-    count, span, columns = query.shape
-    heads = columns // HEAD_DIM
-    rows = pl.BlockSpec((1, span, columns), lambda i, n: (i, 0, 0))
-    return pl.pallas_call(
-        attend_back_kernel,
-        out_shape=jax.ShapeDtypeStruct((count, span, 3 * columns), BF),
-        grid_spec=pltpu.PrefetchScalarGridSpec(
-            num_scalar_prefetch=1,
-            grid=(count,),
-            in_specs=[rows, rows, rows, rows, pl.BlockSpec((1, heads, span), lambda i, n: (i, 0, 0))],
-            out_specs=pl.BlockSpec((1, span, 3 * columns), lambda i, n: (i, 0, 0)),
-            scratch_shapes=[pltpu.VMEM((span, columns), F32), pltpu.VMEM((span, columns), F32)],
-        ),
-        compiler_params=pltpu.CompilerParams(vmem_limit_bytes=48 * 2**20),
-        cost_estimate=pl.CostEstimate(
-            flops=40 * 10**9, bytes_accessed=8 * 2**20, transcendentals=count * heads * span * span
-        ),
-        name="attend_back",
-    )(lens, query, key, value, grad, lse)
 
 
 MESH = pl.DeviceIdType.MESH
@@ -500,6 +381,939 @@
     )(vec, keep, lead, late, dense)
 
 
+def forward_kernel(
+    all_t, all_d, ship_bias,
+    keep, x_q, x_p, w_qkv, qv_bias, w_out, up_piece, w_down, qkv_piece, bias_in, gain, shift, offset, w_colbert,
+    o_q, o_k, o_v, o_lse, o_ctx, o_out, o_up, o_down, o_qkv, o_normed, o_inner, o_active,
+    o_normal, o_vec, o_unit, o_low, o_spread,
+    x, q, k, v, ctx, lse, ctx_rows, out_all, up, down, normed, inner, active, sums, s_out, s_in,
+    first, normal, unit, vec, low, scales, wc, bias_all, bias_row,
+    local, g_send, g_recv, a_send, a_recv, b_send, b_recv, n_send, n_recv, r_send, r_recv,
+):
+    group, rank = lax.axis_index("dp"), lax.axis_index("tensor")
+    ranks, groups = 1 << len(all_t), 1 << len(all_d)
+    span, width = x_q.shape
+    columns = w_qkv.shape[2]
+    share = span // ranks
+    piece = up_piece.shape[0]
+    units = up.shape[0]
+    half, half3 = columns // 2, qkv_piece.shape[0]
+    rows = groups * share
+    heads = columns // HEAD_DIM
+    scale = HEAD_DIM**-0.5
+
+    x_copies = [pltpu.make_async_copy(src, x.at[s], local.at[s]) for s, src in enumerate((x_q, x_p))]
+    for copy in x_copies:
+        copy.start()
+    wc_copy = pltpu.make_async_copy(w_colbert, wc, local.at[2])
+    wc_copy.start()
+    greet([{"tensor": rank ^ item} for item in range(1, ranks)] + [{"dp": group ^ item} for item in all_d])
+
+    tensor = Lattice([("tensor", step) for step in all_t])
+    both = Lattice([("tensor", step) for step in all_t] + [("dp", all_d[-1])])
+    data = Lattice([("dp", step) for step in all_d])
+
+    def halves(ref, size):
+        def view(mask):
+            d, t = both.shift(mask)
+            return ref.at[rank ^ t, pl.ds(pl.multiple_of(((group ^ d) % 2) * size, size), size)]
+
+        return view
+
+    def unit_rows(ref):
+        return lambda mask: ref.at[pl.ds(pl.multiple_of((rank ^ tensor.shift(mask)[1]) * piece, piece), piece)]
+
+    wide, tall = both.count, tensor.count
+    at_half = pl.ds(pl.multiple_of((group % 2) * half, half), half)
+    at_piece = pl.ds(pl.multiple_of(group * piece, piece), piece)
+    take_out = Gather(both, halves(out_all, half), g_send, g_recv, 0, own=w_out.at[at_half])
+    take_up = Gather(tensor, unit_rows(up), g_send, g_recv, wide, own=up_piece)
+    take_down = Gather(tensor, unit_rows(down), g_send, g_recv, wide + tall, own=w_down.at[at_piece])
+    take_qkv = Gather(both, halves(o_qkv, half3), g_send, g_recv, wide + 2 * tall, own=qkv_piece)
+    own_copies = [
+        pltpu.make_async_copy(w_out.at[at_half], take_out.view(0), local.at[3]),
+        pltpu.make_async_copy(up_piece, take_up.view(0), local.at[4]),
+        pltpu.make_async_copy(w_down.at[at_piece], take_down.view(0), local.at[5]),
+        pltpu.make_async_copy(qkv_piece, take_qkv.view(0), local.at[6]),
+    ]
+    take_out.start()
+    take_up.start()
+    for copy in own_copies:
+        copy.start()
+    pending = []
+    bias_copies = []
+    if ship_bias:
+        bias_all[rank] = bias_in[...]
+        for item in range(1, ranks):
+            copy = remote(
+                bias_in, bias_all.at[rank], b_send.at[item], b_recv.at[item], {"tensor": rank ^ item}
+            )
+            copy.start()
+            bias_copies.append(copy)
+
+    def project(s):
+        x_copies[s].wait()
+        tokens = x[s]
+        q[s] = (dot(tokens, w_qkv[0]) + qv_bias[0:1, :].astype(F32)).astype(BF)
+        k[s] = dot(tokens, w_qkv[1]).astype(BF)
+        v[s] = (dot(tokens, w_qkv[2]) + qv_bias[1:2, :].astype(F32)).astype(BF)
+
+    block = min(BLOCK, span)
+
+    def attention(s, begin, end):
+        @pl.loop(begin, end)
+        def _(index):
+            at = pl.ds(pl.multiple_of(index * block, block), block)
+            query = q[s, at, :]
+            total = jnp.zeros((block, columns), F32)
+            for head in range(heads):
+                mask = head_mask(columns, head)
+                mine = jnp.where(mask, query, jnp.zeros_like(query)) * jnp.asarray(scale, BF)
+                scores = inner_rows(mine, k[s]) + keep[s : s + 1, :]
+                top = jnp.max(scores, axis=-1, keepdims=True)
+                raised = jnp.exp(scores - top)
+                mass = jnp.sum(raised, axis=-1, keepdims=True)
+                part = dot(raised.astype(BF), v[s]) / mass
+                total = jnp.where(mask, part, total)
+                column = jnp.broadcast_to(top + jnp.log(mass), (block, 128))
+                lse[s, head : head + 1, at] = column.T[0:1, :]
+            ctx[s, at, :] = total.astype(BF)
+
+    sends = []
+
+    def trade_context(s):
+        at = pl.ds(s * share, share)
+        for item in range(1, ranks):
+            peer = rank ^ item
+            copy = remote(
+                ctx.at[s, pl.ds(pl.multiple_of(peer * share, share), share)],
+                ctx_rows.at[rank, at],
+                a_send.at[s * ranks + item],
+                a_recv.at[s * ranks + item],
+                {"tensor": peer},
+            )
+            copy.start()
+            sends.append(copy)
+        ctx_rows[rank, s * share : (s + 1) * share, :] = ctx[s, pl.ds(pl.multiple_of(rank * share, share), share), :]
+
+    def context_here(s):
+        at = pl.ds(s * share, share)
+        for item in range(1, ranks):
+            place = ctx_rows.at[rank ^ item, at]
+            remote(
+                place, place, a_send.at[s * ranks + item], a_recv.at[s * ranks + item], {"tensor": rank ^ item}
+            ).wait_recv()
+
+    def out_going(src, dst, index):
+        copy = pltpu.make_async_copy(src, dst, local.at[index])
+        copy.start()
+        pending.append(copy)
+
+    project(0)
+    attention(0, 0, span // block)
+    trade_context(0)
+    for copy in own_copies:
+        copy.wait()
+    for mask in range(1, tall // 2):
+        take_out.arrive(mask)
+    take_down.start()
+    project(1)
+    attention(1, 0, span // block // 2)
+    for mask in range(1, tall // 2):
+        take_up.arrive(mask)
+    attention(1, span // block // 2, span // block)
+    trade_context(1)
+    for mask in range(tall // 2, wide):
+        take_out.arrive(mask)
+    out_going(q, o_q, 7)
+    out_going(k, o_k, 8)
+    out_going(v, o_v, 9)
+    out_going(lse, o_lse, 10)
+
+    normed_takes = []
+    for s in range(2):
+        at = slice(s * share, (s + 1) * share)
+        context_here(s)
+        if columns % 128 == 0:
+            mix = jnp.concatenate([ctx_rows[r, at, :] for r in range(ranks)], axis=1)
+            mixed = dot(mix, out_all[...].reshape(ranks * columns, width))
+        else:
+            mixed = dot(ctx_rows[0, at, :], out_all[0])
+            for r in range(1, ranks):
+                mixed = mixed + dot(ctx_rows[r, at, :], out_all[r])
+        mine = x[s, pl.ds(pl.multiple_of(rank * share, share), share), :].astype(F32)
+        value, plain, inverse = layer_norm(mine + mixed + offset[0:1, :], gain[0:1, :], shift[0:1, :])
+        first[at, :] = value
+        normal[0, at, :] = plain
+        scales[0, at, :] = jnp.broadcast_to(inverse, (share, 128))
+        own = pl.ds(pl.multiple_of(group * share, share), share)
+        normed[s, own, :] = value.astype(BF)
+
+        def view(mask, s=s):
+            d, _ = data.shift(mask)
+            return normed.at[s, pl.ds(pl.multiple_of((group ^ d) * share, share), share)]
+
+        taking = Gather(data, view, n_send, n_recv, s * groups)
+        taking.start()
+        normed_takes.append(taking)
+        for mask in range(1, tall // 2):
+            if s == 0:
+                take_down.arrive(mask)
+    take_qkv.start()
+    if ship_bias:
+        for item in range(1, ranks):
+            place = bias_all.at[rank ^ item]
+            remote(place, place, b_send.at[item], b_recv.at[item], {"tensor": rank ^ item}).wait_recv()
+        for r in range(ranks):
+            bias_row[0:1, r * piece : (r + 1) * piece] = bias_all[r, 0:1, :].astype(F32)
+    else:
+        bias_row[0:1, :] = bias_in[0:1, :]
+    for mask in range(tall // 2, tall):
+        take_up.arrive(mask)
+    for taking in normed_takes:
+        for mask in range(1, groups):
+            taking.arrive(mask)
+
+    def spot(mask):
+        return pl.multiple_of((group ^ data.shift(mask)[0]) * share, share)
+
+    gives = []
+    for s in range(2):
+
+        def read(mask, s=s):
+            return sums[s, pl.ds(spot(mask), share), :]
+
+        def write(mask, value, s=s):
+            sums[s, pl.ds(spot(mask), share), :] = value
+
+        gives.append(Scatter(data, read, write, s_out.at[s], s_in.at[s], r_send, r_recv, s * groups))
+
+    tile = min(256, units)
+
+    def expand(s):
+        at_rows = slice(s * rows, (s + 1) * rows)
+
+        @pl.loop(0, units // tile)
+        def _(index):
+            at = pl.ds(pl.multiple_of(index * tile, tile), tile)
+            value = inner_rows(normed[s], up[at, :]) + bias_row[0:1, at]
+            phi = 0.5 * (1.0 + lax.erf(value * 0.7071067811865476))
+            active[at_rows, at] = (value * phi).astype(BF)
+            inner[at_rows, at] = (phi + value * jnp.exp(-0.5 * value * value) * 0.3989422804014327).astype(BF)
+
+    def reduce(s):
+        at_rows = slice(s * rows, (s + 1) * rows)
+
+        @pl.loop(0, width // 256)
+        def _(index):
+            at = pl.ds(pl.multiple_of(index * 256, 256), 256)
+            sums[s, :, at] = dot(active[at_rows, :], down[:, at])
+
+        for mask in reversed(range(groups // 2, groups)):
+            gives[s].put(mask)
+
+    expand(0)
+    for mask in range(tall // 2, tall):
+        take_down.arrive(mask)
+    reduce(0)
+    for mask in range(1, tall // 2):
+        take_qkv.arrive(mask)
+    expand(1)
+    gives[0].level(len(all_d) - 1)
+    reduce(1)
+    out_going(ctx_rows, o_ctx, 11)
+    out_going(out_all, o_out, 12)
+    out_going(up, o_up, 13)
+    out_going(down, o_down, 14)
+    out_going(normed, o_normed, 15)
+    out_going(inner, o_inner, 16)
+    out_going(active, o_active, 17)
+    gives[1].level(len(all_d) - 1)
+    wc_copy.wait()
+    for s in range(2):
+        at = slice(s * share, (s + 1) * share)
+        for level in reversed(range(len(all_d) - 1)):
+            gives[s].level(level)
+        feed = gives[s].read(0)
+        value, plain, inverse = layer_norm(first[at, :] + feed + offset[1:2, :], gain[1:2, :], shift[1:2, :])
+        normal[1, at, :] = plain
+        scales[1, at, :] = jnp.broadcast_to(inverse, (share, 128))
+        short = value.astype(BF)
+        low[at, :] = short
+        place = lax.broadcasted_iota(jnp.int32, (share, 1), 0) + rank * share
+        chosen = jnp.where(place == 0, value, dot(short, wc[...]) + offset[2:3, :])
+        inverse = lax.rsqrt(jnp.sum(chosen * chosen, axis=-1, keepdims=True) + 1e-06)
+        scales[2, at, :] = jnp.broadcast_to(inverse, (share, 128))
+        unit[at, :] = chosen * inverse
+        vec[at, :] = unit[at, :].astype(BF)
+    out_going(normal, o_normal, 18)
+    out_going(unit, o_unit, 19)
+    out_going(vec, o_vec, 20)
+    out_going(low, o_low, 21)
+    out_going(scales, o_spread, 22)
+    for mask in range(tall // 2, wide):
+        take_qkv.arrive(mask)
+    for move in [take_out, take_up, take_down, take_qkv] + normed_takes + gives:
+        move.finish()
+    for copy in sends + bias_copies:
+        copy.wait_send()
+    for copy in pending:
+        copy.wait()
+
+
+def forward(keep, queries, passages, w_qkv, qv_bias, w_out, up_piece, w_down, qkv_piece, bias_in, gain, shift, offset, w_colbert):
+    groups, ranks = lax.axis_size("dp"), lax.axis_size("tensor")
+    all_t, all_d = steps_of(ranks), steps_of(groups)
+    span, width = queries.shape
+    columns = w_qkv.shape[2]
+    heads = columns // HEAD_DIM
+    share = span // ranks
+    piece = up_piece.shape[0]
+    units = piece * ranks
+    rows = groups * share
+    ship_bias = bias_in.shape[0] == 16
+
+    shapes = [
+        ((2, span, columns), BF),
+        ((2, span, columns), BF),
+        ((2, span, columns), BF),
+        ((2, heads, span), F32),
+        ((ranks, 2 * share, columns), BF),
+        ((ranks, columns, width), BF),
+        ((units, width), BF),
+        ((units, width), BF),
+        ((ranks, 3 * columns, width), BF),
+        ((2, rows, width), BF),
+        ((2 * rows, units), BF),
+        ((2 * rows, units), BF),
+        ((2, 2 * share, width), F32),
+        ((2 * share, width), BF),
+        ((2 * share, width), F32),
+        ((2 * share, width), BF),
+        ((3, 2 * share, 128), F32),
+    ]
+    dma = pltpu.SemaphoreType.DMA
+    vmem = pltpu.VMEM
+    hold, leave = pl.BlockSpec(memory_space=pltpu.VMEM), pl.BlockSpec(memory_space=pl.ANY)
+    n_gather = 6 * ranks
+    return pl.pallas_call(
+        functools.partial(forward_kernel, all_t, all_d, ship_bias),
+        out_shape=[jax.ShapeDtypeStruct(*item) for item in shapes],
+        in_specs=[hold, leave, leave, hold, hold, leave, leave, leave, leave, hold, hold, hold, hold, leave],
+        out_specs=[leave] * len(shapes),
+        scratch_shapes=[
+            vmem((2, span, width), BF),
+            vmem((2, span, columns), BF),
+            vmem((2, span, columns), BF),
+            vmem((2, span, columns), BF),
+            vmem((2, span, columns), BF),
+            vmem((2, heads, span), F32),
+            vmem((ranks, 2 * share, columns), BF),
+            vmem((ranks, columns, width), BF),
+            vmem((units, width), BF),
+            vmem((units, width), BF),
+            vmem((2, rows, width), BF),
+            vmem((2 * rows, units), BF),
+            vmem((2 * rows, units), BF),
+            vmem((2, rows, width), F32),
+            vmem((2, groups - 1, share, width), BF),
+            vmem((2, groups - 1, share, width), BF),
+            vmem((2 * share, width), F32),
+            vmem((2, 2 * share, width), F32),
+            vmem((2 * share, width), F32),
+            vmem((2 * share, width), BF),
+            vmem((2 * share, width), BF),
+            vmem((3, 2 * share, 128), F32),
+            vmem((width, width), BF),
+            vmem((ranks, 16, piece), BF),
+            vmem((8, units), F32),
+            dma((23,)),
+            dma((n_gather,)), dma((n_gather,)),
+            dma((2 * ranks,)), dma((2 * ranks,)),
+            dma((ranks,)), dma((ranks,)),
+            dma((2 * groups,)), dma((2 * groups,)),
+            dma((2 * groups,)), dma((2 * groups,)),
+        ],
+        compiler_params=pltpu.CompilerParams(
+            collective_id=2, has_side_effects=True, vmem_limit_bytes=58 * 2**20
+        ),
+        cost_estimate=pl.CostEstimate(flops=10**11, bytes_accessed=40 * 2**20, transcendentals=2**23),
+        name="forward",
+    )(keep, queries, passages, w_qkv, qv_bias, w_out, up_piece, w_down, qkv_piece, bias_in, gain, shift, offset, w_colbert)
+
+
+class Settle:
+    def __init__(self, lattice, view, came, send, recv, base=0):
+        self.lattice, self.view, self.came = lattice, view, came
+        self.send, self.recv, self.base = send, recv, base
+        self.sent = []
+
+    def copy(self, mask):
+        return remote(
+            self.view(mask),
+            self.came.at[mask - 1],
+            self.send.at[self.base + mask],
+            self.recv.at[self.base + mask],
+            self.lattice.peer(mask.bit_length() - 1),
+        )
+
+    def push(self, mask):
+        copy = self.copy(mask)
+        copy.start()
+        self.sent.append(copy)
+
+    def start(self):
+        for mask in reversed(range(self.lattice.count // 2, self.lattice.count)):
+            self.push(mask)
+
+    def level(self, level):
+        for mask in reversed(range(1 << level)):
+            slot = (1 << level) + mask
+            self.copy(slot).wait_recv()
+            place = self.view(mask)
+            place[...] = (place[...].astype(F32) + self.came[slot - 1].astype(F32)).astype(BF)
+            if mask and mask >= 1 << (level - 1):
+                self.push(mask)
+
+    def finish(self):
+        for copy in self.sent:
+            copy.wait_send()
+
+
+def backward_kernel(
+    all_t, all_d,
+    keep, grad_vec, h_unit, h_low, h_scales, h_normals, h_wc, h_down, h_up, h_slope, h_active, h_normed,
+    h_out, h_ctx, h_q, h_k, h_v, h_lse, x_q, x_p, h_qkv, gain,
+    o_tokens, o_down, o_up, o_out, o_wc, o_qkv, o_small,
+    pool, slope, active, out_all, wc, ctx_rows, q, k, v, lse, g1, unit, low, proj, normals, scales, sums,
+    s_out, s_in, turn, ctx_out, heads_grad, turned, turned_rows, dk_sum, dv_sum,
+    g_down, g_down_in, g_up, g_up_in, g_out_in, g_wc_in, qkv_sum, qkv_low, qkv_in,
+    small, small_in, stage, stage_in,
+    local, n_send, n_recv, r_send, r_recv, d_send, d_recv, u_send, u_recv, w_send, w_recv, c_send, c_recv,
+    a_send, a_recv, t_send, t_recv, f_send, f_recv, m_send, m_recv, y_send, y_recv, q_send, q_recv,
+):
+    group, rank = lax.axis_index("dp"), lax.axis_index("tensor")
+    ranks, groups = 1 << len(all_t), 1 << len(all_d)
+    far_d = all_d[:-1]
+    span, width = x_q.shape
+    columns = q.shape[2]
+    share = span // ranks
+    units = h_up.shape[0]
+    piece = units // ranks
+    half = columns // 2
+    rows = groups * share
+    heads = columns // HEAD_DIM
+    scale = HEAD_DIM**-0.5
+    flat = width // ranks // 2
+    at_up, at_down = pl.ds(0, units), pl.ds(units, units)
+    at_normed, at_feed = pl.ds(2 * units, 2 * rows), pl.ds(2 * units + 2 * rows, 2 * rows)
+    feed_at = 2 * units + 2 * rows
+
+    loads = []
+
+    def load(src, dst):
+        copy = pltpu.make_async_copy(src, dst, local.at[len(loads)])
+        copy.start()
+        loads.append(copy)
+        return copy
+
+    early = [load(grad_vec, g1), load(h_unit, unit), load(h_scales, scales), load(h_low, low), load(h_wc, wc)]
+    early.append(load(h_normals, normals))
+    ffn = [load(h_down, pool.at[at_down]), load(h_slope, slope), load(h_up, pool.at[at_up])]
+    later = [load(h_active, active), load(h_normed, pool.at[at_normed])]
+    last = [load(h_out, out_all), load(h_ctx, ctx_rows)]
+    heads_in = [load(h_q, q), load(h_k, k), load(h_v, v), load(h_lse, lse)]
+    greet([{"tensor": rank ^ item} for item in range(1, ranks)] + [{"dp": group ^ item} for item in all_d])
+
+    tensor = Lattice([("tensor", step) for step in all_t])
+    both = Lattice([("tensor", step) for step in all_t] + [("dp", all_d[-1])])
+    data = Lattice([("dp", step) for step in all_d])
+
+    def halves(ref, size):
+        def view(mask):
+            d, t = both.shift(mask)
+            return ref.at[pl.ds(pl.multiple_of(((rank ^ t) * 2 + (group ^ d) % 2) * size, size), size)]
+
+        return view
+
+    def pieces(ref):
+        return lambda mask: ref.at[pl.ds(pl.multiple_of((rank ^ tensor.shift(mask)[1]) * piece, piece), piece)]
+
+    def spot(mask):
+        return pl.multiple_of((group ^ data.shift(mask)[0]) * share, share)
+
+    give_wc = Settle(both, halves(wc, flat), g_wc_in, c_send, c_recv)
+    give_out = Settle(both, halves(out_all, half), g_out_in, w_send, w_recv)
+    give_down = Settle(tensor, pieces(g_down), g_down_in, d_send, d_recv)
+    give_up = Settle(tensor, pieces(g_up), g_up_in, u_send, u_recv)
+
+    small[...] = jnp.zeros_like(small)
+    for copy in early:
+        copy.wait()
+    takes = []
+    for s in range(2):
+        at = slice(s * share, (s + 1) * share)
+        grad, plain = g1[at, :], unit[at, :]
+        chosen = scales[2, at, 0:1] * (grad - plain * jnp.sum(grad * plain, axis=-1, keepdims=True))
+        leading = lax.broadcasted_iota(jnp.int32, (share, 1), 0) + rank * share == 0
+        short = jnp.where(leading, 0.0, chosen).astype(BF)
+        proj[at, :] = short
+        grad = jnp.where(leading, chosen, 0.0) + inner_rows(short, wc[...])
+        middle, gains, shifts = norm_back(grad, normals[1, at, :], scales[1, at, 0:1], gain[1:2, :])
+        g1[at, :] = middle
+        small[0, 1:2, :] += gains[None, :]
+        small[0, 3:4, :] += shifts[None, :]
+        small[0, 5:6, :] += jnp.sum(middle, axis=0, keepdims=True)
+        small[0, 6:7, :] += jnp.sum(short.astype(F32), axis=0, keepdims=True)
+        own = pl.multiple_of(feed_at + s * rows + group * share, share)
+        pool[pl.ds(own, share), :] = middle.astype(BF)
+
+        def view(mask, s=s):
+            place = feed_at + s * rows + (group ^ data.shift(mask)[0]) * share
+            return pool.at[pl.ds(pl.multiple_of(place, share), share)]
+
+        taking = Gather(data, view, n_send, n_recv, s * groups)
+        taking.start()
+        takes.append(taking)
+
+    @pl.loop(0, width // 256)
+    def _(index):
+        at = pl.ds(pl.multiple_of(index * 256, 256), 256)
+        wc[at, :] = outer_rows(low[:, at], proj[...]).astype(BF)
+
+    give_wc.start()
+
+    gives = []
+    for s in range(2):
+
+        def read(mask, s=s):
+            return sums[s, pl.ds(spot(mask), share), :]
+
+        def write(mask, value, s=s):
+            sums[s, pl.ds(spot(mask), share), :] = value
+
+        gives.append(Scatter(data, read, write, s_out.at[s], s_in.at[s], r_send, r_recv, s * groups))
+    for copy in ffn:
+        copy.wait()
+    tile = min(256, units)
+
+    def shrink(s):
+        for mask in range(1, groups):
+            takes[s].arrive(mask)
+        at_rows = slice(s * rows, (s + 1) * rows)
+        feed_rows = slice(feed_at + s * rows, feed_at + (s + 1) * rows)
+
+        @pl.loop(0, units // tile)
+        def _(index):
+            at = pl.ds(pl.multiple_of(index * tile, tile), tile)
+            down_at = pl.ds(pl.multiple_of(units + index * tile, tile), tile)
+            value = inner_rows(pool[feed_rows, :], pool[down_at, :]) * slope[at_rows, at].astype(F32)
+            value = value.astype(BF)
+            slope[at_rows, at] = value
+            small[0, 7:8, at] += jnp.sum(value.astype(F32), axis=0, keepdims=True)
+
+        @pl.loop(0, width // 256)
+        def _(index):
+            at = pl.ds(pl.multiple_of(index * 256, 256), 256)
+            sums[s, :, at] = dot(slope[at_rows, :], pool[at_up, at])
+
+    def put(s):
+        for mask in reversed(range(groups // 2, groups)):
+            gives[s].put(mask)
+
+    top = len(all_d) - 1
+    shrink(0)
+    put(0)
+    give_wc.level(len(all_t))
+    shrink(1)
+    gives[0].level(top)
+    put(1)
+    for copy in later:
+        copy.wait()
+
+    @pl.loop(0, units // tile)
+    def _(index):
+        at = pl.ds(pl.multiple_of(index * tile, tile), tile)
+        g_down[at, :] = outer_rows(active[:, at], pool[at_feed, :]).astype(BF)
+
+    gives[1].level(top)
+    give_down.start()
+    give_wc.level(len(all_t) - 1)
+
+    @pl.loop(0, units // tile)
+    def _(index):
+        at = pl.ds(pl.multiple_of(index * tile, tile), tile)
+        g_up[at, :] = outer_rows(slope[:, at], pool[at_normed, :]).astype(BF)
+
+    for copy in last:
+        copy.wait()
+    sends = []
+    for s in range(2):
+        at = slice(s * share, (s + 1) * share)
+        for level in reversed(range(top)):
+            gives[s].level(level)
+        grad = g1[at, :] + gives[s].read(0)
+        hidden, gains, shifts = norm_back(grad, normals[0, at, :], scales[0, at, 0:1], gain[0:1, :])
+        g1[at, :] = hidden
+        small[0, 0:1, :] += gains[None, :]
+        small[0, 2:3, :] += shifts[None, :]
+        small[0, 4:5, :] += jnp.sum(hidden, axis=0, keepdims=True)
+        short = hidden.astype(BF)
+        turn[at, :] = short
+        if columns % 128 == 0:
+            value = inner_rows(short, out_all[...]).astype(BF)
+            for r in range(ranks):
+                ctx_out[r, at, :] = value[:, r * columns : (r + 1) * columns]
+        else:
+            for r in range(ranks):
+                ctx_out[r, at, :] = inner_rows(short, out_all[r * columns : (r + 1) * columns, :]).astype(BF)
+        mine = pl.ds(pl.multiple_of(rank * share, share), share)
+        for item in range(1, ranks):
+            copy = remote(
+                ctx_out.at[rank ^ item, pl.ds(s * share, share)],
+                heads_grad.at[s, mine],
+                a_send.at[s * ranks + item],
+                a_recv.at[s * ranks + item],
+                {"tensor": rank ^ item},
+            )
+            copy.start()
+            sends.append(copy)
+        heads_grad[s, mine, :] = ctx_out[rank, at, :]
+    give_up.start()
+    for taking in takes:
+        taking.finish()
+    tall = load(x_q, pool.at[pl.ds(0, span)]), load(x_p, pool.at[pl.ds(span, span)])
+    at_qkv = 2 * span
+    back_in = load(h_qkv, pool.at[pl.ds(at_qkv, 3 * columns * ranks)])
+
+    for r in range(ranks):
+        out_all[r * columns : (r + 1) * columns, :] = outer_rows(ctx_rows[r], turn[...]).astype(BF)
+    give_out.start()
+
+    def small_step(level):
+        copy = remote(
+            small.at[level], small_in.at[level], m_send.at[level], m_recv.at[level], {"tensor": rank ^ all_t[level]}
+        )
+        return copy
+
+    small_copies = [small_step(level) for level in range(len(all_t))]
+    small_copies[0].start()
+
+    def small_next(level):
+        small_copies[level].wait_recv()
+        small[level + 1] = small[level] + small_in[level]
+        if level + 1 < len(all_t):
+            small_copies[level + 1].start()
+
+    block = min(BLOCK, span)
+
+    def attention(s, begin, end):
+        @pl.loop(begin, end)
+        def _(index):
+            at = pl.ds(pl.multiple_of(index * block, block), block)
+            query = q[s, at, :]
+            grad = heads_grad[s, at, :]
+            total = jnp.zeros((block, columns), F32)
+            for head in range(heads):
+                mask = head_mask(columns, head)
+                mine = jnp.where(mask, query, jnp.zeros_like(query)) * jnp.asarray(scale, BF)
+                back = jnp.where(mask, grad, jnp.zeros_like(grad))
+                scores = inner_rows(k[s], mine) + keep[:, s : s + 1]
+                probs = jnp.exp(scores - lse[s, head : head + 1, at])
+                slant = inner_rows(v[s], back)
+                middle = jnp.sum(probs * slant, axis=0, keepdims=True)
+                twist = (probs * (slant - middle)).astype(BF)
+                dv_sum[...] += dot(probs.astype(BF), back)
+                dk_sum[...] += dot(twist, mine)
+                part = outer_rows(twist, k[s]) * scale
+                total = jnp.where(mask, part, total)
+            turned[s, at, 0:columns] = total.astype(BF)
+
+    def attention_start(s):
+        for item in range(1, ranks):
+            place = heads_grad.at[s, pl.ds(pl.multiple_of((rank ^ item) * share, share), share)]
+            remote(
+                place, place, a_send.at[s * ranks + item], a_recv.at[s * ranks + item], {"tensor": rank ^ item}
+            ).wait_recv()
+        dk_sum[...] = jnp.zeros_like(dk_sum)
+        dv_sum[...] = jnp.zeros_like(dv_sum)
+
+    def attention_end(s):
+        turned[s, :, columns : 2 * columns] = dk_sum[...].astype(BF)
+        turned[s, :, 2 * columns : 3 * columns] = dv_sum[...].astype(BF)
+        for item in range(1, ranks):
+            copy = remote(
+                turned.at[s, pl.ds(pl.multiple_of((rank ^ item) * share, share), share)],
+                turned_rows.at[rank, pl.ds(s * share, share)],
+                t_send.at[s * ranks + item],
+                t_recv.at[s * ranks + item],
+                {"tensor": rank ^ item},
+            )
+            copy.start()
+            sends.append(copy)
+        turned_rows[rank, s * share : (s + 1) * share, :] = turned[
+            s, pl.ds(pl.multiple_of(rank * share, share), share), :
+        ]
+
+    many = qkv_sum.shape[0]
+
+    def qkv_grad(s):
+        tokens = pool[s * span : (s + 1) * span, :]
+        line = jnp.sum(turned[s].astype(F32), axis=0, keepdims=True)
+        if s == 0:
+            qkv_sum[0:width, :] = outer_rows(tokens, turned[s])
+            qkv_sum[width:many, :] = jnp.broadcast_to(line, (many - width, 3 * columns))
+        else:
+            qkv_sum[0:width, :] += outer_rows(tokens, turned[s])
+            qkv_sum[width:many, :] += jnp.broadcast_to(line, (many - width, 3 * columns))
+
+    for copy in heads_in:
+        copy.wait()
+    attention_start(0)
+    attention(0, 0, span // block // 2)
+    give_wc.level(len(all_t) - 2)
+    small_next(0)
+    attention(0, span // block // 2, span // block)
+    attention_end(0)
+    give_out.level(len(all_t))
+    for copy in tall:
+        copy.wait()
+    qkv_grad(0)
+    attention_start(1)
+    attention(1, 0, span // block // 2)
+    for level in reversed(range(len(all_t) - 2)):
+        give_wc.level(level)
+    small_next(1)
+    give_down.level(len(all_t) - 1)
+    attention(1, span // block // 2, span // block)
+    attention_end(1)
+    qkv_grad(1)
+
+    part = many // 2
+    mine_half, other_half = group % 2, 1 - group % 2
+    at_mine = pl.ds(pl.multiple_of(mine_half * part, part), part)
+    at_other = pl.ds(pl.multiple_of(other_half * part, part), part)
+    qkv_low[0] = qkv_sum[at_other, :].astype(BF)
+    near = {"dp": group ^ all_d[-1]}
+    qkv_copy = remote(qkv_low.at[0], qkv_in.at[0], q_send.at[0], q_recv.at[0], near)
+    qkv_copy.start()
+
+    def settle_stage(which, source, size):
+        copies = []
+        base = which * (len(far_d) + 1)
+        for index, step in enumerate(far_d):
+            src = source if index == 0 else stage.at[base + index - 1, pl.ds(0, size)]
+            dst = stage_in.at[base + index, pl.ds(0, size)]
+            slot = base + index
+            copies.append(remote(src, dst, y_send.at[slot], y_recv.at[slot], {"dp": group ^ step}))
+
+        def begin():
+            copies[0].start()
+
+        def end():
+            value = source[...]
+            for index, copy in enumerate(copies):
+                copy.wait_recv()
+                value = (value.astype(F32) + stage_in[base + index, 0:size, :].astype(F32)).astype(BF)
+                stage[base + index, 0:size, :] = value
+                if index + 1 < len(copies):
+                    copies[index + 1].start()
+            return stage.at[base + len(copies) - 1, pl.ds(0, size)]
+
+        return begin, end, copies
+
+    wc_begin, wc_end, wc_copies = settle_stage(0, give_wc.view(0), flat)
+    out_begin, out_end, out_copies = settle_stage(1, give_out.view(0), half)
+    wc_begin()
+    for level in reversed(range(len(all_t))):
+        if level < len(all_t):
+            give_out.level(level)
+    out_begin()
+    small_next(2) if len(all_t) > 2 else None
+    for level in range(3, len(all_t)):
+        small_next(level)
+    small_own = small.at[len(all_t)]
+    small_take = Gather(data, lambda m: o_small.at[group ^ data.shift(m)[0]], f_send, f_recv, 0, own=small_own)
+    small_take.start()
+    small_copy = load(small_own, o_small.at[group])
+    qkv_copy.wait_recv()
+    sum_half = qkv_sum[at_mine, :].astype(BF).astype(F32) + qkv_in[0].astype(F32)
+    qkv_low[1] = sum_half.astype(BF)
+    qkv_copies = [qkv_copy]
+    for index, step in enumerate(far_d):
+        copy = remote(
+            qkv_low.at[1 + index], qkv_in.at[1 + index], q_send.at[1 + index], q_recv.at[1 + index], {"dp": group ^ step}
+        )
+        qkv_copies.append(copy)
+    qkv_copies[1].start()
+    wc_own = wc_end()
+    wc_take = Gather(both, halves(o_wc, flat), f_send, f_recv, groups, own=wc_own)
+    wc_take.start()
+    wc_copy = load(wc_own, wc_take.view(0))
+    for level in reversed(range(len(all_t) - 1)):
+        give_down.level(level)
+    down_own = give_down.view(0)
+
+    def dp_view(ref):
+        return lambda m: ref.at[pl.ds(pl.multiple_of((group ^ data.shift(m)[0]) * piece, piece), piece)]
+
+    down_take = Gather(data, dp_view(o_down), f_send, f_recv, groups + both.count, own=down_own)
+    down_take.start()
+    down_copy = load(down_own, down_take.view(0))
+    for index in range(len(far_d)):
+        qkv_copies[1 + index].wait_recv()
+        qkv_low[2 + index] = (qkv_low[1 + index].astype(F32) + qkv_in[1 + index].astype(F32)).astype(BF)
+        if index + 2 < len(qkv_copies):
+            qkv_copies[index + 2].start()
+    qkv_own = qkv_low.at[1 + len(far_d)]
+    last_qkv = remote(qkv_own, o_qkv.at[at_mine], q_send.at[1 + len(far_d)], q_recv.at[1 + len(far_d)], near)
+    last_qkv.start()
+    qkv_copies.append(last_qkv)
+    qkv_local = load(qkv_own, o_qkv.at[at_mine])
+    out_own = out_end()
+
+    def out_view(mask):
+        return o_out.at[pl.ds(pl.multiple_of(((group % 2) ^ mask) * half, half), half)]
+
+    core = Lattice([("dp", all_d[-1])])
+    out_take = Gather(core, out_view, f_send, f_recv, 2 * groups + both.count, own=out_own)
+    out_take.start()
+    out_copy = load(out_own, out_view(0))
+    for mask in range(1, both.count // 2):
+        wc_take.arrive(mask)
+
+    back_in.wait()
+    for s in range(2):
+        at = slice(s * share, (s + 1) * share)
+        for item in range(1, ranks):
+            place = turned_rows.at[rank ^ item, pl.ds(s * share, share)]
+            remote(
+                place, place, t_send.at[s * ranks + item], t_recv.at[s * ranks + item], {"tensor": rank ^ item}
+            ).wait_recv()
+        total = g1[at, :]
+        for r in range(ranks):
+            begin = at_qkv + r * 3 * columns
+            total = total + dot(turned_rows[r, at, :], pool[begin : begin + 3 * columns, :])
+        unit[at, :] = total
+    tokens_copy = load(unit, o_tokens)
+    for level in reversed(range(len(all_t))):
+        give_up.level(level)
+    up_own = give_up.view(0)
+    up_take = Gather(data, dp_view(o_up), f_send, f_recv, 2 * groups + both.count + 2, own=up_own)
+    up_take.start()
+    up_copy = load(up_own, up_take.view(0))
+    for mask in range(both.count // 2, both.count):
+        wc_take.arrive(mask)
+    for taking in (small_take, down_take, up_take):
+        for mask in range(1, groups):
+            taking.arrive(mask)
+    out_take.arrive(1)
+    at_theirs = o_qkv.at[at_other]
+    remote(at_theirs, at_theirs, q_send.at[1 + len(far_d)], q_recv.at[1 + len(far_d)], near).wait_recv()
+    for move in [give_wc, give_out, give_down, give_up, small_take, wc_take, down_take, up_take, out_take] + gives:
+        move.finish()
+    for copy in sends + small_copies + qkv_copies + wc_copies + out_copies:
+        copy.wait_send()
+    for copy in (tokens_copy, small_copy, wc_copy, down_copy, qkv_local, out_copy, up_copy):
+        copy.wait()
+
+
+def backward(keep, grad_vec, unit, low, scales, normals, w_colbert, down, up, slope, active, normed, out_all,
+             context_rows, query, key, value, lse, queries, passages, qkv_all, gain):
+    groups, ranks = lax.axis_size("dp"), lax.axis_size("tensor")
+    all_t, all_d = steps_of(ranks), steps_of(groups)
+    span, width = queries.shape
+    columns = query.shape[2]
+    heads = columns // HEAD_DIM
+    share = span // ranks
+    units = up.shape[0]
+    piece = units // ranks
+    rows = groups * share
+    half, flat = columns // 2, width // ranks // 2
+    pool = max(2 * units + 4 * rows, 2 * span + 3 * columns * ranks)
+    many = width + 32
+    far = len(all_d) - 1
+    dma = pltpu.SemaphoreType.DMA
+    vmem = pltpu.VMEM
+    hold, leave = pl.BlockSpec(memory_space=pltpu.VMEM), pl.BlockSpec(memory_space=pl.ANY)
+    shapes = [
+        ((2 * share, width), F32),
+        ((units // ranks * groups, width), BF),
+        ((units // ranks * groups, width), BF),
+        ((columns, width), BF),
+        ((width, width), BF),
+        ((many, 3 * columns), BF),
+        ((groups, 8, width), F32),
+    ]
+    pair = lambda count: [dma((count,)), dma((count,))]
+    return pl.pallas_call(
+        functools.partial(backward_kernel, all_t, all_d),
+        out_shape=[jax.ShapeDtypeStruct(*item) for item in shapes],
+        in_specs=[hold] + [leave] * 20 + [hold],
+        out_specs=[leave] * len(shapes),
+        scratch_shapes=[
+            vmem((pool, width), BF),
+            vmem((2 * rows, units), BF),
+            vmem((2 * rows, units), BF),
+            vmem((ranks * columns, width), BF),
+            vmem((width, width), BF),
+            vmem((ranks, 2 * share, columns), BF),
+            vmem((2, span, columns), BF),
+            vmem((2, span, columns), BF),
+            vmem((2, span, columns), BF),
+            vmem((2, heads, span), F32),
+            vmem((2 * share, width), F32),
+            vmem((2 * share, width), F32),
+            vmem((2 * share, width), BF),
+            vmem((2 * share, width), BF),
+            vmem((2, 2 * share, width), F32),
+            vmem((3, 2 * share, 128), F32),
+            vmem((2, rows, width), F32),
+            vmem((2, groups - 1, share, width), BF),
+            vmem((2, groups - 1, share, width), BF),
+            vmem((2 * share, width), BF),
+            vmem((ranks, 2 * share, columns), BF),
+            vmem((2, span, columns), BF),
+            vmem((2, span, 3 * columns), BF),
+            vmem((ranks, 2 * share, 3 * columns), BF),
+            vmem((span, columns), F32),
+            vmem((span, columns), F32),
+            vmem((units, width), BF),
+            vmem((ranks - 1, piece, width), BF),
+            vmem((units, width), BF),
+            vmem((ranks - 1, piece, width), BF),
+            vmem((2 * ranks - 1, half, width), BF),
+            vmem((2 * ranks - 1, flat, width), BF),
+            vmem((many, 3 * columns), F32),
+            vmem((2 + far, many // 2, 3 * columns), BF),
+            vmem((1 + far, many // 2, 3 * columns), BF),
+            vmem((len(all_t) + 1, 8, width), F32),
+            vmem((len(all_t), 8, width), F32),
+            vmem((2 * (far + 1), max(half, flat), width), BF),
+            vmem((2 * (far + 1), max(half, flat), width), BF),
+            dma((32,)),
+        ]
+        + pair(2 * groups)
+        + pair(2 * groups)
+        + pair(ranks)
+        + pair(ranks)
+        + pair(2 * ranks)
+        + pair(2 * ranks)
+        + pair(2 * ranks)
+        + pair(2 * ranks)
+        + pair(3 * groups + 2 * ranks + 2)
+        + pair(len(all_t))
+        + pair(2 * (far + 1))
+        + pair(2 + far),
+        compiler_params=pltpu.CompilerParams(
+            collective_id=3, has_side_effects=True, vmem_limit_bytes=62 * 2**20
+        ),
+        cost_estimate=pl.CostEstimate(flops=10**11, bytes_accessed=40 * 2**20, transcendentals=2**22),
+        name="backward",
+    )(keep, grad_vec, unit, low, scales, normals, w_colbert, down, up, slope, active, normed, out_all,
+      context_rows, query, key, value, lse, queries, passages, qkv_all, gain)
+
+
 def per_device(
     queries,
     passages,
@@ -521,53 +1335,45 @@
     groups, ranks = lax.axis_size("dp"), lax.axis_size("tensor")
     group, rank = lax.axis_index("dp"), lax.axis_index("tensor")
     all_t, all_d = steps_of(ranks), steps_of(groups)
-    far_t, near_t = all_t[:-1], all_t[-1:]
-    far_d, near_d = all_d[:-1], all_d[-1:]
     span, width = queries.shape
     share = span // ranks
     columns = w_qkv.shape[2]
     hidden = w_in.shape[1]
     piece = hidden // groups
 
-    up_mine = lax.dynamic_slice_in_dim(w_in, group * piece, piece, 1).T
-    down_mine = lax.dynamic_slice_in_dim(w_down, group * piece, piece, 0)
-    up = spread(up_mine, "tensor", all_t).reshape(-1, width)
-    down = spread(down_mine, "tensor", all_t).reshape(-1, width)
-    slim = columns // groups
-    out_mine = lax.dynamic_slice_in_dim(w_out, group * slim, slim, 0)
-    out_all = spread(spread(out_mine, "tensor", all_t), "dp", all_d)
-    out_all = natural(out_all, "dp", all_d).transpose(1, 0, 2, 3).reshape(ranks * columns, width)
-    bias_all = lax.all_gather(in_bias, "tensor").reshape(ranks, groups, piece)
-    bias_mine = lax.dynamic_index_in_dim(bias_all, group, 1, keepdims=False)
-    bias_units = xored(bias_mine, "tensor", all_t).reshape(-1).astype(F32)
-
-    tokens = jnp.stack([queries, passages])
+    up_piece = lax.dynamic_slice_in_dim(w_in, group * piece, piece, 1).T
+    turned = w_qkv.transpose(0, 2, 1).reshape(3 * columns, width)
+    qkv_piece = lax.dynamic_slice_in_dim(turned, (group % 2) * (3 * columns // 2), 3 * columns // 2, 0)
+    if piece % 128 == 0:
+        bias_in = lax.dynamic_slice_in_dim(in_bias, group * piece, piece, 0)
+        bias_in = jnp.broadcast_to(bias_in[None, :], (16, piece))
+    else:
+        bias_in = lax.all_gather(in_bias, "tensor").reshape(ranks, groups, piece)
+        bias_in = lax.dynamic_index_in_dim(bias_in, group, 1, keepdims=False).reshape(1, -1).astype(F32)
     lens = jnp.stack([query_lengths[group], passage_lengths[group]])
-    query, key, value, context, lse = attend(lens, tokens, w_qkv, qv_bias)
-    context = context.reshape(2, ranks, share, columns)
-    context_rows = jnp.concatenate(trade(context, all_t, 1), axis=-1).reshape(2 * share, ranks * columns)
-
-    mine = lax.dynamic_index_in_dim(
-        tokens.reshape(2, ranks, share, width), rank, 1, keepdims=False
-    ).reshape(2 * share, width)
-    first, first_normal, first_inverse = layer_norm(
-        mine.astype(F32) + dot(context_rows, out_all) + layer_bias[0], norm_gain[0], norm_shift[0]
+    keep = jnp.where(jnp.arange(span)[None, :] < lens[:, None], 0.0, -1e30)
+    (
+        query,
+        key,
+        value,
+        lse,
+        context_rows,
+        out_all,
+        up,
+        down,
+        qkv_all,
+        normed,
+        inner,
+        active,
+        normals,
+        vectors,
+        unit,
+        output_low,
+        scales,
+    ) = forward(
+        keep, queries, passages, w_qkv, qv_bias, w_out, up_piece, w_down, qkv_piece, bias_in,
+        norm_gain, norm_shift, layer_bias, w_colbert,
     )
-    normed = spread(first.astype(BF), "dp", all_d).reshape(-1, width)
-    inner = inner_rows(normed, up) + bias_units
-    active = jax.nn.gelu(inner, approximate=False).astype(BF)
-    feed = fold(dot(active, down).reshape(groups, 2 * share, width), "dp", all_d)
-    output, out_normal, out_inverse = layer_norm(
-        first + feed + layer_bias[1], norm_gain[1], norm_shift[1]
-    )
-    output_low = output.astype(BF)
-
-    place = rank * share + jnp.arange(share)
-    leading = jnp.concatenate([place == 0, place == 0])[:, None]
-    chosen = jnp.where(leading, output, dot(output_low, w_colbert) + layer_bias[2])
-    inverse = lax.rsqrt(jnp.sum(chosen * chosen, axis=-1, keepdims=True) + 1e-06)
-    unit = chosen * inverse
-    vectors = unit.astype(BF)
     half_t, half_d = ranks // 2, groups // 2
     spot = jnp.arange(share)
     group_q = (group // 2) * 2 + jnp.arange(2)
@@ -590,109 +1396,33 @@
     dense = jnp.where(lead_q[None], 50.0 * along(dense_cot), 0.0)
     grad_vec = score(vectors, valid_p.astype(F32), lead_p.astype(F32), late, dense)
 
-    grad_chosen = inverse * (grad_vec - unit * jnp.sum(grad_vec * unit, axis=-1, keepdims=True))
-    grad_proj = jnp.where(leading, 0.0, grad_chosen).astype(BF)
-    grad_out = jnp.where(leading, grad_chosen, 0.0) + inner_rows(grad_proj, w_colbert)
-    colbert_bias = jnp.sum(grad_proj.astype(F32), axis=0)
-    left = xored(output_low.reshape(2 * share, ranks, -1), "tensor", all_t, 1).reshape(2 * share, width)
-    right = xored(grad_proj.reshape(2 * share, groups, -1), "dp", all_d, 1)
-    colbert = jnp.stack([outer_rows(left, right[:, index]) for index in range(groups)])
-    colbert = colbert.reshape(groups, ranks, width // ranks, width // groups)
-    colbert = fold(fold(colbert, "dp", all_d), "tensor", all_t).astype(BF)
-    colbert = spread(spread(colbert, "tensor", all_t), "dp", all_d)
-    colbert = natural(natural(colbert, "dp", all_d, 0), "tensor", all_t, 1)
-    colbert = colbert.transpose(1, 2, 0, 3).reshape(width, width).astype(F32)
-
-    grad_mid, gain_two, shift_two = norm_back(grad_out, out_normal, out_inverse, norm_gain[1])
-    feed_grad = spread(grad_mid.astype(BF), "dp", all_d).reshape(-1, width)
-    grad_inner = (inner_rows(feed_grad, down) * gelu_slope(inner)).astype(BF)
-    back = fold(dot(grad_inner, up).reshape(groups, 2 * share, width), "dp", all_d)
-    grad_hidden, gain_one, shift_one = norm_back(
-        grad_mid + back, first_normal, first_inverse, norm_gain[0]
+    tokens, grad_down, grad_up, grad_w_out, colbert, grad_qkv, small = backward(
+        keep.T, grad_vec, unit, output_low, scales, normals, w_colbert, down, up, inner, active,
+        normed.reshape(-1, width), out_all.reshape(-1, width), context_rows, query, key, value, lse,
+        queries, passages, qkv_all.reshape(-1, width), norm_gain,
     )
-    attn_grad = grad_hidden.astype(BF)
-    grad_context = inner_rows(attn_grad, out_all).astype(BF).reshape(2, share, ranks, columns)
-    order = offsets(all_t)
-    parts = []
-    for index, item in enumerate(order):
-        part = grad_context[:, :, index]
-        parts.append(swap(part, "tensor", item) if item else part)
-    heads_grad = natural(jnp.stack(parts, axis=1), "tensor", all_t, 1).reshape(2, span, columns)
-
-    def unit_grads(left, right):
-        whole = outer_rows(left, right).reshape(ranks, piece, width)
-        own = fold(whole, "tensor", all_t).astype(BF)
-        return natural(spread(own, "dp", all_d), "dp", all_d).reshape(hidden, width)
-
-    grad_down = unit_grads(active, feed_grad).astype(F32)
-    grad_up = unit_grads(grad_inner, normed).astype(F32).T
-    grad_in_bias = natural(jnp.sum(grad_inner.astype(F32), axis=0).reshape(ranks, piece), "tensor", all_t)
-
-    whole = outer_rows(context_rows, attn_grad).reshape(ranks, groups, slim, width).transpose(1, 0, 2, 3)
-    whole = fold(xored(whole, "dp", all_d), "dp", all_d)
-    own = fold(whole, "tensor", all_t).astype(BF)
-    grad_w_out = natural(spread(own, "dp", all_d), "dp", all_d).reshape(columns, width).astype(F32)
-
-    turned = attend_back(lens, query, key, value, heads_grad, lse)
-    got = trade(turned.reshape(2, ranks, share, 3 * columns), all_t, 1)
-    got = jnp.concatenate(got, axis=-1).reshape(2 * share, ranks * 3 * columns)
-    slice_in = width // groups
-    w_mine, _ = lax.optimization_barrier(
-        (lax.dynamic_slice_in_dim(w_qkv, group * slice_in, slice_in, 1), output_low)
-    )
-    w_mine = w_mine.transpose(0, 2, 1).reshape(3 * columns, slice_in)
-    w_back = spread(spread(w_mine, "tensor", all_t), "dp", all_d).reshape(groups, -1, slice_in)
-    added = jnp.stack([dot(got, w_back[index]) for index in range(groups)])
-    added = natural(added, "dp", all_d).transpose(1, 0, 2).reshape(2 * share, width)
-    grad_tokens = grad_hidden + added
-    tall = tokens.reshape(2 * span, width)
-    turned = turned.reshape(2 * span, 3 * columns)
-    grad_qkv = outer_rows(tall, turned)
-    sums_qkv = jnp.sum(turned.astype(F32), axis=0, keepdims=True)
-    grad_qkv = jnp.concatenate([grad_qkv, jnp.broadcast_to(sums_qkv, (8, 3 * columns))])
-    for step in reversed(all_d):
-        low = grad_qkv.astype(BF)
-        grad_qkv = low.astype(F32) + swap(low, "dp", step).astype(F32)
+    units = piece * ranks
+    grad_in_bias = small[:, 7, :units].reshape(groups, ranks, piece)
+    grad_in_bias = lax.dynamic_index_in_dim(grad_in_bias, rank, 1, keepdims=False).reshape(-1)
+    small = jnp.sum(small, axis=0)
+    grad_qkv = grad_qkv.astype(F32)
     grad_w_qkv = grad_qkv[:width].reshape(width, 3, columns).transpose(1, 0, 2)
-    sums_qkv = grad_qkv[width].reshape(3, columns)
-    grad_qv_bias = jnp.stack([sums_qkv[0], sums_qkv[2]])
-
-    spaced = jnp.where(
-        (jnp.arange(groups) == group)[None, :, None], grad_in_bias[:, None, :], 0.0
-    ).reshape(-1, width)
-    small = jnp.concatenate(
-        [
-            jnp.stack(
-                [
-                    gain_one,
-                    gain_two,
-                    shift_one,
-                    shift_two,
-                    jnp.sum(grad_hidden, axis=0),
-                    jnp.sum(grad_mid, axis=0),
-                    colbert_bias,
-                ]
-            ),
-            spaced,
-        ]
-    )
-    small = lax.psum(small, ("dp", "tensor"))
-    grad_in_bias = lax.dynamic_index_in_dim(small[7:].reshape(ranks, hidden), rank, 0, keepdims=False)
+    line = grad_qkv[width].reshape(3, columns)
     return (
         output_low[:share],
         output_low[share:],
-        grad_tokens[:share],
-        grad_tokens[share:],
+        tokens[:share],
+        tokens[share:],
         grad_w_qkv,
-        grad_qv_bias,
-        grad_w_out,
-        grad_up,
+        jnp.stack([line[0], line[2]]),
+        grad_w_out.astype(F32),
+        grad_up.astype(F32).T,
         grad_in_bias,
-        grad_down,
+        grad_down.astype(F32),
         small[0:2],
         small[2:4],
         small[4:7],
-        colbert,
+        colbert.astype(F32),
     )
 
 

time: 705 us -> 401 us (0.57)
  Pallas kernels: 90 us -> 354 us
  waiting for transfers between devices: 200 us -> 0 us
  starting transfers between devices: 111 us -> 0 us
  local copies, waits for them, and re-layouts: 96 us -> 26.4 us
  other arithmetic: 72.3 us -> 11.7 us
  blocking collectives: 60.5 us -> 0 us
  matrix products: 39.5 us -> 0 us
  between operations: 26.4 us -> 1.33 us
    pallas_call x2, Pallas kernels: 32.9 us -> 294 us  [the longest x1 177 us: backward(): pl.pallas_call(functools.partial(backward_kernel, all_t, all_d), out_shap...]
    ppermute x74 -> x0, waiting for transfers between devices: 200 us -> none  [swap(): lax.ppermute(value, axis, [(index, index ^ step) for index in range(size)])]
    ppermute x74 -> x0, starting transfers between devices: 111 us -> none  [swap(): lax.ppermute(value, axis, [(index, index ^ step) for index in range(size)])]
    dot_general x20 -> x0, matrix products: 39.5 us -> none  [the longest x4 19.4 us: inner_rows(): lax.dot_general(left, right, (((1,), (1,)), ((), ())), preferred_element_...]
    psum x1 -> x0, blocking collectives: 39.1 us -> none  [per_device(): small = lax.psum(small, ('dp', 'tensor'))]
    concatenate x37 -> x0, other arithmetic: 33.5 us -> none  [the longest x28 29.2 us: spread(): held = jnp.concatenate([held, swap(held, axis, step)], axis=0)]
    unnamed x241 -> x25, local copies, waits for them, and re-layouts: 39.9 us -> 7.88 us
    all_gather x1 -> x0, blocking collectives: 21.4 us -> none  [per_device(): bias_all = lax.all_gather(in_bias, 'tensor').reshape(ranks, groups, piece)]
  transfers between devices with their start and end apart: 74 -> 0, of which waited for: 27 -> 0; matrix products, arithmetic and copies ran while one was open for 21% -> 0% of each run, Pallas kernels for 2% -> 0%
where the time goes in v3:
time: 401 us; the launch traced here: 393 us
  Pallas kernels  354 us (88%)
  local copies, waits for them, and re-layouts  26.4 us (7%)
  other arithmetic  11.7 us (3%)
    pallas_call x1, Pallas kernels, backward(): pl.pallas_call(functools.partial(backward_kernel, all_t, all_d), out_shap...  177 us
    pallas_call x1, Pallas kernels, forward(): pl.pallas_call(functools.partial(forward_kernel, all_t, all_d, ship_bias)...  116 us
    pallas_call x1, Pallas kernels, score(): pl.pallas_call(functools.partial(score_kernel, all_t[:-1], all_t[-1:], al...  60.5 us

profile of v3, /device:TPU:1, one launch (start us, length us, event | category | flops | bytes accessed | tf_op | source)
XLA Modules:
  0.0 393.4 jit_solution(17625938540110005578)
XLA Ops:
  0.7 1.4 dynamic_slice.20
  2.1 1.2 dynamic_slice.19
  3.3 1.4 pad_add_fusion
  4.7 0.8 dynamic_slice.23
  5.8 1.3 gather_fusion
  7.1 0.6 broadcast_in_dim.82.bias_in
  7.7 1.3 gather_fusion.1
  9.1 1.2 gather_fusion.4
  10.4 1.2 gather_fusion.2
  11.7 0.6 gather_fusion.3
  13.1 0.7 compare_select_fusion.keep
  14.2 0.8 copy.45
  15.0 0.8 fusion.keep
  16.1 0.8 constant_dynamic-slice_fusion.1.qkv_piece
  16.9 116.4 %forward.1 = (bf16[2,1024,128]{2,1,0:T(8,128)(2,1)}, bf16[2,1024,128]{2,1,0:T(8,128)(2,1)}, bf16[2,1024,128]{2,1,0:T(8,128)(2,1)}, f32[2,2,1024]{2,1,0:T(2,128)}...) custom-call(f32[2,1024]{1,0:T(2,128)} %compare_select_fusion.keep, ...), custom_call_target="tpu_custom_call" | custom-call | flops 99999997952 | bytes 41943040 | tf_op jit(solution)/shard_map/forward/pallas_call | solution.py:699
  133.3 1.0 copy-done.2
  134.4 60.5 %score.1.grad_vec = f32[256,1024]{1,0:T(8,128)S(1)} custom-call(bf16[256,1024]{1,0:T(8,128)(2,1)S(1)} %copy-done.2, f32[512,1]{1,0:T(8,128)S(1)} %copy.40.keep, f32[512,1]{1,0:T(8,128)S(1)} %copy.41.lead, f32[2,1024]{1,0:T(2,128)S(1)} %broadcast_select_fusion.1.late, f32[2,1024]{1,0:T(2,128)S(1)} %broadcast_select_fusion.dense), custom_call_target="tpu_custom_call" | custom-call | flops 4294967296 | bytes 4194304 | tf_op jit(solution)/shard_map/score/pallas_call | solution.py:354
  194.8 1.0 copy-done.1
  195.8 177.2 %backward.1 = (f32[256,1024]{1,0:T(8,128)}, bf16[512,1024]{1,0:T(8,128)(2,1)}, bf16[512,1024]{1,0:T(8,128)(2,1)}, bf16[128,1024]{1,0:T(8,128)(2,1)}, bf16[1024,1...) custom-call(f32[1024,2]{1,0:T(8,128)} %fusion.keep, f32[256,1024]{1,0:T(8,128)} %copy-done.1, ...), custom_call_target="tpu_custom_call" | custom-call | flops 99999997952 | bytes 41943040 | tf_op jit(solution)/shard_map/backward/pallas_call | solution.py:1249
  373.0 2.4 fusion.6
  375.5 0.8 fusion.8
  376.3 0.6 pad_maximum_fusion
  376.9 0.6 constant_dynamic-slice_fusion
  377.5 0.6 slice.66
  378.1 0.6 fusion.9
  378.7 0.8 convert_element_type.28
  379.7 1.6 copy.42
  381.3 3.0 copy.43
  384.3 1.5 convert_bitcast_fusion
  385.8 1.8 copy.44
  387.6 2.9 convert_element_type.29
  390.5 2.5 convert_element_type.30
  (48 shorter events, 2.2 us)
Async XLA Ops:
  0.6 13.4 %copy-start = (bf16[1024,512]{1,0:T(8,128)(2,1)S(1)}, bf16[1024,512]{1,0:T(8,128)(2,1)}, u32[]{:S(2)}) copy-start(bf16[1024,512]{1,0:T(8,128)(2,1)} %param.23) | copy-start | bytes 3145732
  0.7 15.2 %copy-start.5 = (bf16[3,1024,128]{2,1,0:T(8,128)(2,1)S(1)}, bf16[3,1024,128]{2,1,0:T(8,128)(2,1)}, u32[]{:S(2)}) copy-start(bf16[3,1024,128]{2,1,0:T(8,128)(2,1)} %w_qkv.1) | copy-start | bytes 2359300
  133.3 1.0 copy-start.2
  194.8 1.0 copy-start.1
  373.0 2.4 copy-start.6
  373.0 3.3 copy-start.3
  373.0 3.8 copy-start.8
  373.0 5.7 %copy-start.7 = (bf16[128,1024]{1,0:T(8,128)(2,1)S(1)}, bf16[128,1024]{1,0:T(8,128)(2,1)}, u32[]{:S(2)}) copy-start(bf16[128,1024]{1,0:T(8,128)(2,1)} %get-tuple-element.57) | copy-start | bytes 786436
  387.6 2.9 copy-start.4
